TPU v7x, 32 devices: a whole 2x2x4 slice. The times are simulated.
32 devices in a mesh: rep: 2 (over y), tp: 4 (over z), sp: 4 (over x, core).
Axes of the slice: x: 2, y: 2, z: 4, core: 2. Of those that a mesh axis runs over, the one named last changes fastest.
Arguments:
- hidden: bfloat16 [4096, 8192], P(('rep', 'sp'), 'tp'), parts along dimension 0, may hold values from -6 to 6
- doc_ids: int32 [4096], P(('rep', 'sp')), parts along dimension 0, may hold values from 0 to 3, never falling along the last dimension, each value on 1 to 1536 neighbouring positions
- gain: bfloat16 [8192], replicated, may hold values from 0.099609375 to 1.8984375
- w_query: bfloat16 [8192, 4096], P(None, 'tp'), may hold values from -3 to 3
- w_key: bfloat16 [8192, 512], P('tp'), as said below
- w_value: bfloat16 [8192, 512], P('tp'), may hold values from -0.0625 to 0.0625
- w_out: bfloat16 [4096, 8192], P('tp'), may hold values from -0.75 to 0.75
Outputs:
- layer_out: bfloat16 [4096, 8192], P(('rep', 'sp'), 'tp'), parts along dimension 0
There are 2 independent parts, one for each index of `rep`. A program takes and returns all parts, laid end to end along the dimension named above; an argument that names none is the same for every part. Nothing has to cross between parts.
Inputs may be any that keep to these rules, and one draw needn't show every extreme that they name: `doc_ids`: ids never fall along the span; each prompt covers 1 to 1536 consecutive tokens, one exactly 1536. `w_key`: every entry lies within 6 / sqrt(8192) of zero.
All inputs are finite; a program needn't handle non-finite values.
Results may differ from a plain program's by a relative error of at most 0.019.
Values may be sent and summed in bfloat16 or wider, within the bound.
No kernel may reach another device: no remote copies, remote signals or barrier semaphores. Data moves between devices by JAX's collectives and lax.ppermute only.
A program may use at most 192 MiB of HBM per device.

v0:
```python
import functools

import jax
import jax.numpy as jnp
from jax import lax
from jax.experimental import pallas as pl
from jax.experimental.pallas import tpu as pltpu
from jax.sharding import PartitionSpec as P

HD = 128
HQ = 32
KV = 4
DOCS = 4
PERIODS = 2
STREAMS = 2

rope_base = 500000.0
norm_eps = 1e-05
masked_score = -1e30
log2_e = 1.4426950408889634
VMEM_LIMIT = 46 * 1024 * 1024
BLOCK = 512
VMEM = pl.BlockSpec(memory_space=pltpu.VMEM)
SMEM = pl.BlockSpec(memory_space=pltpu.SMEM)
ANY = pl.BlockSpec(memory_space=pl.ANY)


def rope_tables(positions):
    half_dim = HD // 2
    steps_index = jnp.arange(half_dim, dtype=jnp.float32)
    frequency = jnp.power(rope_base, -2.0 * steps_index / HD)
    angles = positions.astype(jnp.float32)[:, None] * frequency[None, :]
    cosine, sine = jnp.cos(angles), jnp.sin(angles)
    return jnp.concatenate([cosine, cosine], axis=1), jnp.concatenate([-sine, sine], axis=1)


def rotate(field, cosine, sine):
    half_dim = HD // 2
    swapped = jnp.concatenate([field[..., half_dim:], field[..., :half_dim]], axis=-1)
    return field * cosine + swapped * sine


def chunk_kernel(count, pieces_of, low, info_ref, *refs):
    total_pieces = len(pieces_of) + 1
    pieces = refs[:total_pieces]
    w_query, w_out, table, both, out = refs[total_pieces : total_pieces + 5]
    held, query_w, out_w, rows_table, kv, query, top, acc, flat, sems, q_sems, o_sems = refs[
        total_pieces + 5 :
    ]
    rows = held.shape[0]
    width = held.shape[1] // count
    parts, depth, piece_columns = query_w.shape[0], query_w.shape[1], query_w.shape[2]
    heads = query.shape[0]
    rank, start, base = info_ref[0], info_ref[1], info_ref[2]
    even = rank % 2 == 0

    def place(source, block):
        columns = pl.ds(pl.multiple_of(block * width, width), width)
        return pltpu.make_async_copy(source, held.at[:, columns], sems.at[block])

    place(pieces[0].at[pl.ds(low, rows)], rank).start()
    for piece, (kind, step) in zip(pieces[1:], pieces_of):
        block = jnp.where(even == (kind == "outer"), rank + step, rank - step)

        @pl.when((block >= 0) & (block < count))
        def _():
            place(piece, block).start()

    def query_copy(k):
        return pltpu.make_async_copy(
            w_query.at[:, pl.ds(pl.multiple_of(k * piece_columns, piece_columns), piece_columns)],
            query_w.at[k],
            q_sems.at[k],
        )

    for k in range(parts):
        query_copy(k).start()
    table_copy = pltpu.make_async_copy(table.at[pl.ds(low, rows)], rows_table, sems.at[count])
    table_copy.start()
    kv_copy = pltpu.make_async_copy(both, kv, sems.at[count + 1])
    kv_copy.start()
    out_parts = out_w.shape[0]
    out_columns = out_w.shape[2]

    def out_copy(k):
        return pltpu.make_async_copy(
            w_out.at[:, pl.ds(pl.multiple_of(k * out_columns, out_columns), out_columns)],
            out_w.at[k],
            o_sems.at[k],
        )

    for k in range(out_parts):
        out_copy(k).start()

    for block in range(count):
        place(pieces[0].at[pl.ds(low, rows)], block).wait()
    table_copy.wait()
    cos, sin = rows_table[:, :HD], rows_table[:, HD : 2 * HD]
    pair = piece_columns // HD

    @pl.loop(0, parts)
    def _(k):
        query_copy(k).wait()
        total = jnp.dot(held[...], query_w[k], preferred_element_type=jnp.float32)
        for h in range(pair):
            field = total[:, h * HD : (h + 1) * HD]
            swapped = pltpu.roll(field, HD // 2, 1)
            query[k * pair + h] = (field * cos + swapped * sin).astype(jnp.bfloat16)

    kv_copy.wait()
    factor = HD ** (-0.5) * log2_e
    top[...] = jnp.full_like(top, masked_score)
    acc[...] = jnp.zeros_like(acc)
    first = rows_table[:, 2 * HD : 2 * HD + 1].astype(jnp.int32)
    row_index = base + low + lax.broadcasted_iota(jnp.int32, (rows, BLOCK), 0)
    column = lax.broadcasted_iota(jnp.int32, (rows, BLOCK), 1)
    ones = jnp.ones((BLOCK, HD), jnp.bfloat16)

    def step(j, carry):
        offset = pl.multiple_of(j * BLOCK, BLOCK)
        key_index = column + offset
        bias = jnp.where((key_index <= row_index) & (key_index >= first), 0.0, masked_score)
        key = kv[pl.ds(offset, BLOCK), :HD]
        value = jnp.concatenate([kv[pl.ds(offset, BLOCK), HD:], ones], axis=1)
        for h in range(heads):
            scores = lax.dot_general(
                query[h], key, (((1,), (1,)), ((), ())), preferred_element_type=jnp.float32
            )
            scores = scores * factor + bias
            old = top[h]
            new = jnp.maximum(old, jnp.max(scores, axis=1, keepdims=True))
            exps = jnp.exp2(scores - new[:, :1])
            mixed = jnp.dot(exps.astype(jnp.bfloat16), value, preferred_element_type=jnp.float32)
            keep = jnp.exp2(old - new)
            acc[h] = acc[h] * jnp.concatenate([keep, keep], axis=1) + mixed
            top[h] = new
        return carry

    lax.fori_loop(start, (base + low + rows - 1) // BLOCK + 1, step, 0)
    for h in range(heads):
        flat[:, h * HD : (h + 1) * HD] = (acc[h, :, :HD] / acc[h, :, HD:]).astype(jnp.bfloat16)

    per_block = width // out_columns

    @pl.loop(0, count)
    def _(b):
        for k in range(per_block):
            out_copy(b * per_block + k).wait()
            out[b, :, k * out_columns : (k + 1) * out_columns] = jnp.dot(
                flat[...], out_w[b * per_block + k], preferred_element_type=jnp.float32
            ).astype(jnp.bfloat16)


def chunk_terms(count, low, rows, scaled, arrived, info, w_query, w_out, table, both):
    width = scaled.shape[1]
    model, columns = w_query.shape
    inner = w_out.shape[0]
    heads = columns // HD
    tokens = both.shape[0]
    pieces = [scaled] + [piece for _, _, piece in arrived]
    pieces_of = [(kind, step) for kind, step, _ in arrived]
    q_columns = min(columns, 256)
    o_columns = min(width, 1024)
    q_parts, o_parts = columns // q_columns, model // o_columns
    return pl.pallas_call(
        functools.partial(chunk_kernel, count, pieces_of, low),
        out_shape=jax.ShapeDtypeStruct((count, rows, width), jnp.bfloat16),
        in_specs=[SMEM] + [ANY] * (len(pieces) + 4),
        out_specs=VMEM,
        scratch_shapes=[
            pltpu.VMEM((rows, model), jnp.bfloat16),
            pltpu.VMEM((q_parts, model, q_columns), jnp.bfloat16),
            pltpu.VMEM((o_parts, inner, o_columns), jnp.bfloat16),
            pltpu.VMEM((rows, 3 * HD), jnp.float32),
            pltpu.VMEM((tokens, 2 * HD), jnp.bfloat16),
            pltpu.VMEM((heads, rows, HD), jnp.bfloat16),
            pltpu.VMEM((heads, rows, HD), jnp.float32),
            pltpu.VMEM((heads, rows, 2 * HD), jnp.float32),
            pltpu.VMEM((rows, inner), jnp.bfloat16),
            pltpu.SemaphoreType.DMA((count + 2,)),
            pltpu.SemaphoreType.DMA((q_parts,)),
            pltpu.SemaphoreType.DMA((o_parts,)),
        ],
        compiler_params=pltpu.CompilerParams(vmem_limit_bytes=VMEM_LIMIT),
        cost_estimate=pl.CostEstimate(
            flops=4 * rows * model * columns, bytes_accessed=4 * model * columns, transcendentals=0
        ),
        name="chunk_terms",
    )(info, *pieces, w_query, w_out, table, both)


def finish_kernel(count, low, has_inner, info_ref, hidden, terms, outer, inner, *refs):
    out, a, b, c, d, total, sems = refs[-7:]
    rows = a.shape[0]
    rank = info_ref[0]
    copies = [
        pltpu.make_async_copy(source, target, sems.at[k])
        for k, (source, target) in enumerate(
            [(hidden.at[pl.ds(low, rows)], a), (terms.at[rank], b), (outer, c), (inner, d)]
        )
    ]
    for copy in copies:
        copy.start()
    for copy in copies:
        copy.wait()
    summed = b[...].astype(jnp.float32) + c[...].astype(jnp.float32)
    middle = (rank > 0) & (rank < count - 1)
    other = jnp.where(middle, d[...].astype(jnp.float32), 0.0)
    total[...] = (a[...].astype(jnp.float32) + (summed + other)).astype(jnp.bfloat16)
    copy = pltpu.make_async_copy(total, out.at[pl.ds(low, rows)], sems.at[4])
    copy.start()
    copy.wait()


def finish(count, low, info, hidden, terms, last, out):
    _, rows, width = terms.shape
    outer, inner = last
    operands = [info, hidden, terms, outer, inner if inner is not None else outer]
    aliases = {}
    if out is not None:
        aliases = {len(operands): 0}
        operands.append(out)
    return pl.pallas_call(
        functools.partial(finish_kernel, count, low, inner is not None),
        out_shape=jax.ShapeDtypeStruct(hidden.shape, jnp.bfloat16),
        in_specs=[SMEM] + [ANY] * (len(operands) - 1),
        out_specs=ANY,
        scratch_shapes=[pltpu.VMEM((rows, width), jnp.bfloat16)] * 5 + [pltpu.SemaphoreType.DMA((5,))],
        input_output_aliases=aliases,
        compiler_params=pltpu.CompilerParams(vmem_limit_bytes=VMEM_LIMIT),
        name="finish",
    )(*operands)


def after(value, *others):
    return lax.optimization_barrier((value, others))[0]


def all_sum(value, axis, size):
    distance = 1
    while distance < size:
        value = value + lax.ppermute(value, axis, [(i, i ^ distance) for i in range(size)])
        distance *= 2
    return value


class Line:
    def __init__(self, count, sp_count, rank):
        self.count, self.rank = count, rank
        self.even = rank % 2 == 0
        self.middle = (rank > 0) & (rank < count - 1)
        self.outer_pairs = [(i, i ^ 1) for i in range(count)]
        self.inner_pairs = []
        for i in range(count):
            for s in range(sp_count):
                partner = i + 1 if i % 2 else i - 1
                if 0 < i < count - 1:
                    self.inner_pairs.append((i * sp_count + s, partner * sp_count + s))
                else:
                    self.inner_pairs.append((i * sp_count + s, i * sp_count + (s ^ 1)))

    def outer(self, value):
        return lax.ppermute(value, "tp", self.outer_pairs)

    def inner(self, value):
        return lax.ppermute(value, ("tp", "sp"), self.inner_pairs)

    def term(self, terms, upward, step):
        dest = jnp.where(upward, self.rank + self.count - step, self.rank - self.count + step)
        valid = (dest >= 0) & (dest < self.count)
        return lax.dynamic_index_in_dim(terms, jnp.clip(dest, 0, self.count - 1), 0, False), valid

    def round(self, step, own, terms, last):
        count = self.count
        from_outer, from_inner = last
        gather_outer = own is not None and step < count
        gather_inner = own is not None and step < count - 1
        scatter_outer = terms is not None and step > 1
        scatter_inner = terms is not None and step > 2
        to_outer = to_inner = None
        if gather_outer:
            to_outer = own if step == 1 else from_inner
        if gather_inner:
            to_inner = own if step == 1 else from_outer
        if scatter_outer:
            mine, valid = self.term(terms, self.even, step - 1)
            if step > 3:
                added = (mine.astype(jnp.float32) + from_inner.astype(jnp.float32)).astype(jnp.bfloat16)
                mine = jnp.where(self.middle, added, mine)
            to_outer = mine if to_outer is None else jnp.where(valid, mine, to_outer)
        if scatter_inner:
            mine, valid = self.term(terms, ~self.even, step - 1)
            mine = (mine.astype(jnp.float32) + from_outer.astype(jnp.float32)).astype(jnp.bfloat16)
            to_inner = mine if to_inner is None else jnp.where(valid, mine, to_inner)
        got_outer = None if to_outer is None else self.outer(to_outer)
        got_inner = None if to_inner is None else self.inner(to_inner)
        return got_outer, got_inner

    def scatter_only(self, step, terms, last):
        count = self.count
        from_outer, from_inner = last
        mine, _ = self.term(terms, self.even, step)
        if step > 2:
            added = (mine.astype(jnp.float32) + from_inner.astype(jnp.float32)).astype(jnp.bfloat16)
            mine = jnp.where(self.middle, added, mine)
        if step < count - 1:
            pairs = [
                (i, i ^ 1) for i in range(count) if (i <= step - 1 if i % 2 == 0 else i >= count - step)
            ]
            got_outer = lax.ppermute(mine, "tp", pairs)
        else:
            got_outer = self.outer(mine)
        if step < 2:
            return got_outer, None
        mine, _ = self.term(terms, ~self.even, step)
        mine = (mine.astype(jnp.float32) + from_outer.astype(jnp.float32)).astype(jnp.bfloat16)
        return got_outer, self.inner(mine)

    def total(self, terms, last):
        mine = lax.dynamic_index_in_dim(terms, self.rank, 0, False).astype(jnp.float32)
        mine = mine + last[0].astype(jnp.float32)
        return jnp.where(self.middle, mine + last[1].astype(jnp.float32), mine)


def make_body(count, sp_count):
    def body(hidden, doc_ids, gain, w_query, w_key, w_value, w_out):
        rows, width = hidden.shape
        rank = lax.axis_index("tp")
        sp_rank = lax.axis_index("sp")
        heads = w_query.shape[1] // HD
        group = HQ // KV
        model = width * count
        line = Line(count, sp_count, rank)
        gain_own = lax.dynamic_slice_in_dim(gain, rank * width, width, 0).astype(jnp.float32)
        hidden_f = hidden.astype(jnp.float32)
        scaled = (hidden_f * gain_own[None, :]).astype(jnp.bfloat16)
        squares = all_sum(jnp.sum(hidden_f * hidden_f, axis=1), "tp", count)
        inverse = lax.rsqrt(squares / model + norm_eps)[:, None]
        w_query = pltpu.with_memory_space_constraint(w_query, pltpu.HBM)
        w_out = pltpu.with_memory_space_constraint(w_out, pltpu.HBM)
        chunk = rows // (PERIODS * STREAMS)

        labels = jnp.arange(DOCS, dtype=jnp.int32)
        starts = all_sum(
            jnp.sum((doc_ids[None, :] < labels[:, None]).astype(jnp.int32), axis=1), "sp", sp_count
        )
        base = sp_rank * rows
        own_index = base + jnp.arange(rows, dtype=jnp.int32)
        first = jnp.sum(jnp.where(doc_ids[:, None] == labels[None, :], starts[None, :], 0), axis=1)
        cosine, sine = rope_tables(own_index - first)
        table = jnp.concatenate(
            [
                cosine * inverse,
                sine * inverse,
                jnp.broadcast_to(first.astype(jnp.float32)[:, None], (rows, HD)),
            ],
            axis=1,
        )
        infos = [
            jnp.stack([rank, first[k * chunk] // BLOCK, base]).astype(jnp.int32)
            for k in range(PERIODS * STREAMS)
        ]

        key_part = jnp.dot(scaled, w_key, preferred_element_type=jnp.float32).astype(jnp.bfloat16)
        value_part = jnp.dot(scaled, w_value, preferred_element_type=jnp.float32).astype(jnp.bfloat16)
        kv_terms = []
        for d in range(count):
            head = slice(d * heads // group * HD, (d * heads // group + 1) * HD)
            kv_terms.append(jnp.concatenate([key_part[:, head], value_part[:, head]], axis=1))
        kv_terms = jnp.stack(kv_terms)
        kv_last = (None, None)

        out = None
        both = None
        last = [(None, None)] * STREAMS
        terms = [None] * STREAMS
        for period in range(PERIODS + 1):
            gather = period < PERIODS
            owns = [None] * STREAMS
            arrived = [[] for _ in range(STREAMS)]
            fresh = [None] * STREAMS
            for step in range(1, count + 1):
                if period == 0 and step < count:
                    kv_last = line.scatter_only(step, kv_terms, kv_last)
                for j in range(STREAMS):
                    if not (gather and step < count) and not (terms[j] is not None and step > 1):
                        continue
                    if gather and step == 1:
                        low = (period * STREAMS + j) * chunk
                        owns[j] = scaled[low : low + chunk]
                        if period:
                            owns[j] = after(owns[j], last[j], terms[:j])
                    last[j] = line.round(step, owns[j], terms[j], last[j])
                    if gather and step < count:
                        arrived[j].append(("outer", step, last[j][0]))
                        if step < count - 1:
                            arrived[j].append(("inner", step, last[j][1]))
            if period == 0:
                kv = line.total(kv_terms, kv_last) * inverse
                keys = rotate(kv[:, :HD], cosine, sine).astype(jnp.bfloat16)
                both = jnp.concatenate([keys, kv[:, HD:].astype(jnp.bfloat16)], axis=1)
                both = lax.all_gather(both, "sp", axis=0, tiled=True)
            for j in range(STREAMS):
                if terms[j] is not None:
                    low = ((period - 1) * STREAMS + j) * chunk
                    out = finish(count, low, infos[0], hidden, terms[j], last[j], out)
                if gather:
                    k = period * STREAMS + j
                    terms[j] = chunk_terms(
                        count, k * chunk, chunk, scaled, arrived[j], infos[k], w_query, w_out, table, both
                    )
        return out

    return body


def solution(mesh):
    placed = (
        P(("rep", "sp"), "tp"),
        P(("rep", "sp")),
        P(),
        P(None, "tp"),
        P("tp", None),
        P("tp", None),
        P("tp", None),
    )
    body = make_body(mesh.shape["tp"], mesh.shape["sp"])
    return jax.shard_map(
        body, mesh=mesh, in_specs=placed, out_specs=P(("rep", "sp"), "tp"), check_vma=False
    )
```

profile of v0, /device:TPU:10, one launch (start us, length us, event | category | flops | bytes accessed | tf_op | source)
XLA Modules:
  0.0 330.1 jit_solution(3142779768994226379)
XLA Ops:
  8.3 3.5 %fusion.1 = (f32[512]{0:T(512)S(1)}, bf16[512,2048]{1,0:T(8,128)(2,1)}) fusion(bf16[512,2048]{1,0:T(8,128)(2,1)} %hidden.7, f32[2048]{0:T(1024)S(1)} %dynamic-slice_convert_fusion), kind=kLoop, calls=%fused_computation.3 | loop fusion | flops 5242368 | bytes 4204544 | tf_op jit(solution)/shard_map/reduce_sum | solution.py:337
  12.2 3.0 convolution_convert_fusion
  20.9 2.7 collective-permute-start.5
  23.7 3.4 %collective-permute-done.1 = s32[4]{0:T(128)S(1)} collective-permute-done((s32[4]{0:T(128)S(1)}, s32[4]{0:T(128)S(1)}, u32[]{:S(2)}, u32[]{:S(2)}) %collective-permute-start.1) | collective-permute-done | bytes 48 | tf_op jit(solution)/shard_map/ppermute | solution.py:242
  28.1 5.6 %collective-permute-done.15 = bf16[512,256]{1,0:T(8,128)(2,1)S(1)} collective-permute-done((bf16[512,256]{1,0:T(8,128)(2,1)S(1)}, bf16[512,256]{1,0:T(8,128)(2,1)S(1)}, u32[]{:S(2)}, u32[]{:S(2)}) %collective-permute-start.15) | collective-permute-done | bytes 262176 | tf_op jit(solution)/shard_map/ppermute | solution.py:310
  33.8 2.8 collective-permute-start.13
  36.9 6.9 %collective-permute-done.13 = bf16[512,256]{1,0:T(8,128)(2,1)S(1)} collective-permute-done((bf16[512,256]{1,0:T(8,128)(2,1)S(1)}, bf16[512,256]{1,0:T(8,128)(2,1)S(1)}, u32[]{:S(2)}, u32[]{:S(2)}) %collective-permute-start.13) | collective-permute-done | bytes 262176 | tf_op jit(solution)/shard_map/ppermute | solution.py:266
  45.0 2.1 collective-permute-done.11
  47.6 2.7 collective-permute-done.14
  52.7 6.7 %collective-permute-done.8.refs_4_ = bf16[128,2048]{1,0:T(8,128)(2,1)S(1)} collective-permute-done((bf16[128,2048]{1,0:T(8,128)(2,1)S(1)}, bf16[128,2048]{1,0:T(8,128)(2,1)S(1)}, u32[]{:S(2)}, u32[]{:S(2)}) %collective-permute-start.8) | collective-permute-done | bytes 524320 | tf_op jit(solution)/shard_map/ppermute | solution.py:266
  61.5 5.6 %collective-permute-done.2.refs_1_ = bf16[128,2048]{1,0:T(8,128)(2,1)S(1)} collective-permute-done((bf16[128,2048]{1,0:T(8,128)(2,1)S(1)}, bf16[128,2048]{1,0:T(8,128)(2,1)S(1)}, u32[]{:S(2)}, u32[]{:S(2)}) %collective-permute-start.2) | collective-permute-done | bytes 524320 | tf_op jit(solution)/shard_map/ppermute | solution.py:263
  67.1 2.6 collective-permute-start.3
  69.7 5.6 %collective-permute-done.9.refs_5_ = bf16[128,2048]{1,0:T(8,128)(2,1)S(1)} collective-permute-done((bf16[128,2048]{1,0:T(8,128)(2,1)S(1)}, bf16[128,2048]{1,0:T(8,128)(2,1)S(1)}, u32[]{:S(2)}, u32[]{:S(2)}) %collective-permute-start.9) | collective-permute-done | bytes 524320 | tf_op jit(solution)/shard_map/ppermute | solution.py:263
  75.8 1.6 collective-permute-start.7
  86.9 6.5 %collective-permute-done.3.refs_4_ = bf16[128,2048]{1,0:T(8,128)(2,1)} collective-permute-done((bf16[128,2048]{1,0:T(8,128)(2,1)S(1)}, bf16[128,2048]{1,0:T(8,128)(2,1)}, u32[]{:S(2)}, u32[]{:S(2)}) %collective-permute-start.3) | collective-permute-done | bytes 524320 | tf_op jit(solution)/shard_map/ppermute | solution.py:266
  96.7 5.1 %collective-permute-done.7.refs_3_ = bf16[128,2048]{1,0:T(8,128)(2,1)} collective-permute-done((bf16[128,2048]{1,0:T(8,128)(2,1)S(1)}, bf16[128,2048]{1,0:T(8,128)(2,1)}, u32[]{:S(2)}, u32[]{:S(2)}) %collective-permute-start.7) | collective-permute-done | bytes 524320 | tf_op jit(solution)/shard_map/ppermute | solution.py:263
  107.2 16.7 %chunk_terms.4.terms = bf16[4,128,2048]{2,1,0:T(8,128)(2,1)S(1)} custom-call(s32[3]{0:T(128)S(1)} %add_add_fusion.info_ref, bf16[512,2048]{1,0:T(8,128)(2,1)} %get-tuple-element.30.refs_0_, bf16[128,2048]{1,0:T(8,128)(2,1)S(1)} %copy-done.6, bf16[128,2048]{1,0:T(8,128)(2,1)S(1)} %copy-done.14, bf16[128,2048]{1,0:T(8,128)(2,1)} %collective-permute-done.7.refs_3_, ...), custom_call_target="tpu_custom_call" | custom-call | flops 4294967296 | bytes 33554432 | tf_op jit(solution)/shard_map/chunk_terms/pallas_call | solution.py:165
  124.5 2.2 bitcast_select_fusion
  127.2 1.6 collective-permute-start.31
  131.5 2.2 collective-permute-start.18
  136.0 17.2 %chunk_terms.5.terms = bf16[4,128,2048]{2,1,0:T(8,128)(2,1)S(1)} custom-call(s32[3]{0:T(128)S(1)} %add_add_fusion.2.info_ref, bf16[512,2048]{1,0:T(8,128)(2,1)} %get-tuple-element.30.refs_0_, bf16[128,2048]{1,0:T(8,128)(2,1)S(1)} %copy-done.8, bf16[128,2048]{1,0:T(8,128)(2,1)} %collective-permute-done.19.refs_2_, ...), custom_call_target="tpu_custom_call" | custom-call | flops 4294967296 | bytes 33554432 | tf_op jit(solution)/shard_map/chunk_terms/pallas_call | solution.py:165
  153.3 2.9 collective-permute-done.31.refs_3_
  156.2 1.6 fusion.2
  157.8 1.6 collective-permute-start.44
  159.9 17.0 %chunk_terms.7.terms = bf16[4,128,2048]{2,1,0:T(8,128)(2,1)S(1)} custom-call(s32[3]{0:T(128)S(1)} %add_add_fusion.3.info_ref, bf16[512,2048]{1,0:T(8,128)(2,1)} %get-tuple-element.30.refs_0_, bf16[128,2048]{1,0:T(8,128)(2,1)} %collective-permute-done.29.refs_1_, bf16[128,2048]{1,0:T(8,128)(2,1)S(1)} %collective-permute-done.30.refs_2_, ...), custom_call_target="tpu_custom_call" | custom-call | flops 4294967296 | bytes 33554432 | tf_op jit(solution)/shard_map/chunk_terms/pallas_call | solution.py:165
  180.8 5.7 %collective-permute-done.42 = bf16[128,2048]{1,0:T(8,128)(2,1)S(1)} collective-permute-done((bf16[128,2048]{1,0:T(8,128)(2,1)S(1)}, bf16[128,2048]{1,0:T(8,128)(2,1)S(1)}, u32[]{:S(2)}, u32[]{:S(2)}) %collective-permute-start.42) | collective-permute-done | bytes 524320 | tf_op jit(solution)/shard_map/ppermute | solution.py:266
  186.6 4.9 %collective-permute-done.23.refs_5_ = bf16[128,2048]{1,0:T(8,128)(2,1)S(1)} collective-permute-done((bf16[128,2048]{1,0:T(8,128)(2,1)S(1)}, bf16[128,2048]{1,0:T(8,128)(2,1)S(1)}, u32[]{:S(2)}, u32[]{:S(2)}) %collective-permute-start.23) | collective-permute-done | bytes 524320 | tf_op jit(solution)/shard_map/ppermute | solution.py:263
  192.5 10.3 %collective-permute-done.21.refs_3_ = bf16[128,2048]{1,0:T(8,128)(2,1)S(1)} collective-permute-done((bf16[128,2048]{1,0:T(8,128)(2,1)S(1)}, bf16[128,2048]{1,0:T(8,128)(2,1)S(1)}, u32[]{:S(2)}, u32[]{:S(2)}) %collective-permute-start.21) | collective-permute-done | bytes 524320 | tf_op jit(solution)/shard_map/ppermute | solution.py:263
  202.8 17.0 %chunk_terms.6.terms = bf16[4,128,2048]{2,1,0:T(8,128)(2,1)S(1)} custom-call(s32[3]{0:T(128)S(1)} %add_add_fusion.1.info_ref, bf16[512,2048]{1,0:T(8,128)(2,1)} %get-tuple-element.30.refs_0_, bf16[128,2048]{1,0:T(8,128)(2,1)} %collective-permute-done.17.refs_1_, bf16[128,2048]{1,0:T(8,128)(2,1)S(1)} %collective-permute-done.18.refs_2_, ...), custom_call_target="tpu_custom_call" | custom-call | flops 4294967296 | bytes 33554432 | tf_op jit(solution)/shard_map/chunk_terms/pallas_call | solution.py:165
  222.1 3.2 collective-permute-done.34
  225.7 1.6 collective-permute-start.35
  227.6 20.1 %collective-permute-done.27 = bf16[128,2048]{1,0:T(8,128)(2,1)S(1)} collective-permute-done((bf16[128,2048]{1,0:T(8,128)(2,1)S(1)}, bf16[128,2048]{1,0:T(8,128)(2,1)S(1)}, u32[]{:S(2)}, u32[]{:S(2)}) %collective-permute-start.27) | collective-permute-done | bytes 524320 | tf_op jit(solution)/shard_map/ppermute | solution.py:263
  247.8 1.5 collective-permute-start.38
  249.3 9.7 %collective-permute-done.24 = bf16[128,2048]{1,0:T(8,128)(2,1)S(1)} collective-permute-done((bf16[128,2048]{1,0:T(8,128)(2,1)S(1)}, bf16[128,2048]{1,0:T(8,128)(2,1)S(1)}, u32[]{:S(2)}, u32[]{:S(2)}) %collective-permute-start.24) | collective-permute-done | bytes 524320 | tf_op jit(solution)/shard_map/ppermute | solution.py:263
  259.0 1.5 collective-permute-start.39
  261.6 12.2 %collective-permute-done.39 = bf16[128,2048]{1,0:T(8,128)(2,1)S(1)} collective-permute-done((bf16[128,2048]{1,0:T(8,128)(2,1)S(1)}, bf16[128,2048]{1,0:T(8,128)(2,1)S(1)}, u32[]{:S(2)}, u32[]{:S(2)}) %collective-permute-start.39) | collective-permute-done | bytes 524320 | tf_op jit(solution)/shard_map/ppermute | solution.py:266
  273.8 1.5 collective-permute-start.41
  275.5 9.5 %collective-permute-done.25 = bf16[128,2048]{1,0:T(8,128)(2,1)S(1)} collective-permute-done((bf16[128,2048]{1,0:T(8,128)(2,1)S(1)}, bf16[128,2048]{1,0:T(8,128)(2,1)S(1)}, u32[]{:S(2)}, u32[]{:S(2)}) %collective-permute-start.25) | collective-permute-done | bytes 524320 | tf_op jit(solution)/shard_map/ppermute | solution.py:266
  285.3 2.1 collective-permute-start.36
  287.4 1.5 collective-permute-start.28
  288.9 7.4 %collective-permute-done.41.inner = bf16[128,2048]{1,0:T(8,128)(2,1)S(1)} collective-permute-done((bf16[128,2048]{1,0:T(8,128)(2,1)S(1)}, bf16[128,2048]{1,0:T(8,128)(2,1)S(1)}, u32[]{:S(2)}, u32[]{:S(2)}) %collective-permute-start.41) | collective-permute-done | bytes 524320 | tf_op jit(solution)/shard_map/ppermute | solution.py:266
  296.3 1.8 finish.4.refs_0_
  298.1 1.7 collective-permute-done.40.outer
  299.9 1.8 finish.5.refs_0_
  301.7 9.4 %collective-permute-done.36.outer = bf16[128,2048]{1,0:T(8,128)(2,1)S(1)} collective-permute-done((bf16[128,2048]{1,0:T(8,128)(2,1)S(1)}, bf16[128,2048]{1,0:T(8,128)(2,1)S(1)}, u32[]{:S(2)}, u32[]{:S(2)}) %collective-permute-start.36) | collective-permute-done | bytes 524320 | tf_op jit(solution)/shard_map/ppermute | solution.py:263
  311.1 1.8 finish.6.refs_0_
  312.9 8.4 %collective-permute-done.26.outer = bf16[128,2048]{1,0:T(8,128)(2,1)S(1)} collective-permute-done((bf16[128,2048]{1,0:T(8,128)(2,1)S(1)}, bf16[128,2048]{1,0:T(8,128)(2,1)S(1)}, u32[]{:S(2)}, u32[]{:S(2)}) %collective-permute-start.26) | collective-permute-done | bytes 524320 | tf_op jit(solution)/shard_map/ppermute | solution.py:263
  321.4 1.8 finish.7
  (141 shorter events, 39.7 us)
Async XLA Ops:
  6.5 95.3 %all-gather.2.cloned.1.call-start = ((), (), s32[]{:S(2)}) async-start(), calls=%async_computation | async-start | bytes 1310720 | tf_op jit(solution)/shard_map/all_gather | solution.py:402
  7.5 16.0 %collective-permute-start = (s32[4]{0:T(128)S(1)}, s32[4]{0:T(128)S(1)}, u32[]{:S(2)}, u32[]{:S(2)}) collective-permute-start(s32[4]{0:T(128)S(1)} %convert_reduce_fusion), channel_id=1, source_target_pairs={{0,1},{1,0},{2,3},{3,2},{4,5},{5,4},{6,7},{7,6},{8,9},{9,8},{10,11... | collective-permute-start | bytes 56 | tf_op jit(solution)/shard_map/ppermute | solution.py:242
  11.8 24.9 %collective-permute-start.10 = (f32[512]{0:T(512)S(1)}, f32[512]{0:T(512)S(1)}, u32[]{:S(2)}, u32[]{:S(2)}) collective-permute-start(f32[512]{0:T(512)S(1)} %get-tuple-element.29), channel_id=1, source_target_pairs={{0,4},{4,0},{8,12},{12,8},{1,5},{5,1},{9,13},{13,9},{2,6},{6,2},{1... | collective-permute-start | bytes 6152 | tf_op jit(solution)/shard_map/ppermute | solution.py:242
  17.0 11.0 %collective-permute-start.12 = (bf16[512,256]{1,0:T(8,128)(2,1)S(1)}, bf16[512,256]{1,0:T(8,128)(2,1)S(1)}, u32[]{:S(2)}, u32[]{:S(2)}) collective-permute-start(bf16[512,256]{1,0:T(8,128)(2,1)S(1)} %get-tuple-element.33), channel_id=1, source_target_pairs={{0,4},{12,8},{1,5},{13,9},{2,6},{14,10},{3,7},{15,11},{16,20},{28,... | collective-permute-start | bytes 786440 | tf_op jit(solution)/shard_map/ppermute | solution.py:310
  18.3 15.3 %collective-permute-start.15 = (bf16[512,256]{1,0:T(8,128)(2,1)S(1)}, bf16[512,256]{1,0:T(8,128)(2,1)S(1)}, u32[]{:S(2)}, u32[]{:S(2)}) collective-permute-start(bf16[512,256]{1,0:T(8,128)(2,1)S(1)} %get-tuple-element.34), channel_id=1, source_target_pairs={{0,4},{12,8},{1,5},{13,9},{2,6},{14,10},{3,7},{15,11},{16,20},{28,... | collective-permute-start | bytes 786440 | tf_op jit(solution)/shard_map/ppermute | solution.py:310
  20.9 26.3 %collective-permute-start.5 = (bf16[128,2048]{1,0:T(8,128)(2,1)S(1)}, bf16[128,2048]{1,0:T(8,128)(2,1)S(1)}, u32[]{:S(2)}, u32[]{:S(2)}) collective-permute-start(bf16[128,2048]{1,0:T(8,128)(2,1)S(1)} %get-tuple-element.20), channel_id=1, source_target_pairs={{0,4},{4,0},{8,12},{12,8},{1,5},{5,1},{9,13},{13,9},{2,6},{6,2},{1... | collective-permute-start | bytes 1572872 | tf_op jit(solution)/shard_map/ppermute | solution.py:263
  23.5 3.6 %collective-permute-start.1 = (s32[4]{0:T(128)S(1)}, s32[4]{0:T(128)S(1)}, u32[]{:S(2)}, u32[]{:S(2)}) collective-permute-start(s32[4]{0:T(128)S(1)} %add.195), channel_id=1, source_target_pairs={{0,2},{1,3},{2,0},{3,1},{4,6},{5,7},{6,4},{7,5},{8,10},{9,11},{10,... | collective-permute-start | bytes 56 | tf_op jit(solution)/shard_map/ppermute | solution.py:242
  33.8 10.0 %collective-permute-start.13 = (bf16[512,256]{1,0:T(8,128)(2,1)S(1)}, bf16[512,256]{1,0:T(8,128)(2,1)S(1)}, u32[]{:S(2)}, u32[]{:S(2)}) collective-permute-start(bf16[512,256]{1,0:T(8,128)(2,1)S(1)} %get-tuple-element.31), channel_id=1, source_target_pairs={{0,1},{1,0},{2,3},{3,2},{4,8},{5,9},{6,10},{7,11},{8,4},{9,5},{10,... | collective-permute-start | bytes 786440 | tf_op jit(solution)/shard_map/ppermute | solution.py:266
  36.7 10.4 %collective-permute-start.11 = (f32[512]{0:T(512)S(1)}, f32[512]{0:T(512)S(1)}, u32[]{:S(2)}, u32[]{:S(2)}) collective-permute-start(f32[512]{0:T(512)S(1)} %add.200), channel_id=1, source_target_pairs={{0,8},{4,12},{8,0},{12,4},{1,9},{5,13},{9,1},{13,5},{2,10},{6,14},... | collective-permute-start | bytes 6152 | tf_op jit(solution)/shard_map/ppermute | solution.py:242
  36.8 10.9 %collective-permute-start.16 = (bf16[512,256]{1,0:T(8,128)(2,1)S(1)}, bf16[512,256]{1,0:T(8,128)(2,1)S(1)}, u32[]{:S(2)}, u32[]{:S(2)}) collective-permute-start(bf16[512,256]{1,0:T(8,128)(2,1)S(1)} %get-tuple-element.32), channel_id=1, source_target_pairs={{0,1},{1,0},{2,3},{3,2},{4,8},{5,9},{6,10},{7,11},{8,4},{9,5},{10,... | collective-permute-start | bytes 786440 | tf_op jit(solution)/shard_map/ppermute | solution.py:266
  43.9 6.4 %collective-permute-start.14 = (bf16[512,256]{1,0:T(8,128)(2,1)S(1)}, bf16[512,256]{1,0:T(8,128)(2,1)S(1)}, u32[]{:S(2)}, u32[]{:S(2)}) collective-permute-start(bf16[512,256]{1,0:T(8,128)(2,1)S(1)} %fusion.17), channel_id=1, source_target_pairs={{0,4},{4,0},{8,12},{12,8},{1,5},{5,1},{9,13},{13,9},{2,6},{6,2},{1... | collective-permute-start | bytes 786440 | tf_op jit(solution)/shard_map/ppermute | solution.py:263
  47.1 12.2 %collective-permute-start.8 = (bf16[128,2048]{1,0:T(8,128)(2,1)S(1)}, bf16[128,2048]{1,0:T(8,128)(2,1)S(1)}, u32[]{:S(2)}, u32[]{:S(2)}) collective-permute-start(bf16[128,2048]{1,0:T(8,128)(2,1)S(1)} %collective-permute-done.5.refs_1_), channel_id=1, source_target_pairs={{0,1},{1,0},{2,3},{3,2},{4,8},{5,9},{6,10},{7,11},{8,4},{9,5},{10,... | collective-permute-start | bytes 1572872 | tf_op jit(solution)/shard_map/ppermute | solution.py:266
  52.6 14.5 %collective-permute-start.2 = (bf16[128,2048]{1,0:T(8,128)(2,1)S(1)}, bf16[128,2048]{1,0:T(8,128)(2,1)S(1)}, u32[]{:S(2)}, u32[]{:S(2)}) collective-permute-start(bf16[128,2048]{1,0:T(8,128)(2,1)S(1)} %copy-done.16), channel_id=1, source_target_pairs={{0,4},{4,0},{8,12},{12,8},{1,5},{5,1},{9,13},{13,9},{2,6},{6,2},{1... | collective-permute-start | bytes 1572872 | tf_op jit(solution)/shard_map/ppermute | solution.py:263
  59.4 42.4 %copy-start.9 = (bf16[128,2048]{1,0:T(8,128)(2,1)}, bf16[128,2048]{1,0:T(8,128)(2,1)S(1)}, u32[]{:S(2)}) copy-start(bf16[128,2048]{1,0:T(8,128)(2,1)S(1)} %collective-permute-done.8.refs_4_) | copy-start | bytes 1572868
  59.4 16.0 %collective-permute-start.9 = (bf16[128,2048]{1,0:T(8,128)(2,1)S(1)}, bf16[128,2048]{1,0:T(8,128)(2,1)S(1)}, u32[]{:S(2)}, u32[]{:S(2)}) collective-permute-start(bf16[128,2048]{1,0:T(8,128)(2,1)S(1)} %collective-permute-done.8.refs_4_), channel_id=1, source_target_pairs={{0,4},{4,0},{8,12},{12,8},{1,5},{5,1},{9,13},{13,9},{2,6},{6,2},{1... | collective-permute-start | bytes 1572872 | tf_op jit(solution)/shard_map/ppermute | solution.py:263
  59.4 16.4 %collective-permute-start.6 = (bf16[128,2048]{1,0:T(8,128)(2,1)S(1)}, bf16[128,2048]{1,0:T(8,128)(2,1)S(1)}, u32[]{:S(2)}, u32[]{:S(2)}) collective-permute-start(bf16[128,2048]{1,0:T(8,128)(2,1)S(1)} %copy-done.18), channel_id=1, source_target_pairs={{0,1},{1,0},{2,3},{3,2},{4,8},{5,9},{6,10},{7,11},{8,4},{9,5},{10,... | collective-permute-start | bytes 1572872 | tf_op jit(solution)/shard_map/ppermute | solution.py:266
  60.5 26.1 %collective-permute-start.19 = (bf16[128,2048]{1,0:T(8,128)(2,1)S(1)}, bf16[128,2048]{1,0:T(8,128)(2,1)}, u32[]{:S(2)}, u32[]{:S(2)}) collective-permute-start(bf16[128,2048]{1,0:T(8,128)(2,1)S(1)} %copy-done.16), channel_id=1, source_target_pairs={{0,1},{1,0},{2,3},{3,2},{4,8},{5,9},{6,10},{7,11},{8,4},{9,5},{10,... | collective-permute-start | bytes 1572872 | tf_op jit(solution)/shard_map/ppermute | solution.py:266
  67.1 26.3 %collective-permute-start.3 = (bf16[128,2048]{1,0:T(8,128)(2,1)S(1)}, bf16[128,2048]{1,0:T(8,128)(2,1)}, u32[]{:S(2)}, u32[]{:S(2)}) collective-permute-start(bf16[128,2048]{1,0:T(8,128)(2,1)S(1)} %collective-permute-done.2.refs_1_), channel_id=1, source_target_pairs={{0,1},{1,0},{2,3},{3,2},{4,8},{5,9},{6,10},{7,11},{8,4},{9,5},{10,... | collective-permute-start | bytes 1572872 | tf_op jit(solution)/shard_map/ppermute | solution.py:266
  75.4 19.5 %collective-permute-start.29 = (bf16[128,2048]{1,0:T(8,128)(2,1)}, bf16[128,2048]{1,0:T(8,128)(2,1)}, u32[]{:S(2)}, u32[]{:S(2)}) collective-permute-start(bf16[128,2048]{1,0:T(8,128)(2,1)} %get-tuple-element.8), channel_id=1, source_target_pairs={{0,4},{4,0},{8,12},{12,8},{1,5},{5,1},{9,13},{13,9},{2,6},{6,2},{1... | collective-permute-start | bytes 1572872 | tf_op jit(solution)/shard_map/ppermute | solution.py:263
  75.8 26.0 %collective-permute-start.7 = (bf16[128,2048]{1,0:T(8,128)(2,1)S(1)}, bf16[128,2048]{1,0:T(8,128)(2,1)}, u32[]{:S(2)}, u32[]{:S(2)}) collective-permute-start(bf16[128,2048]{1,0:T(8,128)(2,1)S(1)} %collective-permute-done.6.refs_2_), channel_id=1, source_target_pairs={{0,4},{4,0},{8,12},{12,8},{1,5},{5,1},{9,13},{13,9},{2,6},{6,2},{1... | collective-permute-start | bytes 1572872 | tf_op jit(solution)/shard_map/ppermute | solution.py:263
  86.5 47.2 %collective-permute-start.20 = (bf16[128,2048]{1,0:T(8,128)(2,1)}, bf16[128,2048]{1,0:T(8,128)(2,1)}, u32[]{:S(2)}, u32[]{:S(2)}) collective-permute-start(bf16[128,2048]{1,0:T(8,128)(2,1)} %collective-permute-done.19.refs_2_), channel_id=1, source_target_pairs={{0,4},{4,0},{8,12},{12,8},{1,5},{5,1},{9,13},{13,9},{2,6},{6,2},{1... | collective-permute-start | bytes 1572872 | tf_op jit(solution)/shard_map/ppermute | solution.py:263
  93.4 30.5 %collective-permute-start.4 = (bf16[128,2048]{1,0:T(8,128)(2,1)}, bf16[128,2048]{1,0:T(8,128)(2,1)}, u32[]{:S(2)}, u32[]{:S(2)}) collective-permute-start(bf16[128,2048]{1,0:T(8,128)(2,1)} %collective-permute-done.3.refs_4_), channel_id=1, source_target_pairs={{0,4},{4,0},{8,12},{12,8},{1,5},{5,1},{9,13},{13,9},{2,6},{6,2},{1... | collective-permute-start | bytes 1572872 | tf_op jit(solution)/shard_map/ppermute | solution.py:263
  93.4 31.1 %collective-permute-start.30 = (bf16[128,2048]{1,0:T(8,128)(2,1)}, bf16[128,2048]{1,0:T(8,128)(2,1)S(1)}, u32[]{:S(2)}, u32[]{:S(2)}) collective-permute-start(bf16[128,2048]{1,0:T(8,128)(2,1)} %get-tuple-element.8), channel_id=1, source_target_pairs={{0,1},{1,0},{2,3},{3,2},{4,8},{5,9},{6,10},{7,11},{8,4},{9,5},{10,... | collective-permute-start | bytes 1572872 | tf_op jit(solution)/shard_map/ppermute | solution.py:266
  94.9 29.6 %collective-permute-start.32 = (bf16[128,2048]{1,0:T(8,128)(2,1)}, bf16[128,2048]{1,0:T(8,128)(2,1)}, u32[]{:S(2)}, u32[]{:S(2)}) collective-permute-start(bf16[128,2048]{1,0:T(8,128)(2,1)} %collective-permute-done.29.refs_1_), channel_id=1, source_target_pairs={{0,1},{1,0},{2,3},{3,2},{4,8},{5,9},{6,10},{7,11},{8,4},{9,5},{10,... | collective-permute-start | bytes 1572872 | tf_op jit(solution)/shard_map/ppermute | solution.py:266
  123.9 29.3 %collective-permute-start.17 = (bf16[128,2048]{1,0:T(8,128)(2,1)}, bf16[128,2048]{1,0:T(8,128)(2,1)}, u32[]{:S(2)}, u32[]{:S(2)}) collective-permute-start(bf16[128,2048]{1,0:T(8,128)(2,1)} %get-tuple-element.7), channel_id=1, source_target_pairs={{0,4},{4,0},{8,12},{12,8},{1,5},{5,1},{9,13},{13,9},{2,6},{6,2},{1... | collective-permute-start | bytes 1572872 | tf_op jit(solution)/shard_map/ppermute | solution.py:263
  126.8 26.5 %collective-permute-start.33 = (bf16[128,2048]{1,0:T(8,128)(2,1)}, bf16[128,2048]{1,0:T(8,128)(2,1)}, u32[]{:S(2)}, u32[]{:S(2)}) collective-permute-start(bf16[128,2048]{1,0:T(8,128)(2,1)} %get-tuple-element.17), channel_id=1, source_target_pairs={{0,4},{4,0},{8,12},{12,8},{1,5},{5,1},{9,13},{13,9},{2,6},{6,2},{1... | collective-permute-start | bytes 1572872 | tf_op jit(solution)/shard_map/ppermute | solution.py:263
  127.2 29.0 %collective-permute-start.31 = (bf16[128,2048]{1,0:T(8,128)(2,1)}, bf16[128,2048]{1,0:T(8,128)(2,1)}, u32[]{:S(2)}, u32[]{:S(2)}) collective-permute-start(bf16[128,2048]{1,0:T(8,128)(2,1)} %get-tuple-element.18), channel_id=1, source_target_pairs={{0,4},{4,0},{8,12},{12,8},{1,5},{5,1},{9,13},{13,9},{2,6},{6,2},{1... | collective-permute-start | bytes 1572872 | tf_op jit(solution)/shard_map/ppermute | solution.py:263
  131.5 45.4 %collective-permute-start.18 = (bf16[128,2048]{1,0:T(8,128)(2,1)}, bf16[128,2048]{1,0:T(8,128)(2,1)S(1)}, u32[]{:S(2)}, u32[]{:S(2)}) collective-permute-start(bf16[128,2048]{1,0:T(8,128)(2,1)} %get-tuple-element.7), channel_id=1, source_target_pairs={{0,1},{1,0},{2,3},{3,2},{4,8},{5,9},{6,10},{7,11},{8,4},{9,5},{10,... | collective-permute-start | bytes 1572872 | tf_op jit(solution)/shard_map/ppermute | solution.py:266
  153.2 23.7 %collective-permute-start.22 = (bf16[128,2048]{1,0:T(8,128)(2,1)}, bf16[128,2048]{1,0:T(8,128)(2,1)S(1)}, u32[]{:S(2)}, u32[]{:S(2)}) collective-permute-start(bf16[128,2048]{1,0:T(8,128)(2,1)} %collective-permute-done.17.refs_1_), channel_id=1, source_target_pairs={{0,1},{1,0},{2,3},{3,2},{4,8},{5,9},{6,10},{7,11},{8,4},{9,5},{10,... | collective-permute-start | bytes 1572872 | tf_op jit(solution)/shard_map/ppermute | solution.py:266
  157.8 127.5 %collective-permute-start.44 = (bf16[128,2048]{1,0:T(8,128)(2,1)S(1)}, bf16[128,2048]{1,0:T(8,128)(2,1)S(1)}, u32[]{:S(2)}, u32[]{:S(2)}) collective-permute-start(bf16[128,2048]{1,0:T(8,128)(2,1)S(1)} %get-tuple-element.9), channel_id=1, source_target_pairs={{0,1},{1,0},{2,3},{3,2},{4,8},{5,9},{6,10},{7,11},{8,4},{9,5},{10,... | collective-permute-start | bytes 1572872 | tf_op jit(solution)/shard_map/ppermute | solution.py:266
  159.3 27.1 %collective-permute-start.42 = (bf16[128,2048]{1,0:T(8,128)(2,1)S(1)}, bf16[128,2048]{1,0:T(8,128)(2,1)S(1)}, u32[]{:S(2)}, u32[]{:S(2)}) collective-permute-start(bf16[128,2048]{1,0:T(8,128)(2,1)S(1)} %get-tuple-element.10), channel_id=1, source_target_pairs={{0,1},{1,0},{2,3},{3,2},{4,8},{5,9},{6,10},{7,11},{8,4},{9,5},{10,... | collective-permute-start | bytes 1572872 | tf_op jit(solution)/shard_map/ppermute | solution.py:266
  177.1 14.4 %collective-permute-start.23 = (bf16[128,2048]{1,0:T(8,128)(2,1)S(1)}, bf16[128,2048]{1,0:T(8,128)(2,1)S(1)}, u32[]{:S(2)}, u32[]{:S(2)}) collective-permute-start(bf16[128,2048]{1,0:T(8,128)(2,1)S(1)} %get-tuple-element.27), channel_id=1, source_target_pairs={{0,4},{4,0},{8,12},{12,8},{1,5},{5,1},{9,13},{13,9},{2,6},{6,2},{1... | collective-permute-start | bytes 1572872 | tf_op jit(solution)/shard_map/ppermute | solution.py:263
  178.6 24.2 %collective-permute-start.21 = (bf16[128,2048]{1,0:T(8,128)(2,1)S(1)}, bf16[128,2048]{1,0:T(8,128)(2,1)S(1)}, u32[]{:S(2)}, u32[]{:S(2)}) collective-permute-start(bf16[128,2048]{1,0:T(8,128)(2,1)S(1)} %get-tuple-element.28), channel_id=1, source_target_pairs={{0,4},{4,0},{8,12},{12,8},{1,5},{5,1},{9,13},{13,9},{2,6},{6,2},{1... | collective-permute-start | bytes 1572872 | tf_op jit(solution)/shard_map/ppermute | solution.py:263
  179.3 41.7 %collective-permute-start.37 = (bf16[128,2048]{1,0:T(8,128)(2,1)S(1)}, bf16[128,2048]{1,0:T(8,128)(2,1)S(1)}, u32[]{:S(2)}, u32[]{:S(2)}) collective-permute-start(bf16[128,2048]{1,0:T(8,128)(2,1)S(1)} %get-tuple-element.15), channel_id=1, source_target_pairs={{0,4},{4,0},{8,12},{12,8},{1,5},{5,1},{9,13},{13,9},{2,6},{6,2},{1... | collective-permute-start | bytes 1572872 | tf_op jit(solution)/shard_map/ppermute | solution.py:263
  186.5 38.8 %collective-permute-start.34 = (bf16[128,2048]{1,0:T(8,128)(2,1)S(1)}, bf16[128,2048]{1,0:T(8,128)(2,1)S(1)}, u32[]{:S(2)}, u32[]{:S(2)}) collective-permute-start(bf16[128,2048]{1,0:T(8,128)(2,1)S(1)} %get-tuple-element.16), channel_id=1, source_target_pairs={{0,4},{4,0},{8,12},{12,8},{1,5},{5,1},{9,13},{13,9},{2,6},{6,2},{1... | collective-permute-start | bytes 1572872 | tf_op jit(solution)/shard_map/ppermute | solution.py:263
  191.6 95.8 %collective-permute-start.43 = (bf16[128,2048]{1,0:T(8,128)(2,1)S(1)}, bf16[128,2048]{1,0:T(8,128)(2,1)S(1)}, u32[]{:S(2)}, u32[]{:S(2)}) collective-permute-start(bf16[128,2048]{1,0:T(8,128)(2,1)S(1)} %fusion.13), channel_id=1, source_target_pairs={{0,4},{4,0},{8,12},{12,8},{1,5},{5,1},{9,13},{13,9},{2,6},{6,2},{1... | collective-permute-start | bytes 1572872 | tf_op jit(solution)/shard_map/ppermute | solution.py:263
  220.0 27.8 %collective-permute-start.27 = (bf16[128,2048]{1,0:T(8,128)(2,1)S(1)}, bf16[128,2048]{1,0:T(8,128)(2,1)S(1)}, u32[]{:S(2)}, u32[]{:S(2)}) collective-permute-start(bf16[128,2048]{1,0:T(8,128)(2,1)S(1)} %get-tuple-element.25), channel_id=1, source_target_pairs={{0,4},{4,0},{8,12},{12,8},{1,5},{5,1},{9,13},{13,9},{2,6},{6,2},{1... | collective-permute-start | bytes 1572872 | tf_op jit(solution)/shard_map/ppermute | solution.py:263
  221.0 38.0 %collective-permute-start.24 = (bf16[128,2048]{1,0:T(8,128)(2,1)S(1)}, bf16[128,2048]{1,0:T(8,128)(2,1)S(1)}, u32[]{:S(2)}, u32[]{:S(2)}) collective-permute-start(bf16[128,2048]{1,0:T(8,128)(2,1)S(1)} %get-tuple-element.26), channel_id=1, source_target_pairs={{0,4},{4,0},{8,12},{12,8},{1,5},{5,1},{9,13},{13,9},{2,6},{6,2},{1... | collective-permute-start | bytes 1572872 | tf_op jit(solution)/shard_map/ppermute | solution.py:263
  225.7 35.2 %collective-permute-start.35 = (bf16[128,2048]{1,0:T(8,128)(2,1)S(1)}, bf16[128,2048]{1,0:T(8,128)(2,1)S(1)}, u32[]{:S(2)}, u32[]{:S(2)}) collective-permute-start(bf16[128,2048]{1,0:T(8,128)(2,1)S(1)} %get-tuple-element.14), channel_id=1, source_target_pairs={{0,1},{1,0},{2,3},{3,2},{4,8},{5,9},{6,10},{7,11},{8,4},{9,5},{10,... | collective-permute-start | bytes 1572872 | tf_op jit(solution)/shard_map/ppermute | solution.py:266
  247.8 53.9 %collective-permute-start.38 = (bf16[128,2048]{1,0:T(8,128)(2,1)S(1)}, bf16[128,2048]{1,0:T(8,128)(2,1)S(1)}, u32[]{:S(2)}, u32[]{:S(2)}) collective-permute-start(bf16[128,2048]{1,0:T(8,128)(2,1)S(1)} %get-tuple-element.13), channel_id=1, source_target_pairs={{0,1},{1,0},{2,3},{3,2},{4,8},{5,9},{6,10},{7,11},{8,4},{9,5},{10,... | collective-permute-start | bytes 1572872 | tf_op jit(solution)/shard_map/ppermute | solution.py:266
  259.0 14.9 %collective-permute-start.39 = (bf16[128,2048]{1,0:T(8,128)(2,1)S(1)}, bf16[128,2048]{1,0:T(8,128)(2,1)S(1)}, u32[]{:S(2)}, u32[]{:S(2)}) collective-permute-start(bf16[128,2048]{1,0:T(8,128)(2,1)S(1)} %get-tuple-element.12), channel_id=1, source_target_pairs={{0,1},{1,0},{2,3},{3,2},{4,8},{5,9},{6,10},{7,11},{8,4},{9,5},{10,... | collective-permute-start | bytes 1572872 | tf_op jit(solution)/shard_map/ppermute | solution.py:266
  260.9 35.4 %copy-start.2 = (bf16[512,2048]{1,0:T(8,128)(2,1)S(1)}, bf16[512,2048]{1,0:T(8,128)(2,1)}, u32[]{:S(2)}) copy-start(bf16[512,2048]{1,0:T(8,128)(2,1)} %hidden.7) | copy-start | bytes 6291460
  260.9 24.2 %collective-permute-start.25 = (bf16[128,2048]{1,0:T(8,128)(2,1)S(1)}, bf16[128,2048]{1,0:T(8,128)(2,1)S(1)}, u32[]{:S(2)}, u32[]{:S(2)}) collective-permute-start(bf16[128,2048]{1,0:T(8,128)(2,1)S(1)} %get-tuple-element.24), channel_id=1, source_target_pairs={{0,1},{1,0},{2,3},{3,2},{4,8},{5,9},{6,10},{7,11},{8,4},{9,5},{10,... | collective-permute-start | bytes 1572872 | tf_op jit(solution)/shard_map/ppermute | solution.py:266
  273.8 22.5 %collective-permute-start.41 = (bf16[128,2048]{1,0:T(8,128)(2,1)S(1)}, bf16[128,2048]{1,0:T(8,128)(2,1)S(1)}, u32[]{:S(2)}, u32[]{:S(2)}) collective-permute-start(bf16[128,2048]{1,0:T(8,128)(2,1)S(1)} %get-tuple-element.11), channel_id=1, source_target_pairs={{0,1},{1,0},{2,3},{3,2},{4,8},{5,9},{6,10},{7,11},{8,4},{9,5},{10,... | collective-permute-start | bytes 1572872 | tf_op jit(solution)/shard_map/ppermute | solution.py:266
  285.1 14.8 %collective-permute-start.40 = (bf16[128,2048]{1,0:T(8,128)(2,1)S(1)}, bf16[128,2048]{1,0:T(8,128)(2,1)S(1)}, u32[]{:S(2)}, u32[]{:S(2)}) collective-permute-start(bf16[128,2048]{1,0:T(8,128)(2,1)S(1)} %fusion.12), channel_id=1, source_target_pairs={{0,4},{4,0},{8,12},{12,8},{1,5},{5,1},{9,13},{13,9},{2,6},{6,2},{1... | collective-permute-start | bytes 1572872 | tf_op jit(solution)/shard_map/ppermute | solution.py:263
  285.3 25.8 %collective-permute-start.36 = (bf16[128,2048]{1,0:T(8,128)(2,1)S(1)}, bf16[128,2048]{1,0:T(8,128)(2,1)S(1)}, u32[]{:S(2)}, u32[]{:S(2)}) collective-permute-start(bf16[128,2048]{1,0:T(8,128)(2,1)S(1)} %fusion.11), channel_id=1, source_target_pairs={{0,4},{4,0},{8,12},{12,8},{1,5},{5,1},{9,13},{13,9},{2,6},{6,2},{1... | collective-permute-start | bytes 1572872 | tf_op jit(solution)/shard_map/ppermute | solution.py:263
  287.4 25.6 %collective-permute-start.28 = (bf16[128,2048]{1,0:T(8,128)(2,1)S(1)}, bf16[128,2048]{1,0:T(8,128)(2,1)S(1)}, u32[]{:S(2)}, u32[]{:S(2)}) collective-permute-start(bf16[128,2048]{1,0:T(8,128)(2,1)S(1)} %get-tuple-element.23), channel_id=1, source_target_pairs={{0,1},{1,0},{2,3},{3,2},{4,8},{5,9},{6,10},{7,11},{8,4},{9,5},{10,... | collective-permute-start | bytes 1572872 | tf_op jit(solution)/shard_map/ppermute | solution.py:266
  296.3 25.0 %collective-permute-start.26 = (bf16[128,2048]{1,0:T(8,128)(2,1)S(1)}, bf16[128,2048]{1,0:T(8,128)(2,1)S(1)}, u32[]{:S(2)}, u32[]{:S(2)}) collective-permute-start(bf16[128,2048]{1,0:T(8,128)(2,1)S(1)} %fusion.10), channel_id=1, source_target_pairs={{0,4},{4,0},{8,12},{12,8},{1,5},{5,1},{9,13},{13,9},{2,6},{6,2},{1... | collective-permute-start | bytes 1572872 | tf_op jit(solution)/shard_map/ppermute | solution.py:263
  (19 other events, 143.5 us)
Sparse Core Ops, SparseCore 0:
  52.7 16.5 all-gather.1
where the time goes:
time: 331 us; the launch traced here: 330 us
  waiting for transfers between devices  157 us (47%)
  Pallas kernels  75.2 us (23%)
  starting transfers between devices  42.6 us (13%)
  between operations  24 us (7%)
  other arithmetic  16 us (5%)
  local copies, waits for them, and re-layouts  11 us (3%)
  matrix products  4.23 us (1%)
    ppermute x21, waiting for transfers between devices, outer(): return lax.ppermute(value, 'tp', self.outer_pairs)  89.8 us
    pallas_call x4, Pallas kernels, chunk_terms(): pl.pallas_call(functools.partial(chunk_kernel, count, pieces_of, low), ou...  68 us
    ppermute x18, waiting for transfers between devices, inner(): return lax.ppermute(value, ('tp', 'sp'), self.inner_pairs)  55.1 us
    ppermute x18, starting transfers between devices, inner(): return lax.ppermute(value, ('tp', 'sp'), self.inner_pairs)  22.7 us
    ppermute x21, starting transfers between devices, outer(): return lax.ppermute(value, 'tp', self.outer_pairs)  16.6 us
    unnamed x42, local copies, waits for them, and re-layouts  8.51 us
    pallas_call x4, Pallas kernels, finish(): pl.pallas_call(functools.partial(finish_kernel, count, low, inner is not...  7.27 us
  transfers between devices with their start and end apart: 46, of which 24 were waited for; matrix products, arithmetic and copies ran while one was open for 7% of the time, Pallas kernels for 22%

commit v1 on v0

v1 whole, which is shorter than its diff:
```python
import functools

import jax
import jax.numpy as jnp
from jax import lax
from jax.experimental import pallas as pl
from jax.experimental.pallas import tpu as pltpu
from jax.sharding import PartitionSpec as P

HD = 128
HQ = 32
KV = 4
DOCS = 4
PERIODS = 2
STREAMS = 2

rope_base = 500000.0
norm_eps = 1e-05
masked_score = -1e30
log2_e = 1.4426950408889634
VMEM_LIMIT = 46 * 1024 * 1024
GROUP = 2
BLOCK = 1024
VMEM = pl.BlockSpec(memory_space=pltpu.VMEM)
SMEM = pl.BlockSpec(memory_space=pltpu.SMEM)
ANY = pl.BlockSpec(memory_space=pl.ANY)


def rope_tables(positions):
    half_dim = HD // 2
    steps_index = jnp.arange(half_dim, dtype=jnp.float32)
    frequency = jnp.power(rope_base, -2.0 * steps_index / HD)
    angles = positions.astype(jnp.float32)[:, None] * frequency[None, :]
    cosine, sine = jnp.cos(angles), jnp.sin(angles)
    return jnp.concatenate([cosine, cosine], axis=1), jnp.concatenate([-sine, sine], axis=1)


def rotate(field, cosine, sine):
    half_dim = HD // 2
    swapped = jnp.concatenate([field[..., half_dim:], field[..., :half_dim]], axis=-1)
    return field * cosine + swapped * sine


def in_hbm(value):
    return pltpu.with_memory_space_constraint(value, pltpu.HBM)


def wait_for(target, sem):
    pltpu.make_async_copy(target, target, sem).wait()


def chunk_kernel(count, pieces_of, low, info_ref, *refs):
    total_pieces = len(pieces_of) + 1
    pieces = refs[:total_pieces]
    w_query, w_out, table = refs[total_pieces : total_pieces + 3]
    kv_pieces = refs[total_pieces + 3 : -13]
    out, held, query_w, out_w, rows_table, kv, query, top, acc, flat, sems, q_sems, o_sems = refs[-13:]
    rows = held.shape[0]
    width = held.shape[1] // count
    parts, depth, piece_columns = query_w.shape[0], query_w.shape[1], query_w.shape[2]
    heads = query.shape[0] // rows
    rank, start, sp_rank = info_ref[0], info_ref[1], info_ref[2]
    span = kv_pieces[0].shape[0]
    base = sp_rank * span
    even = rank % 2 == 0

    def place(source, block):
        columns = pl.ds(pl.multiple_of(block * width, width), width)
        return pltpu.make_async_copy(source, held.at[:, columns], sems.at[0])

    place(pieces[0].at[pl.ds(low, rows)], rank).start()
    for piece, (kind, step) in zip(pieces[1:], pieces_of):
        block = jnp.where(even == (kind == "outer"), rank + step, rank - step)

        @pl.when((block >= 0) & (block < count))
        def _():
            place(piece, block).start()

    def query_copy(k):
        return pltpu.make_async_copy(
            w_query.at[:, pl.ds(pl.multiple_of(k * piece_columns, piece_columns), piece_columns)],
            query_w.at[k],
            q_sems.at[k * q_sems.shape[0] // parts],
        )

    for k in range(parts):
        query_copy(k).start()
    table_copy = pltpu.make_async_copy(table.at[pl.ds(low, rows)], rows_table, sems.at[1])
    table_copy.start()
    kv_copies = [
        pltpu.make_async_copy(
            piece,
            kv.at[pl.ds(pl.multiple_of((sp_rank ^ d) * span, span), span)],
            sems.at[2],
        )
        for d, piece in enumerate(kv_pieces)
    ]
    for copy in kv_copies:
        copy.start()
    out_parts = out_w.shape[0]
    out_columns = out_w.shape[2]

    def out_copy(k):
        return pltpu.make_async_copy(
            w_out.at[:, pl.ds(pl.multiple_of(k * out_columns, out_columns), out_columns)],
            out_w.at[k],
            o_sems.at[k * o_sems.shape[0] // out_parts],
        )

    wait_for(held, sems.at[0])
    table_copy.wait()
    factor = HD ** (-0.5) * log2_e
    cos, sin = rows_table[:, :HD] * factor, rows_table[:, HD : 2 * HD] * factor
    pair = piece_columns // HD

    @pl.loop(0, parts)
    def _(k):
        query_copy(k).wait()

        @pl.when(k == 0)
        def _():
            for i in range(out_parts):
                out_copy(i).start()

        total = jnp.dot(held[...], query_w[k], preferred_element_type=jnp.float32)
        for h in range(pair):
            field = total[:, h * HD : (h + 1) * HD]
            swapped = pltpu.roll(field, HD // 2, 1)
            at = pl.multiple_of((k * pair + h) * rows, rows)
            query[pl.ds(at, rows), :] = (field * cos + swapped * sin).astype(jnp.bfloat16)

    wait_for(kv, sems.at[2])
    top[...] = jnp.full_like(top, masked_score)
    acc[...] = jnp.zeros_like(acc)
    first = rows_table[:, 2 * HD : 2 * HD + 1].astype(jnp.int32)
    row_index = base + low + lax.broadcasted_iota(jnp.int32, (rows, BLOCK), 0)
    column = lax.broadcasted_iota(jnp.int32, (rows, BLOCK), 1)
    ones = jnp.ones((BLOCK, HD), jnp.bfloat16)
    together = min(heads, GROUP)

    def step(j, carry):
        offset = pl.multiple_of(j * BLOCK, BLOCK)
        key_index = column + offset
        bias = jnp.where((key_index <= row_index) & (key_index >= first), 0.0, masked_score)
        key = kv[pl.ds(offset, BLOCK), :HD]
        value = jnp.concatenate([kv[pl.ds(offset, BLOCK), HD:], ones], axis=1)
        for g in range(heads // together):
            span = slice(g * together * rows, (g + 1) * together * rows)
            scores = lax.dot_general(
                query[span], key, (((1,), (1,)), ((), ())), preferred_element_type=jnp.float32
            )
            scores = (scores.reshape(together, rows, BLOCK) + bias[None]).reshape(-1, BLOCK)
            old = top[span]
            new = jnp.maximum(old, jnp.max(scores, axis=1, keepdims=True))
            exps = jnp.exp2(scores - new[:, :1]).astype(jnp.bfloat16)
            mixed = jnp.dot(exps, value, preferred_element_type=jnp.float32)
            keep = jnp.exp2(old - new)
            acc[span] = acc[span] * jnp.concatenate([keep, keep], axis=1) + mixed
            top[span] = new
        return carry

    lax.fori_loop(start, (base + low + rows - 1) // BLOCK + 1, step, 0)
    for h in range(heads):
        span = slice(h * rows, (h + 1) * rows)
        flat[:, h * HD : (h + 1) * HD] = (acc[span, :HD] / acc[span, HD:]).astype(jnp.bfloat16)

    per_block = width // out_columns

    @pl.loop(0, count)
    def _(b):
        for k in range(per_block):
            out_copy(b * per_block + k).wait()
            out[b, :, k * out_columns : (k + 1) * out_columns] = jnp.dot(
                flat[...], out_w[b * per_block + k], preferred_element_type=jnp.float32
            ).astype(jnp.bfloat16)


def chunk_terms(count, low, rows, scaled, arrived, info, w_query, w_out, table, kv_pieces):
    width = scaled.shape[1]
    model, columns = w_query.shape
    inner = w_out.shape[0]
    heads = columns // HD
    tokens = kv_pieces[0].shape[0] * len(kv_pieces)
    pieces = [scaled] + [piece for _, _, piece in arrived]
    pieces_of = [(kind, step) for kind, step, _ in arrived]
    q_columns = min(columns, 256)
    o_columns = min(width, 1024)
    q_parts, o_parts = columns // q_columns, model // o_columns
    return pl.pallas_call(
        functools.partial(chunk_kernel, count, pieces_of, low),
        out_shape=jax.ShapeDtypeStruct((count, rows, width), jnp.bfloat16),
        in_specs=[SMEM] + [ANY] * (len(pieces) + 3 + len(kv_pieces)),
        out_specs=VMEM,
        scratch_shapes=[
            pltpu.VMEM((rows, model), jnp.bfloat16),
            pltpu.VMEM((q_parts, model, q_columns), jnp.bfloat16),
            pltpu.VMEM((o_parts, inner, o_columns), jnp.bfloat16),
            pltpu.VMEM((rows, table.shape[1]), jnp.float32),
            pltpu.VMEM((tokens, 2 * HD), jnp.bfloat16),
            pltpu.VMEM((heads * rows, HD), jnp.bfloat16),
            pltpu.VMEM((heads * rows, HD), jnp.float32),
            pltpu.VMEM((heads * rows, 2 * HD), jnp.float32),
            pltpu.VMEM((rows, inner), jnp.bfloat16),
            pltpu.SemaphoreType.DMA((3,)),
            pltpu.SemaphoreType.DMA((q_parts,)),
            pltpu.SemaphoreType.DMA((o_parts,)),
        ],
        compiler_params=pltpu.CompilerParams(vmem_limit_bytes=VMEM_LIMIT),
        cost_estimate=pl.CostEstimate(flops=rows * model * columns, bytes_accessed=0, transcendentals=0),
        name="chunk_terms",
    )(info, *[in_hbm(x) for x in (*pieces, w_query, w_out, table, *kv_pieces)])


def kv_kernel(group, slots, info_ref, scaled, w_key, w_value, *refs):
    outs = refs[: len(slots)]
    held, key_w, value_w, key, value, sems = refs[len(slots) :]
    copies = [
        pltpu.make_async_copy(source, target, sems.at[k])
        for k, (source, target) in enumerate(((scaled, held), (w_key, key_w), (w_value, value_w)))
    ]
    for copy in copies:
        copy.start()
    copies[0].wait()
    copies[1].wait()
    key[...] = jnp.dot(held[...], key_w[...], preferred_element_type=jnp.float32).astype(jnp.bfloat16)
    copies[2].wait()
    value[...] = jnp.dot(held[...], value_w[...], preferred_element_type=jnp.float32).astype(jnp.bfloat16)
    width = outs[0].shape[-1]
    rows = key.shape[0] * 2 * HD // width
    for out, devices in zip(outs, slots):
        for n, device in enumerate(devices(info_ref[0])):
            columns = pl.ds(pl.multiple_of(device * info_ref[3] // group * HD, HD), HD)
            for i in range(width // (2 * HD)):
                at = i * 2 * HD
                span = slice(i * rows, (i + 1) * rows)
                out[n * rows : (n + 1) * rows, at : at + HD] = key[span, columns]
                out[n * rows : (n + 1) * rows, at + HD : at + 2 * HD] = value[span, columns]


def kv_terms_of(slots, info, scaled, w_key, w_value):
    rows, width = scaled.shape
    columns = w_key.shape[1]
    pack = rows * 2 * HD // width
    shapes = [
        jax.ShapeDtypeStruct((pack * len(devices(0)), width), jnp.bfloat16) for devices in slots
    ]
    return pl.pallas_call(
        functools.partial(kv_kernel, HQ // KV, slots),
        out_shape=shapes,
        in_specs=[SMEM] + [ANY] * 3,
        out_specs=[VMEM] * len(slots),
        scratch_shapes=[
            pltpu.VMEM((rows, width), jnp.bfloat16),
            pltpu.VMEM((width, columns), jnp.bfloat16),
            pltpu.VMEM((width, columns), jnp.bfloat16),
            pltpu.VMEM((rows, columns), jnp.bfloat16),
            pltpu.VMEM((rows, columns), jnp.bfloat16),
            pltpu.SemaphoreType.DMA((3,)),
        ],
        compiler_params=pltpu.CompilerParams(vmem_limit_bytes=VMEM_LIMIT),
        cost_estimate=pl.CostEstimate(flops=0, bytes_accessed=2 * rows * width, transcendentals=0),
        name="kv_terms",
    )(info, in_hbm(scaled), in_hbm(w_key), in_hbm(w_value))


def kv_total_kernel(packed, table, out):
    rows, width = packed.shape
    for i in range(width // (2 * HD)):
        at = i * 2 * HD
        span = slice(i * rows, (i + 1) * rows)
        key, value = packed[:, at : at + HD], packed[:, at + HD : at + 2 * HD]
        rotated = key * table[span, :HD] + pltpu.roll(key, HD // 2, 1) * table[span, HD : 2 * HD]
        out[span, :HD] = rotated.astype(jnp.bfloat16)
        out[span, HD:] = (value * table[span, 3 * HD :]).astype(jnp.bfloat16)


def kv_total(packed, table):
    return pl.pallas_call(
        kv_total_kernel,
        out_shape=jax.ShapeDtypeStruct((table.shape[0], 2 * HD), jnp.bfloat16),
        in_specs=[VMEM] * 2,
        out_specs=VMEM,
        compiler_params=pltpu.CompilerParams(vmem_limit_bytes=VMEM_LIMIT),
        cost_estimate=pl.CostEstimate(flops=0, bytes_accessed=8 * packed.size, transcendentals=0),
        name="kv_total",
    )(packed, table)


def finish_kernel(count, low, has_inner, info_ref, hidden, terms, outer, inner, *refs):
    out, a, b, c, d, total, sems = refs[-7:]
    rows = a.shape[0]
    rank = info_ref[0]
    copies = [
        pltpu.make_async_copy(source, target, sems.at[k])
        for k, (source, target) in enumerate(
            [(hidden.at[pl.ds(low, rows)], a), (terms.at[rank], b), (outer, c), (inner, d)]
        )
    ]
    for copy in copies:
        copy.start()
    for copy in copies:
        copy.wait()
    summed = b[...].astype(jnp.float32) + c[...].astype(jnp.float32)
    middle = (rank > 0) & (rank < count - 1)
    other = jnp.where(middle, d[...].astype(jnp.float32), 0.0)
    total[...] = (a[...].astype(jnp.float32) + (summed + other)).astype(jnp.bfloat16)
    copy = pltpu.make_async_copy(total, out.at[pl.ds(low, rows)], sems.at[4])
    copy.start()
    copy.wait()


def finish(count, low, info, hidden, terms, last, out):
    _, rows, width = terms.shape
    outer, inner = last
    operands = [info, hidden, terms, outer, inner if inner is not None else outer]
    aliases = {}
    if out is not None:
        aliases = {len(operands): 0}
        operands.append(out)
    return pl.pallas_call(
        functools.partial(finish_kernel, count, low, inner is not None),
        out_shape=jax.ShapeDtypeStruct(hidden.shape, jnp.bfloat16),
        in_specs=[SMEM] + [ANY] * (len(operands) - 1),
        out_specs=ANY,
        scratch_shapes=[pltpu.VMEM((rows, width), jnp.bfloat16)] * 5 + [pltpu.SemaphoreType.DMA((5,))],
        input_output_aliases=aliases,
        cost_estimate=pl.CostEstimate(flops=0, bytes_accessed=6 * rows * width, transcendentals=0),
        compiler_params=pltpu.CompilerParams(vmem_limit_bytes=VMEM_LIMIT),
        name="finish",
    )(*operands)


def after(value, others):
    return lax.optimization_barrier((value, others))[0]


def exchange_sum(value, axis, size):
    parts = [lax.ppermute(value, axis, [(i, i ^ d) for i in range(size)]) for d in range(1, size)]
    return sum(parts, value)


class Line:
    def __init__(self, count, sp_count, rank):
        self.count, self.rank = count, rank
        self.even = rank % 2 == 0
        self.middle = (rank > 0) & (rank < count - 1)
        self.outer_pairs = [(i, i ^ 1) for i in range(count)]
        self.inner_pairs = []
        for i in range(count):
            for s in range(sp_count):
                partner = i + 1 if i % 2 else i - 1
                if 0 < i < count - 1:
                    self.inner_pairs.append((i * sp_count + s, partner * sp_count + s))
                else:
                    self.inner_pairs.append((i * sp_count + s, i * sp_count + (s ^ 1)))

    def outer(self, value, step=None, gather=True):
        pairs = self.outer_pairs
        if step is not None and gather:
            pairs = [
                (i, p) for i, p in pairs if (i >= step - 1 if i % 2 == 0 else i <= self.count - step)
            ]
        elif step is not None:
            pairs = [
                (i, p) for i, p in pairs if (i <= step - 1 if i % 2 == 0 else i >= self.count - step)
            ]
        return lax.ppermute(value, "tp", pairs)

    def inner(self, value):
        return lax.ppermute(value, ("tp", "sp"), self.inner_pairs)

    def term(self, terms, upward, step):
        dest = jnp.where(upward, self.rank + self.count - step, self.rank - self.count + step)
        valid = (dest >= 0) & (dest < self.count)
        return lax.dynamic_index_in_dim(terms, jnp.clip(dest, 0, self.count - 1), 0, False), valid

    def round(self, step, own, terms, last, earlier):
        count = self.count
        from_outer, from_inner = last
        gather_outer = own is not None and step < count
        gather_inner = own is not None and step < count - 1
        scatter_outer = terms is not None and step > 1
        scatter_inner = terms is not None and step > 2
        to_outer = to_inner = None
        if gather_outer:
            to_outer = own if step == 1 else from_inner
        if gather_inner:
            to_inner = own if step == 1 else from_outer
        if scatter_outer:
            mine, valid = self.term(terms, self.even, step - 1)
            if step > 3:
                added = (mine.astype(jnp.float32) + from_inner.astype(jnp.float32)).astype(jnp.bfloat16)
                mine = jnp.where(self.middle, added, mine)
            to_outer = mine if to_outer is None else jnp.where(valid, mine, to_outer)
        if scatter_inner:
            mine, valid = self.term(terms, ~self.even, step - 1)
            mine = (mine.astype(jnp.float32) + from_outer.astype(jnp.float32)).astype(jnp.bfloat16)
            to_inner = mine if to_inner is None else jnp.where(valid, mine, to_inner)
        to_outer, to_inner = after((to_outer, to_inner), earlier)
        alone = step if terms is None and step > 1 else None
        got_outer = None if to_outer is None else self.outer(to_outer, alone)
        got_inner = None if to_inner is None else self.inner(to_inner)
        return got_outer, got_inner

    def scatter(self, terms, earlier):
        last = (None, None)
        for step in range(2, self.count + 1):
            last = self.round(step, None, terms, last, earlier)
        return self.total(terms, last)

    def add(self, a, b):
        return (a.astype(jnp.float32) + b.astype(jnp.float32)).astype(jnp.bfloat16)

    def total(self, terms, last):
        mine = lax.dynamic_index_in_dim(terms, self.rank, 0, False).astype(jnp.float32)
        mine = mine + last[0].astype(jnp.float32)
        return jnp.where(self.middle, mine + last[1].astype(jnp.float32), mine)


def make_body(count, sp_count):
    def body(hidden, doc_ids, gain, w_query, w_key, w_value, w_out):
        rows, width = hidden.shape
        rank = lax.axis_index("tp")
        sp_rank = lax.axis_index("sp")
        heads = w_query.shape[1] // HD
        group = HQ // KV
        model = width * count
        line = Line(count, sp_count, rank)
        gain_own = lax.dynamic_slice_in_dim(gain, rank * width, width, 0).astype(jnp.float32)
        hidden_f = hidden.astype(jnp.float32)
        scaled = (hidden_f * gain_own[None, :]).astype(jnp.bfloat16)
        squares = exchange_sum(jnp.sum(hidden_f * hidden_f, axis=1), "tp", count)
        chunk = rows // (PERIODS * STREAMS)

        labels = jnp.arange(DOCS, dtype=jnp.int32)
        starts = exchange_sum(
            jnp.sum((doc_ids[None, :] < labels[:, None]).astype(jnp.int32), axis=1), "sp", sp_count
        )
        pack = rows * 2 * HD // width
        packed = count == 4 and chunk == 2 * pack
        kv_info = jnp.stack([rank, rank, rank, jnp.int32(heads)]).astype(jnp.int32)
        if packed:
            ends, across, swap, kv_own = kv_terms_of(
                (
                    lambda r: (3 - r, jnp.where(r == 0, 2, 1)),
                    lambda r: (jnp.where(r == 1, 3, 0), jnp.where(r == 1, 2, 1)),
                    lambda r: (r ^ 1,),
                    lambda r: (r,),
                ),
                kv_info,
                after(scaled, squares),
                w_key,
                w_value,
            )
        else:
            (kv_terms,) = kv_terms_of((lambda r: tuple(range(count)),), kv_info, scaled, w_key, w_value)
            kv_terms = kv_terms.reshape(count, pack, width)

        def positions():
            base = sp_rank * rows
            own_index = base + jnp.arange(rows, dtype=jnp.int32)
            first = jnp.sum(
                jnp.where(doc_ids[:, None] == labels[None, :], starts[None, :], 0), axis=1
            )
            cosine, sine = rope_tables(own_index - first)
            inverse = lax.rsqrt(squares / model + norm_eps)[:, None]
            table = jnp.concatenate(
                [
                    cosine * inverse,
                    sine * inverse,
                    jnp.broadcast_to(first.astype(jnp.float32)[:, None], (rows, HD)),
                    jnp.broadcast_to(inverse, (rows, HD)),
                ],
                axis=1,
            )
            infos = [
                jnp.stack([rank, first[k * chunk] // BLOCK, sp_rank]).astype(jnp.int32)
                for k in range(PERIODS * STREAMS)
            ]
            return table, infos

        out = None
        kv_pieces = None
        last = [(None, None)] * STREAMS
        terms = [None] * STREAMS
        history = []
        for period in range(PERIODS + 1):
            gather = period < PERIODS
            owns = [None] * STREAMS
            arrived = [[] for _ in range(STREAMS)]
            for step in range(1, count + 1):
                for j in range(STREAMS):
                    if not (gather and step < count) and not (terms[j] is not None and step > 1):
                        continue
                    if gather and step == 1:
                        low = (period * STREAMS + j) * chunk
                        owns[j] = scaled[low : low + chunk]
                    earlier = [history[-STREAMS - 1 : -STREAMS], last[j]]

                    last[j] = line.round(step, owns[j], terms[j], last[j], earlier)
                    history.append(last[j])
                    if gather and step < count:
                        arrived[j].append(("outer", step, last[j][0]))
                        if step < count - 1:
                            arrived[j].append(("inner", step, last[j][1]))
                    if packed and period == 0 and j == STREAMS - 1 and step == 1:
                        met = line.outer(ends, 1, gather=False)
                        crossed = line.inner(after(line.add(across, met), last[j]))
                    if packed and period == 0 and j == STREAMS - 1 and step == 2:
                        mine = jnp.where(line.middle, line.add(swap, crossed[:pack]), swap)
                        met = line.outer(after(mine, last[j])).astype(jnp.float32)
                        kv = kv_own.astype(jnp.float32) + met
                        kv = jnp.where(line.middle, kv + crossed[pack:].astype(jnp.float32), kv)
            if period == 0:
                table, infos = positions()
                if not packed:
                    kv = line.scatter(kv_terms, history[-1])
                kv = kv_total(kv, table)
                kv_pieces = [kv] + [
                    lax.ppermute(kv, "sp", [(i, i ^ d) for i in range(sp_count)])
                    for d in range(1, sp_count)
                ]
            for j in range(STREAMS):
                if terms[j] is not None:
                    low = ((period - 1) * STREAMS + j) * chunk
                    out = finish(count, low, infos[0], hidden, terms[j], last[j], out)
                if gather:
                    k = period * STREAMS + j
                    terms[j] = chunk_terms(
                        count, k * chunk, chunk, scaled, arrived[j], infos[k], w_query, w_out, table, kv_pieces
                    )
        return out

    return body


def solution(mesh):
    placed = (
        P(("rep", "sp"), "tp"),
        P(("rep", "sp")),
        P(),
        P(None, "tp"),
        P("tp", None),
        P("tp", None),
        P("tp", None),
    )
    body = make_body(mesh.shape["tp"], mesh.shape["sp"])
    return jax.shard_map(
        body, mesh=mesh, in_specs=placed, out_specs=P(("rep", "sp"), "tp"), check_vma=False
    )
```

time: 331 us -> 287 us (0.87)
  waiting for transfers between devices: 157 us -> 119 us
  between operations: 24 us -> 10.3 us
  starting transfers between devices: 42.6 us -> 55.7 us
  matrix products: 4.23 us -> 0 us
    ppermute x27 -> x31, waiting for transfers between devices: 102 us -> 62 us  [the longest x22 58.7 us: outer(): return lax.ppermute(value, 'tp', pairs)]
    ppermute x27 -> x31, starting transfers between devices: 19.9 us -> 30.7 us  [the longest x22 23.4 us: outer(): return lax.ppermute(value, 'tp', pairs)]
    pallas_call x0 -> x2, Pallas kernels: none -> 5.69 us  [the longest x1 5.55 us: kv_terms_of(): pl.pallas_call(functools.partial(kv_kernel, HQ // KV, slots), out_shape=s...]
    dot_general x2 -> x0, matrix products: 4.23 us -> none  [the longest x1 2.98 us: body(): jnp.dot(scaled, w_value, preferred_element_type=jnp.float32)]
    pallas_call x4, Pallas kernels: 68 us -> 64.4 us  [chunk_terms(): pl.pallas_call(functools.partial(chunk_kernel, count, pieces_of, low), ou...]
    unnamed x42 -> x62, local copies, waits for them, and re-layouts: 8.51 us -> 5.29 us
    ppermute x18 -> x17, starting transfers between devices: 22.7 us -> 25 us  [inner(): return lax.ppermute(value, ('tp', 'sp'), self.inner_pairs)]
    ppermute x18 -> x17, waiting for transfers between devices: 55.1 us -> 56.6 us  [inner(): return lax.ppermute(value, ('tp', 'sp'), self.inner_pairs)]
  transfers between devices with their start and end apart: 46 -> 48, of which waited for: 24 -> 20; matrix products, arithmetic and copies ran while one was open for 7% -> 5% of each run, Pallas kernels for 22% -> 26%
where the time goes in v1:
time: 287 us; the launch traced here: 286 us
  waiting for transfers between devices  119 us (41%)
  Pallas kernels  77.4 us (27%)
  starting transfers between devices  55.7 us (19%)
  other arithmetic  15.1 us (5%)
  between operations  10.3 us (4%)
  local copies, waits for them, and re-layouts  8.7 us (3%)
    pallas_call x4, Pallas kernels, chunk_terms(): pl.pallas_call(functools.partial(chunk_kernel, count, pieces_of, low), ou...  64.4 us
    ppermute x22, waiting for transfers between devices, outer(): return lax.ppermute(value, 'tp', pairs)  58.7 us
    ppermute x17, waiting for transfers between devices, inner(): return lax.ppermute(value, ('tp', 'sp'), self.inner_pairs)  56.6 us
    ppermute x17, starting transfers between devices, inner(): return lax.ppermute(value, ('tp', 'sp'), self.inner_pairs)  25 us
    ppermute x22, starting transfers between devices, outer(): return lax.ppermute(value, 'tp', pairs)  23.4 us
    pallas_call x4, Pallas kernels, finish(): pl.pallas_call(functools.partial(finish_kernel, count, low, inner is not...  7.27 us
  transfers between devices with their start and end apart: 48, of which 20 were waited for; matrix products, arithmetic and copies ran while one was open for 5% of the time, Pallas kernels for 26%

profile of v1, /device:TPU:10, one launch (start us, length us, event | category | flops | bytes accessed | tf_op | source)
XLA Modules:
  0.0 285.8 jit_solution(2744591785661174149)
XLA Ops:
  0.7 2.3 fusion.1
  3.0 1.6 collective-permute-start.17
  8.5 1.5 collective-permute-start.3
  10.1 5.5 %kv_terms.1 = (bf16[128,2048]{1,0:T(8,128)(2,1)S(1)}, bf16[128,2048]{1,0:T(8,128)(2,1)S(1)}, bf16[64,2048]{1,0:T(8,128)(2,1)S(1)}, bf16[64,2048]{1,0:T(8,128)(2,1)S(1)}) custom-call(s32[4]{0:T(128)S(1)} %pad_add_fusion.info_ref, bf16[512,2048]{1,0:T(8,128)(2,1)} %copy-done.11, bf16[2048,512]{1,0:T(8,128)(2,1)} %w_key.1, bf16[2048,512]{1,0:T(8,128)(2,1)} %w_value.1), custom_call_target="tpu_custom_call" | custom-call | bytes 2097152 | tf_op jit(solution)/shard_map/kv_terms/pallas_call | solution.py:247
  18.3 1.8 collective-permute-done.2
  20.7 3.4 %collective-permute-start.6 = (bf16[128,2048]{1,0:T(8,128)(2,1)}, bf16[128,2048]{1,0:T(8,128)(2,1)S(1)}, u32[]{:S(2)}, u32[]{:S(2)}) collective-permute-start(bf16[128,2048]{1,0:T(8,128)(2,1)} %get-tuple-element.52), channel_id=1, source_target_pairs={{0,4},{4,0},{8,12},{12,8},{1,5},{5,1},{9,13},{13,9},{2,6},{6,2},{1... | collective-permute-start | bytes 1572872 | tf_op jit(solution)/shard_map/ppermute | solution.py:367
  24.2 2.1 collective-permute-start.7
  26.5 2.1 collective-permute-start.8
  28.6 7.8 %collective-permute-done.18 = bf16[128,2048]{1,0:T(8,128)(2,1)} collective-permute-done((bf16[128,2048]{1,0:T(8,128)(2,1)S(1)}, bf16[128,2048]{1,0:T(8,128)(2,1)}, u32[]{:S(2)}, u32[]{:S(2)}) %collective-permute-start.18) | collective-permute-done | bytes 524320 | tf_op jit(solution)/shard_map/ppermute | solution.py:367
  36.4 2.0 add_convert_fusion.4
  38.3 7.1 %collective-permute-done.6.refs_1_ = bf16[128,2048]{1,0:T(8,128)(2,1)S(1)} collective-permute-done((bf16[128,2048]{1,0:T(8,128)(2,1)}, bf16[128,2048]{1,0:T(8,128)(2,1)S(1)}, u32[]{:S(2)}, u32[]{:S(2)}) %collective-permute-start.6) | collective-permute-done | bytes 524320 | tf_op jit(solution)/shard_map/ppermute | solution.py:367
  45.5 1.8 collective-permute-start.19
  54.0 7.9 %collective-permute-done.19 = bf16[128,2048]{1,0:T(8,128)(2,1)} collective-permute-done((bf16[128,2048]{1,0:T(8,128)(2,1)}, bf16[128,2048]{1,0:T(8,128)(2,1)}, u32[]{:S(2)}, u32[]{:S(2)}) %collective-permute-start.19) | collective-permute-done | bytes 524320 | tf_op jit(solution)/shard_map/ppermute | solution.py:370
  62.9 9.1 %collective-permute-done.10.refs_4_ = bf16[128,2048]{1,0:T(8,128)(2,1)} collective-permute-done((bf16[128,2048]{1,0:T(8,128)(2,1)S(1)}, bf16[128,2048]{1,0:T(8,128)(2,1)}, u32[]{:S(2)}, u32[]{:S(2)}) %collective-permute-start.10) | collective-permute-done | bytes 524320 | tf_op jit(solution)/shard_map/ppermute | solution.py:370
  73.4 4.0 %collective-permute-start.12 = (bf16[128,2048]{1,0:T(8,128)(2,1)}, bf16[128,2048]{1,0:T(8,128)(2,1)}, u32[]{:S(2)}, u32[]{:S(2)}) collective-permute-start(bf16[128,2048]{1,0:T(8,128)(2,1)} %collective-permute-done.10.refs_4_), channel_id=1, source_target_pairs={{4,0},{8,12},{5,1},{9,13},{6,2},{10,14},{7,3},{11,15},{20,16},{24,... | collective-permute-start | bytes 1572872 | tf_op jit(solution)/shard_map/ppermute | solution.py:367
  77.4 1.7 collective-permute-start.25
  87.3 1.6 collective-permute-done.12.refs_5_
  88.9 2.5 collective-permute-start.13
  91.4 1.7 collective-permute-start.14
  93.9 2.1 collective-permute-start.24
  96.8 16.0 %chunk_terms.5.terms = bf16[4,128,2048]{2,1,0:T(8,128)(2,1)S(1)} custom-call(s32[3]{0:T(128)S(1)} %add_add_fusion.1.info_ref, bf16[512,2048]{1,0:T(8,128)(2,1)} %copy-done.11, bf16[128,2048]{1,0:T(8,128)(2,1)} %copy-done.23, bf16[128,2048]{1,0:T(8,128)(2,1)} %copy-done.22, bf16[128,2048]{1,0:T(8,128)(2,1)} %collective-permute-done.8.refs_3_, ...), custom_call_target="tpu_custom_call" | custom-call | flops 1073741824 | tf_op jit(solution)/shard_map/chunk_terms/pallas_call | solution.py:189
  112.9 1.5 bitcast_select_fusion.1
  115.6 16.2 %chunk_terms.4.terms = bf16[4,128,2048]{2,1,0:T(8,128)(2,1)S(1)} custom-call(s32[3]{0:T(128)S(1)} %add_add_fusion.3.info_ref, bf16[512,2048]{1,0:T(8,128)(2,1)} %copy-done.11, bf16[128,2048]{1,0:T(8,128)(2,1)} %copy-done.24, bf16[128,2048]{1,0:T(8,128)(2,1)} %collective-permute-done.7.refs_2_, bf16[128,2048]{1,0:T(8,128)(2,1)} %copy-done.25, ...), custom_call_target="tpu_custom_call" | custom-call | flops 1073741824 | tf_op jit(solution)/shard_map/chunk_terms/pallas_call | solution.py:189
  131.8 1.8 collective-permute-start.29
  135.5 11.2 %collective-permute-done.29.refs_4_ = bf16[128,2048]{1,0:T(8,128)(2,1)S(1)} collective-permute-done((bf16[128,2048]{1,0:T(8,128)(2,1)S(1)}, bf16[128,2048]{1,0:T(8,128)(2,1)S(1)}, u32[]{:S(2)}, u32[]{:S(2)}) %collective-permute-start.29) | collective-permute-done | bytes 524320 | tf_op jit(solution)/shard_map/ppermute | solution.py:370
  146.8 1.8 collective-permute-start.31
  148.7 9.2 %collective-permute-done.27.refs_4_ = bf16[128,2048]{1,0:T(8,128)(2,1)S(1)} collective-permute-done((bf16[128,2048]{1,0:T(8,128)(2,1)S(1)}, bf16[128,2048]{1,0:T(8,128)(2,1)S(1)}, u32[]{:S(2)}, u32[]{:S(2)}) %collective-permute-start.27) | collective-permute-done | bytes 524320 | tf_op jit(solution)/shard_map/ppermute | solution.py:370
  158.1 1.8 collective-permute-start.35
  159.9 9.3 %collective-permute-done.31 = bf16[128,2048]{1,0:T(8,128)(2,1)S(1)} collective-permute-done((bf16[128,2048]{1,0:T(8,128)(2,1)S(1)}, bf16[128,2048]{1,0:T(8,128)(2,1)S(1)}, u32[]{:S(2)}, u32[]{:S(2)}) %collective-permute-start.31) | collective-permute-done | bytes 524320 | tf_op jit(solution)/shard_map/ppermute | solution.py:370
  169.6 1.8 collective-permute-start.34
  172.4 8.0 %collective-permute-done.35 = bf16[128,2048]{1,0:T(8,128)(2,1)S(1)} collective-permute-done((bf16[128,2048]{1,0:T(8,128)(2,1)S(1)}, bf16[128,2048]{1,0:T(8,128)(2,1)S(1)}, u32[]{:S(2)}, u32[]{:S(2)}) %collective-permute-start.35) | collective-permute-done | bytes 524320 | tf_op jit(solution)/shard_map/ppermute | solution.py:370
  181.4 1.7 collective-permute-start.37
  183.1 16.0 %chunk_terms.7.terms = bf16[4,128,2048]{2,1,0:T(8,128)(2,1)S(1)} custom-call(s32[3]{0:T(128)S(1)} %add_add_fusion.4.info_ref, bf16[512,2048]{1,0:T(8,128)(2,1)} %copy-done.11, bf16[128,2048]{1,0:T(8,128)(2,1)} %copy-done.28, bf16[128,2048]{1,0:T(8,128)(2,1)} %collective-permute-done.25.refs_2_, bf16[128,2048]{1,0:T(8,128)(2,1)} %copy-done.17, ...), custom_call_target="tpu_custom_call" | custom-call | flops 1073741824 | tf_op jit(solution)/shard_map/chunk_terms/pallas_call | solution.py:189
  206.1 16.2 %chunk_terms.6.terms = bf16[4,128,2048]{2,1,0:T(8,128)(2,1)S(1)} custom-call(s32[3]{0:T(128)S(1)} %add_add_fusion.2.info_ref, bf16[512,2048]{1,0:T(8,128)(2,1)} %copy-done.11, bf16[128,2048]{1,0:T(8,128)(2,1)} %copy-done.26, bf16[128,2048]{1,0:T(8,128)(2,1)} %copy-done.19, bf16[128,2048]{1,0:T(8,128)(2,1)} %copy-done.15, bf16[128,2048]{1,0:T(8,128)(2,1)} %copy-done.20, ...), custom_call_target="tpu_custom_call" | custom-call | flops 1073741824 | tf_op jit(solution)/shard_map/chunk_terms/pallas_call | solution.py:189
  222.5 1.8 collective-permute-start.38
  227.5 9.7 %collective-permute-done.38 = bf16[128,2048]{1,0:T(8,128)(2,1)S(1)} collective-permute-done((bf16[128,2048]{1,0:T(8,128)(2,1)S(1)}, bf16[128,2048]{1,0:T(8,128)(2,1)S(1)}, u32[]{:S(2)}, u32[]{:S(2)}) %collective-permute-start.38) | collective-permute-done | bytes 524320 | tf_op jit(solution)/shard_map/ppermute | solution.py:367
  237.4 1.8 collective-permute-start.40
  239.4 9.1 %collective-permute-done.42 = bf16[128,2048]{1,0:T(8,128)(2,1)S(1)} collective-permute-done((bf16[128,2048]{1,0:T(8,128)(2,1)S(1)}, bf16[128,2048]{1,0:T(8,128)(2,1)S(1)}, u32[]{:S(2)}, u32[]{:S(2)}) %collective-permute-start.42) | collective-permute-done | bytes 524320 | tf_op jit(solution)/shard_map/ppermute | solution.py:367
  248.9 1.7 collective-permute-done.40
  250.7 8.3 %collective-permute-done.41 = bf16[128,2048]{1,0:T(8,128)(2,1)S(1)} collective-permute-done((bf16[128,2048]{1,0:T(8,128)(2,1)S(1)}, bf16[128,2048]{1,0:T(8,128)(2,1)S(1)}, u32[]{:S(2)}, u32[]{:S(2)}) %collective-permute-start.41) | collective-permute-done | bytes 524320 | tf_op jit(solution)/shard_map/ppermute | solution.py:367
  259.5 1.7 collective-permute-start.47
  261.3 1.7 collective-permute-start.45
  263.0 1.8 finish.4.refs_0_
  264.8 1.8 finish.5.refs_0_
  266.7 7.4 %collective-permute-done.46.outer = bf16[128,2048]{1,0:T(8,128)(2,1)S(1)} collective-permute-done((bf16[128,2048]{1,0:T(8,128)(2,1)S(1)}, bf16[128,2048]{1,0:T(8,128)(2,1)S(1)}, u32[]{:S(2)}, u32[]{:S(2)}) %collective-permute-start.46) | collective-permute-done | bytes 524320 | tf_op jit(solution)/shard_map/ppermute | solution.py:367
  274.4 1.8 finish.6.refs_0_
  276.2 7.5 %collective-permute-done.44.outer = bf16[128,2048]{1,0:T(8,128)(2,1)S(1)} collective-permute-done((bf16[128,2048]{1,0:T(8,128)(2,1)S(1)}, bf16[128,2048]{1,0:T(8,128)(2,1)S(1)}, u32[]{:S(2)}, u32[]{:S(2)}) %collective-permute-start.44) | collective-permute-done | bytes 524320 | tf_op jit(solution)/shard_map/ppermute | solution.py:367
  283.8 1.8 finish.7
  (161 shorter events, 35.3 us)
Async XLA Ops:
  3.0 7.1 %collective-permute-start.17 = (f32[512]{0:T(512)S(1)}, f32[512]{0:T(512)S(1)}, u32[]{:S(2)}, u32[]{:S(2)}) collective-permute-start(f32[512]{0:T(512)S(1)} %get-tuple-element.101), channel_id=1, source_target_pairs={{0,12},{4,8},{8,4},{12,0},{1,13},{5,9},{9,5},{13,1},{2,14},{6,10},... | collective-permute-start | bytes 6152 | tf_op jit(solution)/shard_map/ppermute | solution.py:338
  4.6 5.4 %collective-permute-start.16 = (f32[512]{0:T(512)S(1)}, f32[512]{0:T(512)S(1)}, u32[]{:S(2)}, u32[]{:S(2)}) collective-permute-start(f32[512]{0:T(512)S(1)} %get-tuple-element.101), channel_id=1, source_target_pairs={{0,8},{4,12},{8,0},{12,4},{1,9},{5,13},{9,1},{13,5},{2,10},{6,14},... | collective-permute-start | bytes 6152 | tf_op jit(solution)/shard_map/ppermute | solution.py:338
  5.9 4.2 %collective-permute-start.15 = (f32[512]{0:T(512)S(1)}, f32[512]{0:T(512)S(1)}, u32[]{:S(2)}, u32[]{:S(2)}) collective-permute-start(f32[512]{0:T(512)S(1)} %get-tuple-element.101), channel_id=1, source_target_pairs={{0,4},{4,0},{8,12},{12,8},{1,5},{5,1},{9,13},{13,9},{2,6},{6,2},{1... | collective-permute-start | bytes 6152 | tf_op jit(solution)/shard_map/ppermute | solution.py:338
  8.5 17.9 %collective-permute-start.3 = (bf16[128,2048]{1,0:T(8,128)(2,1)}, bf16[128,2048]{1,0:T(8,128)(2,1)S(1)}, u32[]{:S(2)}, u32[]{:S(2)}) collective-permute-start(bf16[128,2048]{1,0:T(8,128)(2,1)} %get-tuple-element.49), channel_id=1, source_target_pairs={{0,1},{1,0},{2,3},{3,2},{4,8},{5,9},{6,10},{7,11},{8,4},{9,5},{10,... | collective-permute-start | bytes 1572872 | tf_op jit(solution)/shard_map/ppermute | solution.py:370
  10.0 16.4 %collective-permute-start.4 = (bf16[128,2048]{1,0:T(8,128)(2,1)}, bf16[128,2048]{1,0:T(8,128)(2,1)S(1)}, u32[]{:S(2)}, u32[]{:S(2)}) collective-permute-start(bf16[128,2048]{1,0:T(8,128)(2,1)} %get-tuple-element.49), channel_id=1, source_target_pairs={{0,4},{4,0},{8,12},{12,8},{1,5},{5,1},{9,13},{13,9},{2,6},{6,2},{1... | collective-permute-start | bytes 1572872 | tf_op jit(solution)/shard_map/ppermute | solution.py:367
  15.6 20.7 %collective-permute-start.18 = (bf16[128,2048]{1,0:T(8,128)(2,1)S(1)}, bf16[128,2048]{1,0:T(8,128)(2,1)}, u32[]{:S(2)}, u32[]{:S(2)}) collective-permute-start(bf16[128,2048]{1,0:T(8,128)(2,1)S(1)} %get-tuple-element.64), channel_id=1, source_target_pairs={{0,4},{12,8},{1,5},{13,9},{2,6},{14,10},{3,7},{15,11},{16,20},{28,... | collective-permute-start | bytes 1572872 | tf_op jit(solution)/shard_map/ppermute | solution.py:367
  17.1 3.0 %collective-permute-start.2 = (s32[4]{0:T(128)S(1)}, s32[4]{0:T(128)S(1)}, u32[]{:S(2)}, u32[]{:S(2)}) collective-permute-start(s32[4]{0:T(128)S(1)} %convert_reduce_fusion), channel_id=1, source_target_pairs={{0,3},{1,2},{2,1},{3,0},{4,7},{5,6},{6,5},{7,4},{8,11},{9,10},{10,... | collective-permute-start | bytes 56 | tf_op jit(solution)/shard_map/ppermute | solution.py:338
  17.1 3.6 %collective-permute-start.1 = (s32[4]{0:T(128)S(1)}, s32[4]{0:T(128)S(1)}, u32[]{:S(2)}, u32[]{:S(2)}) collective-permute-start(s32[4]{0:T(128)S(1)} %convert_reduce_fusion), channel_id=1, source_target_pairs={{0,2},{1,3},{2,0},{3,1},{4,6},{5,7},{6,4},{7,5},{8,10},{9,11},{10,... | collective-permute-start | bytes 56 | tf_op jit(solution)/shard_map/ppermute | solution.py:338
  20.1 4.1 %collective-permute-start = (s32[4]{0:T(128)S(1)}, s32[4]{0:T(128)S(1)}, u32[]{:S(2)}, u32[]{:S(2)}) collective-permute-start(s32[4]{0:T(128)S(1)} %convert_reduce_fusion), channel_id=1, source_target_pairs={{0,1},{1,0},{2,3},{3,2},{4,5},{5,4},{6,7},{7,6},{8,9},{9,8},{10,11... | collective-permute-start | bytes 56 | tf_op jit(solution)/shard_map/ppermute | solution.py:338
  20.7 24.7 %collective-permute-start.6 = (bf16[128,2048]{1,0:T(8,128)(2,1)}, bf16[128,2048]{1,0:T(8,128)(2,1)S(1)}, u32[]{:S(2)}, u32[]{:S(2)}) collective-permute-start(bf16[128,2048]{1,0:T(8,128)(2,1)} %get-tuple-element.52), channel_id=1, source_target_pairs={{0,4},{4,0},{8,12},{12,8},{1,5},{5,1},{9,13},{13,9},{2,6},{6,2},{1... | collective-permute-start | bytes 1572872 | tf_op jit(solution)/shard_map/ppermute | solution.py:367
  24.2 21.3 %collective-permute-start.7 = (bf16[128,2048]{1,0:T(8,128)(2,1)}, bf16[128,2048]{1,0:T(8,128)(2,1)}, u32[]{:S(2)}, u32[]{:S(2)}) collective-permute-start(bf16[128,2048]{1,0:T(8,128)(2,1)} %get-tuple-element.52), channel_id=1, source_target_pairs={{0,1},{1,0},{2,3},{3,2},{4,8},{5,9},{6,10},{7,11},{8,4},{9,5},{10,... | collective-permute-start | bytes 1572872 | tf_op jit(solution)/shard_map/ppermute | solution.py:370
  26.4 26.3 %collective-permute-start.5 = (bf16[128,2048]{1,0:T(8,128)(2,1)S(1)}, bf16[128,2048]{1,0:T(8,128)(2,1)}, u32[]{:S(2)}, u32[]{:S(2)}) collective-permute-start(bf16[128,2048]{1,0:T(8,128)(2,1)S(1)} %collective-permute-done.4.refs_1_), channel_id=1, source_target_pairs={{0,1},{1,0},{2,3},{3,2},{4,8},{5,9},{6,10},{7,11},{8,4},{9,5},{10,... | collective-permute-start | bytes 1572872 | tf_op jit(solution)/shard_map/ppermute | solution.py:370
  26.5 26.2 %collective-permute-start.8 = (bf16[128,2048]{1,0:T(8,128)(2,1)S(1)}, bf16[128,2048]{1,0:T(8,128)(2,1)}, u32[]{:S(2)}, u32[]{:S(2)}) collective-permute-start(bf16[128,2048]{1,0:T(8,128)(2,1)S(1)} %collective-permute-done.3.refs_2_), channel_id=1, source_target_pairs={{4,0},{8,12},{5,1},{9,13},{6,2},{10,14},{7,3},{11,15},{20,16},{24,... | collective-permute-start | bytes 1572872 | tf_op jit(solution)/shard_map/ppermute | solution.py:367
  45.5 16.4 %collective-permute-start.19 = (bf16[128,2048]{1,0:T(8,128)(2,1)}, bf16[128,2048]{1,0:T(8,128)(2,1)}, u32[]{:S(2)}, u32[]{:S(2)}) collective-permute-start(bf16[128,2048]{1,0:T(8,128)(2,1)} %add_convert_fusion.4), channel_id=1, source_target_pairs={{0,1},{1,0},{2,3},{3,2},{4,8},{5,9},{6,10},{7,11},{8,4},{9,5},{10,... | collective-permute-start | bytes 1572872 | tf_op jit(solution)/shard_map/ppermute | solution.py:370
  48.3 23.7 %collective-permute-start.10 = (bf16[128,2048]{1,0:T(8,128)(2,1)S(1)}, bf16[128,2048]{1,0:T(8,128)(2,1)}, u32[]{:S(2)}, u32[]{:S(2)}) collective-permute-start(bf16[128,2048]{1,0:T(8,128)(2,1)S(1)} %collective-permute-done.6.refs_1_), channel_id=1, source_target_pairs={{0,1},{1,0},{2,3},{3,2},{4,8},{5,9},{6,10},{7,11},{8,4},{9,5},{10,... | collective-permute-start | bytes 1572872 | tf_op jit(solution)/shard_map/ppermute | solution.py:370
  48.6 23.4 %collective-permute-start.11 = (bf16[128,2048]{1,0:T(8,128)(2,1)}, bf16[128,2048]{1,0:T(8,128)(2,1)S(1)}, u32[]{:S(2)}, u32[]{:S(2)}) collective-permute-start(bf16[128,2048]{1,0:T(8,128)(2,1)} %collective-permute-done.7.refs_2_), channel_id=1, source_target_pairs={{4,0},{8,12},{5,1},{9,13},{6,2},{10,14},{7,3},{11,15},{20,16},{24,... | collective-permute-start | bytes 1572872 | tf_op jit(solution)/shard_map/ppermute | solution.py:367
  52.7 24.7 %collective-permute-start.9 = (bf16[128,2048]{1,0:T(8,128)(2,1)}, bf16[128,2048]{1,0:T(8,128)(2,1)S(1)}, u32[]{:S(2)}, u32[]{:S(2)}) collective-permute-start(bf16[128,2048]{1,0:T(8,128)(2,1)} %collective-permute-done.5.refs_4_), channel_id=1, source_target_pairs={{4,0},{8,12},{5,1},{9,13},{6,2},{10,14},{7,3},{11,15},{20,16},{24,... | collective-permute-start | bytes 1572872 | tf_op jit(solution)/shard_map/ppermute | solution.py:367
  72.0 7.2 %collective-permute-start.20 = (bf16[64,2048]{1,0:T(8,128)(2,1)S(1)}, bf16[64,2048]{1,0:T(8,128)(2,1)S(1)}, u32[]{:S(2)}, u32[]{:S(2)}) collective-permute-start(bf16[64,2048]{1,0:T(8,128)(2,1)S(1)} %fusion.14), channel_id=1, source_target_pairs={{0,4},{4,0},{8,12},{12,8},{1,5},{5,1},{9,13},{13,9},{2,6},{6,2},{1... | collective-permute-start | bytes 786440 | tf_op jit(solution)/shard_map/ppermute | solution.py:367
  73.4 15.4 %collective-permute-start.12 = (bf16[128,2048]{1,0:T(8,128)(2,1)}, bf16[128,2048]{1,0:T(8,128)(2,1)}, u32[]{:S(2)}, u32[]{:S(2)}) collective-permute-start(bf16[128,2048]{1,0:T(8,128)(2,1)} %collective-permute-done.10.refs_4_), channel_id=1, source_target_pairs={{4,0},{8,12},{5,1},{9,13},{6,2},{10,14},{7,3},{11,15},{20,16},{24,... | collective-permute-start | bytes 1572872 | tf_op jit(solution)/shard_map/ppermute | solution.py:367
  77.4 35.5 %collective-permute-start.25 = (bf16[128,2048]{1,0:T(8,128)(2,1)}, bf16[128,2048]{1,0:T(8,128)(2,1)}, u32[]{:S(2)}, u32[]{:S(2)}) collective-permute-start(bf16[128,2048]{1,0:T(8,128)(2,1)} %get-tuple-element.68), channel_id=1, source_target_pairs={{0,1},{1,0},{2,3},{3,2},{4,8},{5,9},{6,10},{7,11},{8,4},{9,5},{10,... | collective-permute-start | bytes 1572872 | tf_op jit(solution)/shard_map/ppermute | solution.py:370
  80.4 11.0 %collective-permute-start.23 = (bf16[512,256]{1,0:T(8,128)(2,1)S(1)}, bf16[512,256]{1,0:T(8,128)(2,1)S(1)}, u32[]{:S(2)}, u32[]{:S(2)}) collective-permute-start(bf16[512,256]{1,0:T(8,128)(2,1)S(1)} %kv_total.1.refs_9_), channel_id=1, source_target_pairs={{0,3},{1,2},{2,1},{3,0},{4,7},{5,6},{6,5},{7,4},{8,11},{9,10},{10,... | collective-permute-start | bytes 786440 | tf_op jit(solution)/shard_map/ppermute | solution.py:520
  80.5 13.4 %collective-permute-start.22 = (bf16[512,256]{1,0:T(8,128)(2,1)S(1)}, bf16[512,256]{1,0:T(8,128)(2,1)S(1)}, u32[]{:S(2)}, u32[]{:S(2)}) collective-permute-start(bf16[512,256]{1,0:T(8,128)(2,1)S(1)} %kv_total.1.refs_9_), channel_id=1, source_target_pairs={{0,2},{1,3},{2,0},{3,1},{4,6},{5,7},{6,4},{7,5},{8,10},{9,11},{10,... | collective-permute-start | bytes 786440 | tf_op jit(solution)/shard_map/ppermute | solution.py:520
  81.6 14.5 %collective-permute-start.21 = (bf16[512,256]{1,0:T(8,128)(2,1)S(1)}, bf16[512,256]{1,0:T(8,128)(2,1)S(1)}, u32[]{:S(2)}, u32[]{:S(2)}) collective-permute-start(bf16[512,256]{1,0:T(8,128)(2,1)S(1)} %kv_total.1.refs_9_), channel_id=1, source_target_pairs={{0,1},{1,0},{2,3},{3,2},{4,5},{5,4},{6,7},{7,6},{8,9},{9,8},{10,11... | collective-permute-start | bytes 786440 | tf_op jit(solution)/shard_map/ppermute | solution.py:520
  88.9 45.5 %collective-permute-start.13 = (bf16[128,2048]{1,0:T(8,128)(2,1)}, bf16[128,2048]{1,0:T(8,128)(2,1)S(1)}, u32[]{:S(2)}, u32[]{:S(2)}) collective-permute-start(bf16[128,2048]{1,0:T(8,128)(2,1)} %get-tuple-element.59), channel_id=1, source_target_pairs={{0,4},{4,0},{8,12},{12,8},{1,5},{5,1},{9,13},{13,9},{2,6},{6,2},{1... | collective-permute-start | bytes 1572872 | tf_op jit(solution)/shard_map/ppermute | solution.py:367
  91.4 42.2 %collective-permute-start.14 = (bf16[128,2048]{1,0:T(8,128)(2,1)}, bf16[128,2048]{1,0:T(8,128)(2,1)S(1)}, u32[]{:S(2)}, u32[]{:S(2)}) collective-permute-start(bf16[128,2048]{1,0:T(8,128)(2,1)} %get-tuple-element.59), channel_id=1, source_target_pairs={{0,1},{1,0},{2,3},{3,2},{4,8},{5,9},{6,10},{7,11},{8,4},{9,5},{10,... | collective-permute-start | bytes 1572872 | tf_op jit(solution)/shard_map/ppermute | solution.py:370
  93.9 20.5 %collective-permute-start.24 = (bf16[128,2048]{1,0:T(8,128)(2,1)}, bf16[128,2048]{1,0:T(8,128)(2,1)S(1)}, u32[]{:S(2)}, u32[]{:S(2)}) collective-permute-start(bf16[128,2048]{1,0:T(8,128)(2,1)} %get-tuple-element.68), channel_id=1, source_target_pairs={{0,4},{4,0},{8,12},{12,8},{1,5},{5,1},{9,13},{13,9},{2,6},{6,2},{1... | collective-permute-start | bytes 1572872 | tf_op jit(solution)/shard_map/ppermute | solution.py:367
  114.4 20.9 %collective-permute-start.28 = (bf16[128,2048]{1,0:T(8,128)(2,1)S(1)}, bf16[128,2048]{1,0:T(8,128)(2,1)S(1)}, u32[]{:S(2)}, u32[]{:S(2)}) collective-permute-start(bf16[128,2048]{1,0:T(8,128)(2,1)S(1)} %bitcast_select_fusion.1), channel_id=1, source_target_pairs={{0,4},{4,0},{8,12},{12,8},{1,5},{5,1},{9,13},{13,9},{2,6},{6,2},{1... | collective-permute-start | bytes 1572872 | tf_op jit(solution)/shard_map/ppermute | solution.py:367
  131.8 14.9 %collective-permute-start.29 = (bf16[128,2048]{1,0:T(8,128)(2,1)S(1)}, bf16[128,2048]{1,0:T(8,128)(2,1)S(1)}, u32[]{:S(2)}, u32[]{:S(2)}) collective-permute-start(bf16[128,2048]{1,0:T(8,128)(2,1)S(1)} %collective-permute-done.24.refs_1_), channel_id=1, source_target_pairs={{0,1},{1,0},{2,3},{3,2},{4,8},{5,9},{6,10},{7,11},{8,4},{9,5},{10,... | collective-permute-start | bytes 1572872 | tf_op jit(solution)/shard_map/ppermute | solution.py:370
  134.4 14.2 %collective-permute-start.26 = (bf16[128,2048]{1,0:T(8,128)(2,1)S(1)}, bf16[128,2048]{1,0:T(8,128)(2,1)S(1)}, u32[]{:S(2)}, u32[]{:S(2)}) collective-permute-start(bf16[128,2048]{1,0:T(8,128)(2,1)S(1)} %bitcast_select_fusion.3), channel_id=1, source_target_pairs={{0,4},{4,0},{8,12},{12,8},{1,5},{5,1},{9,13},{13,9},{2,6},{6,2},{1... | collective-permute-start | bytes 1572872 | tf_op jit(solution)/shard_map/ppermute | solution.py:367
  134.4 23.6 %collective-permute-start.27 = (bf16[128,2048]{1,0:T(8,128)(2,1)S(1)}, bf16[128,2048]{1,0:T(8,128)(2,1)S(1)}, u32[]{:S(2)}, u32[]{:S(2)}) collective-permute-start(bf16[128,2048]{1,0:T(8,128)(2,1)S(1)} %collective-permute-done.13.refs_1_), channel_id=1, source_target_pairs={{0,1},{1,0},{2,3},{3,2},{4,8},{5,9},{6,10},{7,11},{8,4},{9,5},{10,... | collective-permute-start | bytes 1572872 | tf_op jit(solution)/shard_map/ppermute | solution.py:370
  146.8 22.4 %collective-permute-start.31 = (bf16[128,2048]{1,0:T(8,128)(2,1)S(1)}, bf16[128,2048]{1,0:T(8,128)(2,1)S(1)}, u32[]{:S(2)}, u32[]{:S(2)}) collective-permute-start(bf16[128,2048]{1,0:T(8,128)(2,1)S(1)} %fusion.7), channel_id=1, source_target_pairs={{0,1},{1,0},{2,3},{3,2},{4,8},{5,9},{6,10},{7,11},{8,4},{9,5},{10,... | collective-permute-start | bytes 1572872 | tf_op jit(solution)/shard_map/ppermute | solution.py:370
  148.6 20.8 %collective-permute-start.32 = (bf16[128,2048]{1,0:T(8,128)(2,1)S(1)}, bf16[128,2048]{1,0:T(8,128)(2,1)S(1)}, u32[]{:S(2)}, u32[]{:S(2)}) collective-permute-start(bf16[128,2048]{1,0:T(8,128)(2,1)S(1)} %bitcast_select_fusion), channel_id=1, source_target_pairs={{0,4},{4,0},{8,12},{12,8},{1,5},{5,1},{9,13},{13,9},{2,6},{6,2},{1... | collective-permute-start | bytes 1572872 | tf_op jit(solution)/shard_map/ppermute | solution.py:367
  158.0 13.4 %collective-permute-start.30 = (bf16[128,2048]{1,0:T(8,128)(2,1)S(1)}, bf16[128,2048]{1,0:T(8,128)(2,1)S(1)}, u32[]{:S(2)}, u32[]{:S(2)}) collective-permute-start(bf16[128,2048]{1,0:T(8,128)(2,1)S(1)} %bitcast_select_fusion.2), channel_id=1, source_target_pairs={{0,4},{4,0},{8,12},{12,8},{1,5},{5,1},{9,13},{13,9},{2,6},{6,2},{1... | collective-permute-start | bytes 1572872 | tf_op jit(solution)/shard_map/ppermute | solution.py:367
  158.1 22.3 %collective-permute-start.35 = (bf16[128,2048]{1,0:T(8,128)(2,1)S(1)}, bf16[128,2048]{1,0:T(8,128)(2,1)S(1)}, u32[]{:S(2)}, u32[]{:S(2)}) collective-permute-start(bf16[128,2048]{1,0:T(8,128)(2,1)S(1)} %fusion.9), channel_id=1, source_target_pairs={{0,1},{1,0},{2,3},{3,2},{4,8},{5,9},{6,10},{7,11},{8,4},{9,5},{10,... | collective-permute-start | bytes 1572872 | tf_op jit(solution)/shard_map/ppermute | solution.py:370
  169.5 32.0 %collective-permute-start.33 = (bf16[128,2048]{1,0:T(8,128)(2,1)S(1)}, bf16[128,2048]{1,0:T(8,128)(2,1)S(1)}, u32[]{:S(2)}, u32[]{:S(2)}) collective-permute-start(bf16[128,2048]{1,0:T(8,128)(2,1)S(1)} %fusion.10), channel_id=1, source_target_pairs={{0,4},{4,0},{8,12},{12,8},{1,5},{5,1},{9,13},{13,9},{2,6},{6,2},{1... | collective-permute-start | bytes 1572872 | tf_op jit(solution)/shard_map/ppermute | solution.py:367
  169.6 32.8 %collective-permute-start.34 = (bf16[128,2048]{1,0:T(8,128)(2,1)S(1)}, bf16[128,2048]{1,0:T(8,128)(2,1)S(1)}, u32[]{:S(2)}, u32[]{:S(2)}) collective-permute-start(bf16[128,2048]{1,0:T(8,128)(2,1)S(1)} %fusion.6), channel_id=1, source_target_pairs={{0,1},{1,0},{2,3},{3,2},{4,8},{5,9},{6,10},{7,11},{8,4},{9,5},{10,... | collective-permute-start | bytes 1572872 | tf_op jit(solution)/shard_map/ppermute | solution.py:370
  181.4 41.1 %collective-permute-start.36 = (bf16[128,2048]{1,0:T(8,128)(2,1)}, bf16[128,2048]{1,0:T(8,128)(2,1)S(1)}, u32[]{:S(2)}, u32[]{:S(2)}) collective-permute-start(bf16[128,2048]{1,0:T(8,128)(2,1)} %fusion.11), channel_id=1, source_target_pairs={{0,4},{4,0},{8,12},{12,8},{1,5},{5,1},{9,13},{13,9},{2,6},{6,2},{1... | collective-permute-start | bytes 1572872 | tf_op jit(solution)/shard_map/ppermute | solution.py:367
  181.4 41.1 %collective-permute-start.37 = (bf16[128,2048]{1,0:T(8,128)(2,1)}, bf16[128,2048]{1,0:T(8,128)(2,1)S(1)}, u32[]{:S(2)}, u32[]{:S(2)}) collective-permute-start(bf16[128,2048]{1,0:T(8,128)(2,1)} %fusion.5), channel_id=1, source_target_pairs={{0,1},{1,0},{2,3},{3,2},{4,8},{5,9},{6,10},{7,11},{8,4},{9,5},{10,... | collective-permute-start | bytes 1572872 | tf_op jit(solution)/shard_map/ppermute | solution.py:370
  203.2 21.1 %collective-permute-start.39 = (bf16[128,2048]{1,0:T(8,128)(2,1)}, bf16[128,2048]{1,0:T(8,128)(2,1)}, u32[]{:S(2)}, u32[]{:S(2)}) collective-permute-start(bf16[128,2048]{1,0:T(8,128)(2,1)} %get-tuple-element.82), channel_id=1, source_target_pairs={{0,4},{4,0},{8,12},{12,8},{1,5},{5,1},{9,13},{13,9},{2,6},{6,2},{1... | collective-permute-start | bytes 1572872 | tf_op jit(solution)/shard_map/ppermute | solution.py:367
  222.5 14.8 %collective-permute-start.38 = (bf16[128,2048]{1,0:T(8,128)(2,1)S(1)}, bf16[128,2048]{1,0:T(8,128)(2,1)S(1)}, u32[]{:S(2)}, u32[]{:S(2)}) collective-permute-start(bf16[128,2048]{1,0:T(8,128)(2,1)S(1)} %get-tuple-element.81), channel_id=1, source_target_pairs={{0,4},{4,0},{8,12},{12,8},{1,5},{5,1},{9,13},{13,9},{2,6},{6,2},{1... | collective-permute-start | bytes 1572872 | tf_op jit(solution)/shard_map/ppermute | solution.py:367
  225.4 23.1 %collective-permute-start.42 = (bf16[128,2048]{1,0:T(8,128)(2,1)S(1)}, bf16[128,2048]{1,0:T(8,128)(2,1)S(1)}, u32[]{:S(2)}, u32[]{:S(2)}) collective-permute-start(bf16[128,2048]{1,0:T(8,128)(2,1)S(1)} %copy-done.29), channel_id=1, source_target_pairs={{0,4},{4,0},{8,12},{12,8},{1,5},{5,1},{9,13},{13,9},{2,6},{6,2},{1... | collective-permute-start | bytes 1572872 | tf_op jit(solution)/shard_map/ppermute | solution.py:367
  226.9 21.8 %collective-permute-start.43 = (bf16[128,2048]{1,0:T(8,128)(2,1)S(1)}, bf16[128,2048]{1,0:T(8,128)(2,1)S(1)}, u32[]{:S(2)}, u32[]{:S(2)}) collective-permute-start(bf16[128,2048]{1,0:T(8,128)(2,1)S(1)} %fusion.3), channel_id=1, source_target_pairs={{0,1},{1,0},{2,3},{3,2},{4,8},{5,9},{6,10},{7,11},{8,4},{9,5},{10,... | collective-permute-start | bytes 1572872 | tf_op jit(solution)/shard_map/ppermute | solution.py:370
  237.4 13.1 %collective-permute-start.40 = (bf16[128,2048]{1,0:T(8,128)(2,1)S(1)}, bf16[128,2048]{1,0:T(8,128)(2,1)S(1)}, u32[]{:S(2)}, u32[]{:S(2)}) collective-permute-start(bf16[128,2048]{1,0:T(8,128)(2,1)S(1)} %fusion.8), channel_id=1, source_target_pairs={{0,1},{1,0},{2,3},{3,2},{4,8},{5,9},{6,10},{7,11},{8,4},{9,5},{10,... | collective-permute-start | bytes 1572872 | tf_op jit(solution)/shard_map/ppermute | solution.py:370
  239.2 19.8 %collective-permute-start.41 = (bf16[128,2048]{1,0:T(8,128)(2,1)S(1)}, bf16[128,2048]{1,0:T(8,128)(2,1)S(1)}, u32[]{:S(2)}, u32[]{:S(2)}) collective-permute-start(bf16[128,2048]{1,0:T(8,128)(2,1)S(1)} %get-tuple-element.84), channel_id=1, source_target_pairs={{0,4},{4,0},{8,12},{12,8},{1,5},{5,1},{9,13},{13,9},{2,6},{6,2},{1... | collective-permute-start | bytes 1572872 | tf_op jit(solution)/shard_map/ppermute | solution.py:367
  259.2 14.9 %collective-permute-start.46 = (bf16[128,2048]{1,0:T(8,128)(2,1)S(1)}, bf16[128,2048]{1,0:T(8,128)(2,1)S(1)}, u32[]{:S(2)}, u32[]{:S(2)}) collective-permute-start(bf16[128,2048]{1,0:T(8,128)(2,1)S(1)} %fusion.13), channel_id=1, source_target_pairs={{0,4},{4,0},{8,12},{12,8},{1,5},{5,1},{9,13},{13,9},{2,6},{6,2},{1... | collective-permute-start | bytes 1572872 | tf_op jit(solution)/shard_map/ppermute | solution.py:367
  259.5 14.9 %collective-permute-start.47 = (bf16[128,2048]{1,0:T(8,128)(2,1)S(1)}, bf16[128,2048]{1,0:T(8,128)(2,1)S(1)}, u32[]{:S(2)}, u32[]{:S(2)}) collective-permute-start(bf16[128,2048]{1,0:T(8,128)(2,1)S(1)} %fusion.2), channel_id=1, source_target_pairs={{0,1},{1,0},{2,3},{3,2},{4,8},{5,9},{6,10},{7,11},{8,4},{9,5},{10,... | collective-permute-start | bytes 1572872 | tf_op jit(solution)/shard_map/ppermute | solution.py:370
  261.3 22.4 %collective-permute-start.44 = (bf16[128,2048]{1,0:T(8,128)(2,1)S(1)}, bf16[128,2048]{1,0:T(8,128)(2,1)S(1)}, u32[]{:S(2)}, u32[]{:S(2)}) collective-permute-start(bf16[128,2048]{1,0:T(8,128)(2,1)S(1)} %fusion.12), channel_id=1, source_target_pairs={{0,4},{4,0},{8,12},{12,8},{1,5},{5,1},{9,13},{13,9},{2,6},{6,2},{1... | collective-permute-start | bytes 1572872 | tf_op jit(solution)/shard_map/ppermute | solution.py:367
  261.3 22.5 %collective-permute-start.45 = (bf16[128,2048]{1,0:T(8,128)(2,1)S(1)}, bf16[128,2048]{1,0:T(8,128)(2,1)S(1)}, u32[]{:S(2)}, u32[]{:S(2)}) collective-permute-start(bf16[128,2048]{1,0:T(8,128)(2,1)S(1)} %fusion.4), channel_id=1, source_target_pairs={{0,1},{1,0},{2,3},{3,2},{4,8},{5,9},{6,10},{7,11},{8,4},{9,5},{10,... | collective-permute-start | bytes 1572872 | tf_op jit(solution)/shard_map/ppermute | solution.py:370
  (31 other events, 414.8 us)

commit v2 on v1

--- a/solution.py
+++ b/solution.py
@@ -18,9 +18,9 @@
 norm_eps = 1e-05
 masked_score = -1e30
 log2_e = 1.4426950408889634
-VMEM_LIMIT = 46 * 1024 * 1024
+VMEM_LIMIT = 52 * 1024 * 1024
 GROUP = 2
-BLOCK = 1024
+BLOCK = 512
 VMEM = pl.BlockSpec(memory_space=pltpu.VMEM)
 SMEM = pl.BlockSpec(memory_space=pltpu.SMEM)
 ANY = pl.BlockSpec(memory_space=pl.ANY)
@@ -49,13 +49,18 @@
     pltpu.make_async_copy(target, target, sem).wait()
 
 
-def chunk_kernel(count, pieces_of, low, info_ref, *refs):
-    total_pieces = len(pieces_of) + 1
-    pieces = refs[:total_pieces]
-    w_query, w_out, table = refs[total_pieces : total_pieces + 3]
-    kv_pieces = refs[total_pieces + 3 : -13]
-    out, held, query_w, out_w, rows_table, kv, query, top, acc, flat, sems, q_sems, o_sems = refs[-13:]
+def chunk_kernel(count, pieces_of, low, info_ref, scaled, *refs):
+    streams = len(pieces_of)
+    kept = []
+    for of in pieces_of:
+        kept.append(refs[: len(of)])
+        refs = refs[len(of) :]
+    w_query, w_out, table = refs[:3]
+    outs, refs = refs[-12 - streams : -12], refs[3 : -12 - streams] + refs[-12:]
+    kv_pieces = refs[:-12]
+    held, query_w, out_w, rows_table, kv, query, top, acc, flat, sems, q_sems, o_sems = refs[-12:]
     rows = held.shape[0]
+    each = rows // streams
     width = held.shape[1] // count
     parts, depth, piece_columns = query_w.shape[0], query_w.shape[1], query_w.shape[2]
     heads = query.shape[0] // rows
@@ -64,17 +69,19 @@
     base = sp_rank * span
     even = rank % 2 == 0
 
-    def place(source, block):
+    def place(source, first_row, count_rows, block):
         columns = pl.ds(pl.multiple_of(block * width, width), width)
-        return pltpu.make_async_copy(source, held.at[:, columns], sems.at[0])
-
-    place(pieces[0].at[pl.ds(low, rows)], rank).start()
-    for piece, (kind, step) in zip(pieces[1:], pieces_of):
-        block = jnp.where(even == (kind == "outer"), rank + step, rank - step)
-
-        @pl.when((block >= 0) & (block < count))
-        def _():
-            place(piece, block).start()
+        target = held.at[first_row : first_row + count_rows, columns]
+        return pltpu.make_async_copy(source, target, sems.at[0])
+
+    place(scaled.at[pl.ds(low, rows)], 0, rows, rank).start()
+    for j in range(streams):
+        for piece, (kind, step) in zip(kept[j], pieces_of[j]):
+            block = jnp.where(even == (kind == "outer"), rank + step, rank - step)
+
+            @pl.when((block >= 0) & (block < count))
+            def _():
+                place(piece, j * each, each, block).start()
 
     def query_copy(k):
         return pltpu.make_async_copy(
@@ -170,27 +177,30 @@
     def _(b):
         for k in range(per_block):
             out_copy(b * per_block + k).wait()
-            out[b, :, k * out_columns : (k + 1) * out_columns] = jnp.dot(
-                flat[...], out_w[b * per_block + k], preferred_element_type=jnp.float32
-            ).astype(jnp.bfloat16)
-
-
-def chunk_terms(count, low, rows, scaled, arrived, info, w_query, w_out, table, kv_pieces):
+            mixed = jnp.dot(flat[...], out_w[b * per_block + k], preferred_element_type=jnp.float32)
+            for j in range(streams):
+                outs[j][b, :, k * out_columns : (k + 1) * out_columns] = mixed[
+                    j * each : (j + 1) * each
+                ].astype(jnp.bfloat16)
+
+
+def chunk_terms(count, low, each, scaled, arrived, info, w_query, w_out, table, kv_pieces):
+    rows = each * len(arrived)
     width = scaled.shape[1]
     model, columns = w_query.shape
     inner = w_out.shape[0]
     heads = columns // HD
     tokens = kv_pieces[0].shape[0] * len(kv_pieces)
-    pieces = [scaled] + [piece for _, _, piece in arrived]
-    pieces_of = [(kind, step) for kind, step, _ in arrived]
+    pieces = [scaled] + [piece for of in arrived for _, _, piece in of]
+    pieces_of = [[(kind, step) for kind, step, _ in of] for of in arrived]
     q_columns = min(columns, 256)
     o_columns = min(width, 1024)
     q_parts, o_parts = columns // q_columns, model // o_columns
     return pl.pallas_call(
         functools.partial(chunk_kernel, count, pieces_of, low),
-        out_shape=jax.ShapeDtypeStruct((count, rows, width), jnp.bfloat16),
+        out_shape=[jax.ShapeDtypeStruct((count, each, width), jnp.bfloat16)] * len(arrived),
         in_specs=[SMEM] + [ANY] * (len(pieces) + 3 + len(kv_pieces)),
-        out_specs=VMEM,
+        out_specs=[VMEM] * len(arrived),
         scratch_shapes=[
             pltpu.VMEM((rows, model), jnp.bfloat16),
             pltpu.VMEM((q_parts, model, q_columns), jnp.bfloat16),
@@ -474,8 +484,8 @@
                 axis=1,
             )
             infos = [
-                jnp.stack([rank, first[k * chunk] // BLOCK, sp_rank]).astype(jnp.int32)
-                for k in range(PERIODS * STREAMS)
+                jnp.stack([rank, first[k * STREAMS * chunk] // BLOCK, sp_rank]).astype(jnp.int32)
+                for k in range(PERIODS)
             ]
             return table, infos
 
@@ -524,11 +534,11 @@
                 if terms[j] is not None:
                     low = ((period - 1) * STREAMS + j) * chunk
                     out = finish(count, low, infos[0], hidden, terms[j], last[j], out)
-                if gather:
-                    k = period * STREAMS + j
-                    terms[j] = chunk_terms(
-                        count, k * chunk, chunk, scaled, arrived[j], infos[k], w_query, w_out, table, kv_pieces
-                    )
+            if gather:
+                low = period * STREAMS * chunk
+                terms = chunk_terms(
+                    count, low, chunk, scaled, arrived, infos[period], w_query, w_out, table, kv_pieces
+                )
         return out
 
     return body

time: 287 us -> 269 us (0.937)
  Pallas kernels: 77.4 us -> 64.9 us
  waiting for transfers between devices: 119 us -> 128 us
  other arithmetic: 15.1 us -> 9.57 us
  between operations: 10.3 us -> 5.91 us
  local copies, waits for them, and re-layouts: 8.7 us -> 4.5 us
    ppermute x22, waiting for transfers between devices: 58.7 us -> 95.1 us  [outer(): return lax.ppermute(value, 'tp', pairs)]
    ppermute x17, waiting for transfers between devices: 56.6 us -> 29 us  [inner(): return lax.ppermute(value, ('tp', 'sp'), self.inner_pairs)]
    ppermute x22, starting transfers between devices: 23.4 us -> 41 us  [outer(): return lax.ppermute(value, 'tp', pairs)]
    ppermute x17, starting transfers between devices: 25 us -> 7.78 us  [inner(): return lax.ppermute(value, ('tp', 'sp'), self.inner_pairs)]
    pallas_call x4 -> x2, Pallas kernels: 64.4 us -> 47.7 us  [chunk_terms(): pl.pallas_call(functools.partial(chunk_kernel, count, pieces_of, low), ou...]
    unnamed x62 -> x60, local copies, waits for them, and re-layouts: 5.29 us -> 0.81 us
    pallas_call x4, Pallas kernels: 7.27 us -> 11.5 us  [finish(): pl.pallas_call(functools.partial(finish_kernel, count, low, inner is not...]
  transfers between devices with their start and end apart: 48 -> 48, of which waited for: 20 -> 27; matrix products, arithmetic and copies ran while one was open for 5% -> 4% of each run, Pallas kernels for 26% -> 23%
where the time goes in v2:
time: 269 us; the launch traced here: 268 us
  waiting for transfers between devices  128 us (48%)
  Pallas kernels  64.9 us (24%)
  starting transfers between devices  55.7 us (21%)
  other arithmetic  9.57 us (4%)
  between operations  5.91 us (2%)
  local copies, waits for them, and re-layouts  4.5 us (2%)
    ppermute x22, waiting for transfers between devices, outer(): return lax.ppermute(value, 'tp', pairs)  95.1 us
    pallas_call x2, Pallas kernels, chunk_terms(): pl.pallas_call(functools.partial(chunk_kernel, count, pieces_of, low), ou...  47.7 us
    ppermute x22, starting transfers between devices, outer(): return lax.ppermute(value, 'tp', pairs)  41 us
    ppermute x17, waiting for transfers between devices, inner(): return lax.ppermute(value, ('tp', 'sp'), self.inner_pairs)  29 us
    pallas_call x4, Pallas kernels, finish(): pl.pallas_call(functools.partial(finish_kernel, count, low, inner is not...  11.5 us
    ppermute x17, starting transfers between devices, inner(): return lax.ppermute(value, ('tp', 'sp'), self.inner_pairs)  7.78 us
    pallas_call x1, Pallas kernels, kv_terms_of(): pl.pallas_call(functools.partial(kv_kernel, HQ // KV, slots), out_shape=s...  5.55 us
  transfers between devices with their start and end apart: 48, of which 27 were waited for; matrix products, arithmetic and copies ran while one was open for 4% of the time, Pallas kernels for 23%

profile of v2, /device:TPU:10, one launch (start us, length us, event | category | flops | bytes accessed | tf_op | source)
XLA Modules:
  0.0 268.3 jit_solution(10990548800764230258)
XLA Ops:
  0.7 2.3 fusion.1
  3.5 2.6 collective-permute-start.16
  6.5 1.4 fusion.16
  7.9 1.3 collective-permute-start.5
  9.2 2.7 %collective-permute-start.6 = (bf16[128,2048]{1,0:T(8,128)(2,1)}, bf16[128,2048]{1,0:T(8,128)(2,1)S(1)}, u32[]{:S(2)}, u32[]{:S(2)}) collective-permute-start(bf16[128,2048]{1,0:T(8,128)(2,1)} %get-tuple-element.55), channel_id=1, source_target_pairs={{0,1},{1,0},{2,3},{3,2},{4,8},{5,9},{6,10},{7,11},{8,4},{9,5},{10,... | collective-permute-start | bytes 1572872 | tf_op jit(solution)/shard_map/ppermute | solution.py:380
  12.1 5.5 %kv_terms.1 = (bf16[128,2048]{1,0:T(8,128)(2,1)S(1)}, bf16[128,2048]{1,0:T(8,128)(2,1)S(1)}, bf16[64,2048]{1,0:T(8,128)(2,1)S(1)}, bf16[64,2048]{1,0:T(8,128)(2,1)S(1)}) custom-call(s32[4]{0:T(128)S(1)} %pad_add_fusion.info_ref, bf16[512,2048]{1,0:T(8,128)(2,1)} %copy-done.2, bf16[2048,512]{1,0:T(8,128)(2,1)} %w_key.1, bf16[2048,512]{1,0:T(8,128)(2,1)} %w_value.1), custom_call_target="tpu_custom_call" | custom-call | bytes 2097152 | tf_op jit(solution)/shard_map/kv_terms/pallas_call | solution.py:257
  21.1 1.7 collective-permute-done.1
  23.2 2.7 collective-permute-start.4
  25.9 2.0 collective-permute-start.10
  28.8 5.5 %collective-permute-done.18 = bf16[128,2048]{1,0:T(8,128)(2,1)S(1)} collective-permute-done((bf16[128,2048]{1,0:T(8,128)(2,1)S(1)}, bf16[128,2048]{1,0:T(8,128)(2,1)S(1)}, u32[]{:S(2)}, u32[]{:S(2)}) %collective-permute-start.18) | collective-permute-done | bytes 524320 | tf_op jit(solution)/shard_map/ppermute | solution.py:377
  34.5 3.3 %collective-permute-done.3.refs_6_ = bf16[128,2048]{1,0:T(8,128)(2,1)S(1)} collective-permute-done((bf16[128,2048]{1,0:T(8,128)(2,1)}, bf16[128,2048]{1,0:T(8,128)(2,1)S(1)}, u32[]{:S(2)}, u32[]{:S(2)}) %collective-permute-start.3) | collective-permute-done | bytes 524320 | tf_op jit(solution)/shard_map/ppermute | solution.py:380
  37.8 5.6 %collective-permute-done.4.refs_5_ = bf16[128,2048]{1,0:T(8,128)(2,1)S(1)} collective-permute-done((bf16[128,2048]{1,0:T(8,128)(2,1)}, bf16[128,2048]{1,0:T(8,128)(2,1)S(1)}, u32[]{:S(2)}, u32[]{:S(2)}) %collective-permute-start.4) | collective-permute-done | bytes 524320 | tf_op jit(solution)/shard_map/ppermute | solution.py:377
  43.4 2.3 collective-permute-start.19
  49.6 4.4 %collective-permute-start.11 = (bf16[128,2048]{1,0:T(8,128)(2,1)S(1)}, bf16[128,2048]{1,0:T(8,128)(2,1)S(1)}, u32[]{:S(2)}, u32[]{:S(2)}) collective-permute-start(bf16[128,2048]{1,0:T(8,128)(2,1)S(1)} %collective-permute-done.9.refs_3_), channel_id=1, source_target_pairs={{4,0},{8,12},{5,1},{9,13},{6,2},{10,14},{7,3},{11,15},{20,16},{24,... | collective-permute-start | bytes 1572872 | tf_op jit(solution)/shard_map/ppermute | solution.py:377
  54.0 6.2 %collective-permute-done.19 = bf16[128,2048]{1,0:T(8,128)(2,1)S(1)} collective-permute-done((bf16[128,2048]{1,0:T(8,128)(2,1)S(1)}, bf16[128,2048]{1,0:T(8,128)(2,1)S(1)}, u32[]{:S(2)}, u32[]{:S(2)}) %collective-permute-start.19) | collective-permute-done | bytes 524320 | tf_op jit(solution)/shard_map/ppermute | solution.py:380
  60.8 9.3 %collective-permute-done.8.refs_8_ = bf16[128,2048]{1,0:T(8,128)(2,1)} collective-permute-done((bf16[128,2048]{1,0:T(8,128)(2,1)S(1)}, bf16[128,2048]{1,0:T(8,128)(2,1)}, u32[]{:S(2)}, u32[]{:S(2)}) %collective-permute-start.8) | collective-permute-done | bytes 524320 | tf_op jit(solution)/shard_map/ppermute | solution.py:380
  70.9 4.9 %collective-permute-start.14 = (bf16[128,2048]{1,0:T(8,128)(2,1)}, bf16[128,2048]{1,0:T(8,128)(2,1)}, u32[]{:S(2)}, u32[]{:S(2)}) collective-permute-start(bf16[128,2048]{1,0:T(8,128)(2,1)} %collective-permute-done.8.refs_8_), channel_id=1, source_target_pairs={{4,0},{8,12},{5,1},{9,13},{6,2},{10,14},{7,3},{11,15},{20,16},{24,... | collective-permute-start | bytes 1572872 | tf_op jit(solution)/shard_map/ppermute | solution.py:377
  76.0 1.6 collective-permute-done.20
  85.6 2.7 %collective-permute-done.14.refs_9_ = bf16[128,2048]{1,0:T(8,128)(2,1)} collective-permute-done((bf16[128,2048]{1,0:T(8,128)(2,1)}, bf16[128,2048]{1,0:T(8,128)(2,1)}, u32[]{:S(2)}, u32[]{:S(2)}) %collective-permute-start.14) | collective-permute-done | bytes 524320 | tf_op jit(solution)/shard_map/ppermute | solution.py:377
  88.3 2.5 collective-permute-start.12
  92.7 24.0 %chunk_terms.2 = (bf16[4,128,2048]{2,1,0:T(8,128)(2,1)}, bf16[4,128,2048]{2,1,0:T(8,128)(2,1)}) custom-call(s32[3]{0:T(128)S(1)} %add_add_fusion.1.info_ref, bf16[512,2048]{1,0:T(8,128)(2,1)} %copy-done.2, bf16[128,2048]{1,0:T(8,128)(2,1)} %copy-done.18, bf16[128,2048]{1,0:T(8,128)(2,1)} %copy-done.19, bf16[128,2048]{1,0:T(8,128)(2,1)} %copy-done.22, ...), custom_call_target="tpu_custom_call" | custom-call | flops 2147483648 | tf_op jit(solution)/shard_map/chunk_terms/pallas_call | solution.py:199
  118.0 2.5 collective-permute-start.24
  122.0 2.6 collective-permute-start.29
  124.6 6.7 %collective-permute-done.24.refs_2_ = bf16[128,2048]{1,0:T(8,128)(2,1)S(1)} collective-permute-done((bf16[128,2048]{1,0:T(8,128)(2,1)S(1)}, bf16[128,2048]{1,0:T(8,128)(2,1)S(1)}, u32[]{:S(2)}, u32[]{:S(2)}) %collective-permute-start.24) | collective-permute-done | bytes 524320 | tf_op jit(solution)/shard_map/ppermute | solution.py:377
  131.5 2.5 collective-permute-done.25.refs_3_
  134.2 8.3 %collective-permute-done.29.refs_7_ = bf16[128,2048]{1,0:T(8,128)(2,1)S(1)} collective-permute-done((bf16[128,2048]{1,0:T(8,128)(2,1)S(1)}, bf16[128,2048]{1,0:T(8,128)(2,1)S(1)}, u32[]{:S(2)}, u32[]{:S(2)}) %collective-permute-start.29) | collective-permute-done | bytes 524320 | tf_op jit(solution)/shard_map/ppermute | solution.py:377
  142.7 2.5 collective-permute-done.30.refs_8_
  145.5 8.3 %collective-permute-done.28.refs_4_ = bf16[128,2048]{1,0:T(8,128)(2,1)S(1)} collective-permute-done((bf16[128,2048]{1,0:T(8,128)(2,1)S(1)}, bf16[128,2048]{1,0:T(8,128)(2,1)S(1)}, u32[]{:S(2)}, u32[]{:S(2)}) %collective-permute-start.28) | collective-permute-done | bytes 524320 | tf_op jit(solution)/shard_map/ppermute | solution.py:377
  153.9 2.5 collective-permute-done.32
  156.8 8.2 %collective-permute-done.31.refs_9_ = bf16[128,2048]{1,0:T(8,128)(2,1)S(1)} collective-permute-done((bf16[128,2048]{1,0:T(8,128)(2,1)S(1)}, bf16[128,2048]{1,0:T(8,128)(2,1)S(1)}, u32[]{:S(2)}, u32[]{:S(2)}) %collective-permute-start.31) | collective-permute-done | bytes 524320 | tf_op jit(solution)/shard_map/ppermute | solution.py:377
  165.2 2.5 collective-permute-done.35
  168.0 23.8 %chunk_terms.3 = (bf16[4,128,2048]{2,1,0:T(8,128)(2,1)}, bf16[4,128,2048]{2,1,0:T(8,128)(2,1)}) custom-call(s32[3]{0:T(128)S(1)} %add_add_fusion.2.info_ref, bf16[512,2048]{1,0:T(8,128)(2,1)} %copy-done.2, bf16[128,2048]{1,0:T(8,128)(2,1)} %copy-done.26, bf16[128,2048]{1,0:T(8,128)(2,1)} %copy-done.11, bf16[128,2048]{1,0:T(8,128)(2,1)} %copy-done.7, ...), custom_call_target="tpu_custom_call" | custom-call | flops 2147483648 | tf_op jit(solution)/shard_map/chunk_terms/pallas_call | solution.py:199
  191.8 1.4 dynamic-slice_bitcast_fusion
  193.3 4.5 %collective-permute-start.39 = (bf16[128,2048]{1,0:T(8,128)(2,1)S(1)}, bf16[128,2048]{1,0:T(8,128)(2,1)S(1)}, u32[]{:S(2)}, u32[]{:S(2)}) collective-permute-start(bf16[128,2048]{1,0:T(8,128)(2,1)S(1)} %get-tuple-element.90), channel_id=1, source_target_pairs={{0,4},{4,0},{8,12},{12,8},{1,5},{5,1},{9,13},{13,9},{2,6},{6,2},{1... | collective-permute-start | bytes 1572872 | tf_op jit(solution)/shard_map/ppermute | solution.py:377
  198.4 10.7 %collective-permute-done.39 = bf16[128,2048]{1,0:T(8,128)(2,1)S(1)} collective-permute-done((bf16[128,2048]{1,0:T(8,128)(2,1)S(1)}, bf16[128,2048]{1,0:T(8,128)(2,1)S(1)}, u32[]{:S(2)}, u32[]{:S(2)}) %collective-permute-start.39) | collective-permute-done | bytes 524320 | tf_op jit(solution)/shard_map/ppermute | solution.py:377
  209.2 2.5 collective-permute-start.42
  212.0 8.4 %collective-permute-done.38 = bf16[128,2048]{1,0:T(8,128)(2,1)S(1)} collective-permute-done((bf16[128,2048]{1,0:T(8,128)(2,1)S(1)}, bf16[128,2048]{1,0:T(8,128)(2,1)S(1)}, u32[]{:S(2)}, u32[]{:S(2)}) %collective-permute-start.38) | collective-permute-done | bytes 524320 | tf_op jit(solution)/shard_map/ppermute | solution.py:377
  220.5 2.5 collective-permute-start.41
  223.2 8.4 %collective-permute-done.42 = bf16[128,2048]{1,0:T(8,128)(2,1)S(1)} collective-permute-done((bf16[128,2048]{1,0:T(8,128)(2,1)S(1)}, bf16[128,2048]{1,0:T(8,128)(2,1)S(1)}, u32[]{:S(2)}, u32[]{:S(2)}) %collective-permute-start.42) | collective-permute-done | bytes 524320 | tf_op jit(solution)/shard_map/ppermute | solution.py:377
  231.9 2.5 collective-permute-start.46
  234.6 8.2 %collective-permute-done.41 = bf16[128,2048]{1,0:T(8,128)(2,1)S(1)} collective-permute-done((bf16[128,2048]{1,0:T(8,128)(2,1)S(1)}, bf16[128,2048]{1,0:T(8,128)(2,1)S(1)}, u32[]{:S(2)}, u32[]{:S(2)}) %collective-permute-start.41) | collective-permute-done | bytes 524320 | tf_op jit(solution)/shard_map/ppermute | solution.py:377
  243.1 2.5 collective-permute-start.44
  245.9 2.9 %finish.4.refs_0_ = bf16[512,2048]{1,0:T(8,128)(2,1)} custom-call(s32[3]{0:T(128)S(1)} %add_add_fusion.1.info_ref, bf16[512,2048]{1,0:T(8,128)(2,1)} %hidden.7, bf16[4,128,2048]{2,1,0:T(8,128)(2,1)} %get-tuple-element.71.terms, bf16[128,2048]{1,0:T(8,128)(2,1)S(1)} %collective-permute-done.33.outer, bf16[128,2048]{1,0:T(8,128)(2,1)S(1)} %collective-permute-done.34.inner), custom_call_target="tpu_custom_call" | custom-call | bytes 1572864 | tf_op jit(solution)/shard_map/finish/pallas_call | solution.py:330
  248.7 2.9 %finish.5.refs_0_ = bf16[512,2048]{1,0:T(8,128)(2,1)} custom-call(s32[3]{0:T(128)S(1)} %add_add_fusion.1.info_ref, bf16[512,2048]{1,0:T(8,128)(2,1)} %hidden.7, bf16[4,128,2048]{2,1,0:T(8,128)(2,1)} %get-tuple-element.77.terms, bf16[128,2048]{1,0:T(8,128)(2,1)S(1)} %collective-permute-done.36.outer, ...), custom_call_target="tpu_custom_call", output_to_operand_aliasing={{}: (5, {})} | custom-call | bytes 1572864 | tf_op jit(solution)/shard_map/finish/pallas_call | solution.py:330
  251.6 2.4 collective-permute-done.46.outer
  254.0 2.9 %finish.6.refs_0_ = bf16[512,2048]{1,0:T(8,128)(2,1)} custom-call(s32[3]{0:T(128)S(1)} %add_add_fusion.1.info_ref, bf16[512,2048]{1,0:T(8,128)(2,1)} %hidden.7, bf16[4,128,2048]{2,1,0:T(8,128)(2,1)} %get-tuple-element.89.terms, bf16[128,2048]{1,0:T(8,128)(2,1)S(1)} %collective-permute-done.46.outer, ...), custom_call_target="tpu_custom_call", output_to_operand_aliasing={{}: (5, {})} | custom-call | bytes 1572864 | tf_op jit(solution)/shard_map/finish/pallas_call | solution.py:330
  256.9 8.4 %collective-permute-done.44.outer = bf16[128,2048]{1,0:T(8,128)(2,1)S(1)} collective-permute-done((bf16[128,2048]{1,0:T(8,128)(2,1)S(1)}, bf16[128,2048]{1,0:T(8,128)(2,1)S(1)}, u32[]{:S(2)}, u32[]{:S(2)}) %collective-permute-start.44) | collective-permute-done | bytes 524320 | tf_op jit(solution)/shard_map/ppermute | solution.py:377
  265.3 2.9 %finish.7 = bf16[512,2048]{1,0:T(8,128)(2,1)} custom-call(s32[3]{0:T(128)S(1)} %add_add_fusion.1.info_ref, bf16[512,2048]{1,0:T(8,128)(2,1)} %hidden.7, bf16[4,128,2048]{2,1,0:T(8,128)(2,1)} %get-tuple-element.81.terms, bf16[128,2048]{1,0:T(8,128)(2,1)S(1)} %collective-permute-done.44.outer, ...), custom_call_target="tpu_custom_call", output_to_operand_aliasing={{}: (5, {})} | custom-call | bytes 1572864 | tf_op jit(solution)/shard_map/finish/pallas_call | solution.py:330
  (155 shorter events, 23.3 us)
Async XLA Ops:
  3.0 9.0 %collective-permute-start.15 = (f32[512]{0:T(512)S(1)}, f32[512]{0:T(512)S(1)}, u32[]{:S(2)}, u32[]{:S(2)}) collective-permute-start(f32[512]{0:T(512)S(1)} %get-tuple-element.109), channel_id=1, source_target_pairs={{0,4},{4,0},{8,12},{12,8},{1,5},{5,1},{9,13},{13,9},{2,6},{6,2},{1... | collective-permute-start | bytes 6152 | tf_op jit(solution)/shard_map/ppermute | solution.py:348
  3.5 8.5 %collective-permute-start.16 = (f32[512]{0:T(512)S(1)}, f32[512]{0:T(512)S(1)}, u32[]{:S(2)}, u32[]{:S(2)}) collective-permute-start(f32[512]{0:T(512)S(1)} %get-tuple-element.109), channel_id=1, source_target_pairs={{0,8},{4,12},{8,0},{12,4},{1,9},{5,13},{9,1},{13,5},{2,10},{6,14},... | collective-permute-start | bytes 6152 | tf_op jit(solution)/shard_map/ppermute | solution.py:348
  6.1 5.9 %collective-permute-start.17 = (f32[512]{0:T(512)S(1)}, f32[512]{0:T(512)S(1)}, u32[]{:S(2)}, u32[]{:S(2)}) collective-permute-start(f32[512]{0:T(512)S(1)} %get-tuple-element.109), channel_id=1, source_target_pairs={{0,12},{4,8},{8,4},{12,0},{1,13},{5,9},{9,5},{13,1},{2,14},{6,10},... | collective-permute-start | bytes 6152 | tf_op jit(solution)/shard_map/ppermute | solution.py:348
  7.9 18.0 %collective-permute-start.5 = (bf16[128,2048]{1,0:T(8,128)(2,1)}, bf16[128,2048]{1,0:T(8,128)(2,1)S(1)}, u32[]{:S(2)}, u32[]{:S(2)}) collective-permute-start(bf16[128,2048]{1,0:T(8,128)(2,1)} %get-tuple-element.55), channel_id=1, source_target_pairs={{0,4},{4,0},{8,12},{12,8},{1,5},{5,1},{9,13},{13,9},{2,6},{6,2},{1... | collective-permute-start | bytes 1572872 | tf_op jit(solution)/shard_map/ppermute | solution.py:377
  9.2 16.6 %collective-permute-start.6 = (bf16[128,2048]{1,0:T(8,128)(2,1)}, bf16[128,2048]{1,0:T(8,128)(2,1)S(1)}, u32[]{:S(2)}, u32[]{:S(2)}) collective-permute-start(bf16[128,2048]{1,0:T(8,128)(2,1)} %get-tuple-element.55), channel_id=1, source_target_pairs={{0,1},{1,0},{2,3},{3,2},{4,8},{5,9},{6,10},{7,11},{8,4},{9,5},{10,... | collective-permute-start | bytes 1572872 | tf_op jit(solution)/shard_map/ppermute | solution.py:380
  17.6 16.8 %collective-permute-start.18 = (bf16[128,2048]{1,0:T(8,128)(2,1)S(1)}, bf16[128,2048]{1,0:T(8,128)(2,1)S(1)}, u32[]{:S(2)}, u32[]{:S(2)}) collective-permute-start(bf16[128,2048]{1,0:T(8,128)(2,1)S(1)} %get-tuple-element.68), channel_id=1, source_target_pairs={{0,4},{12,8},{1,5},{13,9},{2,6},{14,10},{3,7},{15,11},{16,20},{28,... | collective-permute-start | bytes 1572872 | tf_op jit(solution)/shard_map/ppermute | solution.py:377
  19.0 1.2 collective-permute-start
  19.1 3.6 %collective-permute-start.1 = (s32[4]{0:T(128)S(1)}, s32[4]{0:T(128)S(1)}, u32[]{:S(2)}, u32[]{:S(2)}) collective-permute-start(s32[4]{0:T(128)S(1)} %convert_reduce_fusion), channel_id=1, source_target_pairs={{0,2},{1,3},{2,0},{3,1},{4,6},{5,7},{6,4},{7,5},{8,10},{9,11},{10,... | collective-permute-start | bytes 56 | tf_op jit(solution)/shard_map/ppermute | solution.py:348
  20.2 3.0 %collective-permute-start.2 = (s32[4]{0:T(128)S(1)}, s32[4]{0:T(128)S(1)}, u32[]{:S(2)}, u32[]{:S(2)}) collective-permute-start(s32[4]{0:T(128)S(1)} %convert_reduce_fusion), channel_id=1, source_target_pairs={{0,3},{1,2},{2,1},{3,0},{4,7},{5,6},{6,5},{7,4},{8,11},{9,10},{10,... | collective-permute-start | bytes 56 | tf_op jit(solution)/shard_map/ppermute | solution.py:348
  22.7 15.1 %collective-permute-start.3 = (bf16[128,2048]{1,0:T(8,128)(2,1)}, bf16[128,2048]{1,0:T(8,128)(2,1)S(1)}, u32[]{:S(2)}, u32[]{:S(2)}) collective-permute-start(bf16[128,2048]{1,0:T(8,128)(2,1)} %get-tuple-element.53), channel_id=1, source_target_pairs={{0,1},{1,0},{2,3},{3,2},{4,8},{5,9},{6,10},{7,11},{8,4},{9,5},{10,... | collective-permute-start | bytes 1572872 | tf_op jit(solution)/shard_map/ppermute | solution.py:380
  23.2 20.2 %collective-permute-start.4 = (bf16[128,2048]{1,0:T(8,128)(2,1)}, bf16[128,2048]{1,0:T(8,128)(2,1)S(1)}, u32[]{:S(2)}, u32[]{:S(2)}) collective-permute-start(bf16[128,2048]{1,0:T(8,128)(2,1)} %get-tuple-element.53), channel_id=1, source_target_pairs={{0,4},{4,0},{8,12},{12,8},{1,5},{5,1},{9,13},{13,9},{2,6},{6,2},{1... | collective-permute-start | bytes 1572872 | tf_op jit(solution)/shard_map/ppermute | solution.py:377
  25.9 23.7 %collective-permute-start.10 = (bf16[128,2048]{1,0:T(8,128)(2,1)S(1)}, bf16[128,2048]{1,0:T(8,128)(2,1)S(1)}, u32[]{:S(2)}, u32[]{:S(2)}) collective-permute-start(bf16[128,2048]{1,0:T(8,128)(2,1)S(1)} %collective-permute-done.6.refs_1_), channel_id=1, source_target_pairs={{4,0},{8,12},{5,1},{9,13},{6,2},{10,14},{7,3},{11,15},{20,16},{24,... | collective-permute-start | bytes 1572872 | tf_op jit(solution)/shard_map/ppermute | solution.py:377
  27.9 21.7 %collective-permute-start.9 = (bf16[128,2048]{1,0:T(8,128)(2,1)S(1)}, bf16[128,2048]{1,0:T(8,128)(2,1)S(1)}, u32[]{:S(2)}, u32[]{:S(2)}) collective-permute-start(bf16[128,2048]{1,0:T(8,128)(2,1)S(1)} %collective-permute-done.5.refs_0_), channel_id=1, source_target_pairs={{0,1},{1,0},{2,3},{3,2},{4,8},{5,9},{6,10},{7,11},{8,4},{9,5},{10,... | collective-permute-start | bytes 1572872 | tf_op jit(solution)/shard_map/ppermute | solution.py:380
  43.4 16.9 %collective-permute-start.19 = (bf16[128,2048]{1,0:T(8,128)(2,1)S(1)}, bf16[128,2048]{1,0:T(8,128)(2,1)S(1)}, u32[]{:S(2)}, u32[]{:S(2)}) collective-permute-start(bf16[128,2048]{1,0:T(8,128)(2,1)S(1)} %add_convert_fusion.4), channel_id=1, source_target_pairs={{0,1},{1,0},{2,3},{3,2},{4,8},{5,9},{6,10},{7,11},{8,4},{9,5},{10,... | collective-permute-start | bytes 1572872 | tf_op jit(solution)/shard_map/ppermute | solution.py:380
  45.8 15.0 %collective-permute-start.7 = (bf16[128,2048]{1,0:T(8,128)(2,1)S(1)}, bf16[128,2048]{1,0:T(8,128)(2,1)S(1)}, u32[]{:S(2)}, u32[]{:S(2)}) collective-permute-start(bf16[128,2048]{1,0:T(8,128)(2,1)S(1)} %collective-permute-done.3.refs_6_), channel_id=1, source_target_pairs={{4,0},{8,12},{5,1},{9,13},{6,2},{10,14},{7,3},{11,15},{20,16},{24,... | collective-permute-start | bytes 1572872 | tf_op jit(solution)/shard_map/ppermute | solution.py:377
  47.1 23.0 %collective-permute-start.8 = (bf16[128,2048]{1,0:T(8,128)(2,1)S(1)}, bf16[128,2048]{1,0:T(8,128)(2,1)}, u32[]{:S(2)}, u32[]{:S(2)}) collective-permute-start(bf16[128,2048]{1,0:T(8,128)(2,1)S(1)} %collective-permute-done.4.refs_5_), channel_id=1, source_target_pairs={{0,1},{1,0},{2,3},{3,2},{4,8},{5,9},{6,10},{7,11},{8,4},{9,5},{10,... | collective-permute-start | bytes 1572872 | tf_op jit(solution)/shard_map/ppermute | solution.py:380
  49.6 26.1 %collective-permute-start.11 = (bf16[128,2048]{1,0:T(8,128)(2,1)S(1)}, bf16[128,2048]{1,0:T(8,128)(2,1)S(1)}, u32[]{:S(2)}, u32[]{:S(2)}) collective-permute-start(bf16[128,2048]{1,0:T(8,128)(2,1)S(1)} %collective-permute-done.9.refs_3_), channel_id=1, source_target_pairs={{4,0},{8,12},{5,1},{9,13},{6,2},{10,14},{7,3},{11,15},{20,16},{24,... | collective-permute-start | bytes 1572872 | tf_op jit(solution)/shard_map/ppermute | solution.py:377
  70.2 7.5 %collective-permute-start.20 = (bf16[64,2048]{1,0:T(8,128)(2,1)S(1)}, bf16[64,2048]{1,0:T(8,128)(2,1)S(1)}, u32[]{:S(2)}, u32[]{:S(2)}) collective-permute-start(bf16[64,2048]{1,0:T(8,128)(2,1)S(1)} %fusion.14), channel_id=1, source_target_pairs={{0,4},{4,0},{8,12},{12,8},{1,5},{5,1},{9,13},{13,9},{2,6},{6,2},{1... | collective-permute-start | bytes 786440 | tf_op jit(solution)/shard_map/ppermute | solution.py:377
  70.9 17.4 %collective-permute-start.14 = (bf16[128,2048]{1,0:T(8,128)(2,1)}, bf16[128,2048]{1,0:T(8,128)(2,1)}, u32[]{:S(2)}, u32[]{:S(2)}) collective-permute-start(bf16[128,2048]{1,0:T(8,128)(2,1)} %collective-permute-done.8.refs_8_), channel_id=1, source_target_pairs={{4,0},{8,12},{5,1},{9,13},{6,2},{10,14},{7,3},{11,15},{20,16},{24,... | collective-permute-start | bytes 1572872 | tf_op jit(solution)/shard_map/ppermute | solution.py:377
  75.7 40.9 %collective-permute-start.13 = (bf16[128,2048]{1,0:T(8,128)(2,1)}, bf16[128,2048]{1,0:T(8,128)(2,1)S(1)}, u32[]{:S(2)}, u32[]{:S(2)}) collective-permute-start(bf16[128,2048]{1,0:T(8,128)(2,1)} %get-tuple-element.62), channel_id=1, source_target_pairs={{0,1},{1,0},{2,3},{3,2},{4,8},{5,9},{6,10},{7,11},{8,4},{9,5},{10,... | collective-permute-start | bytes 1572872 | tf_op jit(solution)/shard_map/ppermute | solution.py:380
  78.0 12.8 %collective-permute-start.21 = (bf16[512,256]{1,0:T(8,128)(2,1)S(1)}, bf16[512,256]{1,0:T(8,128)(2,1)S(1)}, u32[]{:S(2)}, u32[]{:S(2)}) collective-permute-start(bf16[512,256]{1,0:T(8,128)(2,1)S(1)} %kv_total.1.refs_13_), channel_id=1, source_target_pairs={{0,1},{1,0},{2,3},{3,2},{4,5},{5,4},{6,7},{7,6},{8,9},{9,8},{10,11... | collective-permute-start | bytes 786440 | tf_op jit(solution)/shard_map/ppermute | solution.py:530
  78.0 12.8 %collective-permute-start.22 = (bf16[512,256]{1,0:T(8,128)(2,1)S(1)}, bf16[512,256]{1,0:T(8,128)(2,1)S(1)}, u32[]{:S(2)}, u32[]{:S(2)}) collective-permute-start(bf16[512,256]{1,0:T(8,128)(2,1)S(1)} %kv_total.1.refs_13_), channel_id=1, source_target_pairs={{0,2},{1,3},{2,0},{3,1},{4,6},{5,7},{6,4},{7,5},{8,10},{9,11},{10,... | collective-permute-start | bytes 786440 | tf_op jit(solution)/shard_map/ppermute | solution.py:530
  79.2 12.8 %collective-permute-start.23 = (bf16[512,256]{1,0:T(8,128)(2,1)S(1)}, bf16[512,256]{1,0:T(8,128)(2,1)S(1)}, u32[]{:S(2)}, u32[]{:S(2)}) collective-permute-start(bf16[512,256]{1,0:T(8,128)(2,1)S(1)} %kv_total.1.refs_13_), channel_id=1, source_target_pairs={{0,3},{1,2},{2,1},{3,0},{4,7},{5,6},{6,5},{7,4},{8,11},{9,10},{10,... | collective-permute-start | bytes 786440 | tf_op jit(solution)/shard_map/ppermute | solution.py:530
  88.3 29.7 %collective-permute-start.12 = (bf16[128,2048]{1,0:T(8,128)(2,1)}, bf16[128,2048]{1,0:T(8,128)(2,1)S(1)}, u32[]{:S(2)}, u32[]{:S(2)}) collective-permute-start(bf16[128,2048]{1,0:T(8,128)(2,1)} %get-tuple-element.62), channel_id=1, source_target_pairs={{0,4},{4,0},{8,12},{12,8},{1,5},{5,1},{9,13},{13,9},{2,6},{6,2},{1... | collective-permute-start | bytes 1572872 | tf_op jit(solution)/shard_map/ppermute | solution.py:377
  90.8 31.2 %collective-permute-start.26 = (bf16[128,2048]{1,0:T(8,128)(2,1)S(1)}, bf16[128,2048]{1,0:T(8,128)(2,1)S(1)}, u32[]{:S(2)}, u32[]{:S(2)}) collective-permute-start(bf16[128,2048]{1,0:T(8,128)(2,1)S(1)} %copy-done.28), channel_id=1, source_target_pairs={{0,4},{4,0},{8,12},{12,8},{1,5},{5,1},{9,13},{13,9},{2,6},{6,2},{1... | collective-permute-start | bytes 1572872 | tf_op jit(solution)/shard_map/ppermute | solution.py:377
  90.9 29.7 %collective-permute-start.27 = (bf16[128,2048]{1,0:T(8,128)(2,1)S(1)}, bf16[128,2048]{1,0:T(8,128)(2,1)S(1)}, u32[]{:S(2)}, u32[]{:S(2)}) collective-permute-start(bf16[128,2048]{1,0:T(8,128)(2,1)S(1)} %copy-done.28), channel_id=1, source_target_pairs={{0,1},{1,0},{2,3},{3,2},{4,8},{5,9},{6,10},{7,11},{8,4},{9,5},{10,... | collective-permute-start | bytes 1572872 | tf_op jit(solution)/shard_map/ppermute | solution.py:380
  118.0 13.3 %collective-permute-start.24 = (bf16[128,2048]{1,0:T(8,128)(2,1)S(1)}, bf16[128,2048]{1,0:T(8,128)(2,1)S(1)}, u32[]{:S(2)}, u32[]{:S(2)}) collective-permute-start(bf16[128,2048]{1,0:T(8,128)(2,1)S(1)} %bitcast_select_fusion.3), channel_id=1, source_target_pairs={{0,4},{4,0},{8,12},{12,8},{1,5},{5,1},{9,13},{13,9},{2,6},{6,2},{1... | collective-permute-start | bytes 1572872 | tf_op jit(solution)/shard_map/ppermute | solution.py:377
  120.6 13.4 %collective-permute-start.25 = (bf16[128,2048]{1,0:T(8,128)(2,1)S(1)}, bf16[128,2048]{1,0:T(8,128)(2,1)S(1)}, u32[]{:S(2)}, u32[]{:S(2)}) collective-permute-start(bf16[128,2048]{1,0:T(8,128)(2,1)S(1)} %collective-permute-done.12.refs_0_), channel_id=1, source_target_pairs={{0,1},{1,0},{2,3},{3,2},{4,8},{5,9},{6,10},{7,11},{8,4},{9,5},{10,... | collective-permute-start | bytes 1572872 | tf_op jit(solution)/shard_map/ppermute | solution.py:380
  122.0 20.6 %collective-permute-start.29 = (bf16[128,2048]{1,0:T(8,128)(2,1)S(1)}, bf16[128,2048]{1,0:T(8,128)(2,1)S(1)}, u32[]{:S(2)}, u32[]{:S(2)}) collective-permute-start(bf16[128,2048]{1,0:T(8,128)(2,1)S(1)} %bitcast_select_fusion.1), channel_id=1, source_target_pairs={{0,4},{4,0},{8,12},{12,8},{1,5},{5,1},{9,13},{13,9},{2,6},{6,2},{1... | collective-permute-start | bytes 1572872 | tf_op jit(solution)/shard_map/ppermute | solution.py:377
  124.6 20.6 %collective-permute-start.30 = (bf16[128,2048]{1,0:T(8,128)(2,1)S(1)}, bf16[128,2048]{1,0:T(8,128)(2,1)S(1)}, u32[]{:S(2)}, u32[]{:S(2)}) collective-permute-start(bf16[128,2048]{1,0:T(8,128)(2,1)S(1)} %collective-permute-done.26.refs_5_), channel_id=1, source_target_pairs={{0,1},{1,0},{2,3},{3,2},{4,8},{5,9},{6,10},{7,11},{8,4},{9,5},{10,... | collective-permute-start | bytes 1572872 | tf_op jit(solution)/shard_map/ppermute | solution.py:380
  134.1 19.7 %collective-permute-start.28 = (bf16[128,2048]{1,0:T(8,128)(2,1)S(1)}, bf16[128,2048]{1,0:T(8,128)(2,1)S(1)}, u32[]{:S(2)}, u32[]{:S(2)}) collective-permute-start(bf16[128,2048]{1,0:T(8,128)(2,1)S(1)} %bitcast_select_fusion.2), channel_id=1, source_target_pairs={{0,4},{4,0},{8,12},{12,8},{1,5},{5,1},{9,13},{13,9},{2,6},{6,2},{1... | collective-permute-start | bytes 1572872 | tf_op jit(solution)/shard_map/ppermute | solution.py:377
  134.2 22.3 %collective-permute-start.32 = (bf16[128,2048]{1,0:T(8,128)(2,1)S(1)}, bf16[128,2048]{1,0:T(8,128)(2,1)S(1)}, u32[]{:S(2)}, u32[]{:S(2)}) collective-permute-start(bf16[128,2048]{1,0:T(8,128)(2,1)S(1)} %fusion.9), channel_id=1, source_target_pairs={{0,1},{1,0},{2,3},{3,2},{4,8},{5,9},{6,10},{7,11},{8,4},{9,5},{10,... | collective-permute-start | bytes 1572872 | tf_op jit(solution)/shard_map/ppermute | solution.py:380
  145.3 19.7 %collective-permute-start.31 = (bf16[128,2048]{1,0:T(8,128)(2,1)S(1)}, bf16[128,2048]{1,0:T(8,128)(2,1)S(1)}, u32[]{:S(2)}, u32[]{:S(2)}) collective-permute-start(bf16[128,2048]{1,0:T(8,128)(2,1)S(1)} %bitcast_select_fusion), channel_id=1, source_target_pairs={{0,4},{4,0},{8,12},{12,8},{1,5},{5,1},{9,13},{13,9},{2,6},{6,2},{1... | collective-permute-start | bytes 1572872 | tf_op jit(solution)/shard_map/ppermute | solution.py:377
  145.4 22.3 %collective-permute-start.35 = (bf16[128,2048]{1,0:T(8,128)(2,1)S(1)}, bf16[128,2048]{1,0:T(8,128)(2,1)S(1)}, u32[]{:S(2)}, u32[]{:S(2)}) collective-permute-start(bf16[128,2048]{1,0:T(8,128)(2,1)S(1)} %fusion.8), channel_id=1, source_target_pairs={{0,1},{1,0},{2,3},{3,2},{4,8},{5,9},{6,10},{7,11},{8,4},{9,5},{10,... | collective-permute-start | bytes 1572872 | tf_op jit(solution)/shard_map/ppermute | solution.py:380
  156.6 36.6 %collective-permute-start.33 = (bf16[128,2048]{1,0:T(8,128)(2,1)S(1)}, bf16[128,2048]{1,0:T(8,128)(2,1)S(1)}, u32[]{:S(2)}, u32[]{:S(2)}) collective-permute-start(bf16[128,2048]{1,0:T(8,128)(2,1)S(1)} %fusion.10), channel_id=1, source_target_pairs={{0,4},{4,0},{8,12},{12,8},{1,5},{5,1},{9,13},{13,9},{2,6},{6,2},{1... | collective-permute-start | bytes 1572872 | tf_op jit(solution)/shard_map/ppermute | solution.py:377
  156.7 36.6 %collective-permute-start.34 = (bf16[128,2048]{1,0:T(8,128)(2,1)S(1)}, bf16[128,2048]{1,0:T(8,128)(2,1)S(1)}, u32[]{:S(2)}, u32[]{:S(2)}) collective-permute-start(bf16[128,2048]{1,0:T(8,128)(2,1)S(1)} %fusion.6), channel_id=1, source_target_pairs={{0,1},{1,0},{2,3},{3,2},{4,8},{5,9},{6,10},{7,11},{8,4},{9,5},{10,... | collective-permute-start | bytes 1572872 | tf_op jit(solution)/shard_map/ppermute | solution.py:380
  167.9 30.1 %collective-permute-start.36 = (bf16[128,2048]{1,0:T(8,128)(2,1)S(1)}, bf16[128,2048]{1,0:T(8,128)(2,1)S(1)}, u32[]{:S(2)}, u32[]{:S(2)}) collective-permute-start(bf16[128,2048]{1,0:T(8,128)(2,1)S(1)} %fusion.11), channel_id=1, source_target_pairs={{0,4},{4,0},{8,12},{12,8},{1,5},{5,1},{9,13},{13,9},{2,6},{6,2},{1... | collective-permute-start | bytes 1572872 | tf_op jit(solution)/shard_map/ppermute | solution.py:377
  167.9 30.0 %collective-permute-start.37 = (bf16[128,2048]{1,0:T(8,128)(2,1)S(1)}, bf16[128,2048]{1,0:T(8,128)(2,1)S(1)}, u32[]{:S(2)}, u32[]{:S(2)}) collective-permute-start(bf16[128,2048]{1,0:T(8,128)(2,1)S(1)} %fusion.5), channel_id=1, source_target_pairs={{0,1},{1,0},{2,3},{3,2},{4,8},{5,9},{6,10},{7,11},{8,4},{9,5},{10,... | collective-permute-start | bytes 1572872 | tf_op jit(solution)/shard_map/ppermute | solution.py:380
  193.3 15.8 %collective-permute-start.39 = (bf16[128,2048]{1,0:T(8,128)(2,1)S(1)}, bf16[128,2048]{1,0:T(8,128)(2,1)S(1)}, u32[]{:S(2)}, u32[]{:S(2)}) collective-permute-start(bf16[128,2048]{1,0:T(8,128)(2,1)S(1)} %get-tuple-element.90), channel_id=1, source_target_pairs={{0,4},{4,0},{8,12},{12,8},{1,5},{5,1},{9,13},{13,9},{2,6},{6,2},{1... | collective-permute-start | bytes 1572872 | tf_op jit(solution)/shard_map/ppermute | solution.py:377
  197.9 22.4 %collective-permute-start.38 = (bf16[128,2048]{1,0:T(8,128)(2,1)S(1)}, bf16[128,2048]{1,0:T(8,128)(2,1)S(1)}, u32[]{:S(2)}, u32[]{:S(2)}) collective-permute-start(bf16[128,2048]{1,0:T(8,128)(2,1)S(1)} %get-tuple-element.88), channel_id=1, source_target_pairs={{0,4},{4,0},{8,12},{12,8},{1,5},{5,1},{9,13},{13,9},{2,6},{6,2},{1... | collective-permute-start | bytes 1572872 | tf_op jit(solution)/shard_map/ppermute | solution.py:377
  209.2 22.3 %collective-permute-start.42 = (bf16[128,2048]{1,0:T(8,128)(2,1)S(1)}, bf16[128,2048]{1,0:T(8,128)(2,1)S(1)}, u32[]{:S(2)}, u32[]{:S(2)}) collective-permute-start(bf16[128,2048]{1,0:T(8,128)(2,1)S(1)} %get-tuple-element.93), channel_id=1, source_target_pairs={{0,4},{4,0},{8,12},{12,8},{1,5},{5,1},{9,13},{13,9},{2,6},{6,2},{1... | collective-permute-start | bytes 1572872 | tf_op jit(solution)/shard_map/ppermute | solution.py:377
  211.8 19.9 %collective-permute-start.43 = (bf16[128,2048]{1,0:T(8,128)(2,1)S(1)}, bf16[128,2048]{1,0:T(8,128)(2,1)S(1)}, u32[]{:S(2)}, u32[]{:S(2)}) collective-permute-start(bf16[128,2048]{1,0:T(8,128)(2,1)S(1)} %fusion.3), channel_id=1, source_target_pairs={{0,1},{1,0},{2,3},{3,2},{4,8},{5,9},{6,10},{7,11},{8,4},{9,5},{10,... | collective-permute-start | bytes 1572872 | tf_op jit(solution)/shard_map/ppermute | solution.py:380
  220.5 22.3 %collective-permute-start.41 = (bf16[128,2048]{1,0:T(8,128)(2,1)S(1)}, bf16[128,2048]{1,0:T(8,128)(2,1)S(1)}, u32[]{:S(2)}, u32[]{:S(2)}) collective-permute-start(bf16[128,2048]{1,0:T(8,128)(2,1)S(1)} %get-tuple-element.92), channel_id=1, source_target_pairs={{0,4},{4,0},{8,12},{12,8},{1,5},{5,1},{9,13},{13,9},{2,6},{6,2},{1... | collective-permute-start | bytes 1572872 | tf_op jit(solution)/shard_map/ppermute | solution.py:377
  223.0 19.9 %collective-permute-start.40 = (bf16[128,2048]{1,0:T(8,128)(2,1)S(1)}, bf16[128,2048]{1,0:T(8,128)(2,1)S(1)}, u32[]{:S(2)}, u32[]{:S(2)}) collective-permute-start(bf16[128,2048]{1,0:T(8,128)(2,1)S(1)} %fusion.7), channel_id=1, source_target_pairs={{0,1},{1,0},{2,3},{3,2},{4,8},{5,9},{6,10},{7,11},{8,4},{9,5},{10,... | collective-permute-start | bytes 1572872 | tf_op jit(solution)/shard_map/ppermute | solution.py:380
  231.9 22.2 %collective-permute-start.46 = (bf16[128,2048]{1,0:T(8,128)(2,1)S(1)}, bf16[128,2048]{1,0:T(8,128)(2,1)S(1)}, u32[]{:S(2)}, u32[]{:S(2)}) collective-permute-start(bf16[128,2048]{1,0:T(8,128)(2,1)S(1)} %fusion.13), channel_id=1, source_target_pairs={{0,4},{4,0},{8,12},{12,8},{1,5},{5,1},{9,13},{13,9},{2,6},{6,2},{1... | collective-permute-start | bytes 1572872 | tf_op jit(solution)/shard_map/ppermute | solution.py:377
  234.4 19.6 %collective-permute-start.47 = (bf16[128,2048]{1,0:T(8,128)(2,1)S(1)}, bf16[128,2048]{1,0:T(8,128)(2,1)S(1)}, u32[]{:S(2)}, u32[]{:S(2)}) collective-permute-start(bf16[128,2048]{1,0:T(8,128)(2,1)S(1)} %fusion.2), channel_id=1, source_target_pairs={{0,1},{1,0},{2,3},{3,2},{4,8},{5,9},{6,10},{7,11},{8,4},{9,5},{10,... | collective-permute-start | bytes 1572872 | tf_op jit(solution)/shard_map/ppermute | solution.py:380
  243.1 22.2 %collective-permute-start.44 = (bf16[128,2048]{1,0:T(8,128)(2,1)S(1)}, bf16[128,2048]{1,0:T(8,128)(2,1)S(1)}, u32[]{:S(2)}, u32[]{:S(2)}) collective-permute-start(bf16[128,2048]{1,0:T(8,128)(2,1)S(1)} %fusion.12), channel_id=1, source_target_pairs={{0,4},{4,0},{8,12},{12,8},{1,5},{5,1},{9,13},{13,9},{2,6},{6,2},{1... | collective-permute-start | bytes 1572872 | tf_op jit(solution)/shard_map/ppermute | solution.py:377
  245.7 19.6 %collective-permute-start.45 = (bf16[128,2048]{1,0:T(8,128)(2,1)S(1)}, bf16[128,2048]{1,0:T(8,128)(2,1)S(1)}, u32[]{:S(2)}, u32[]{:S(2)}) collective-permute-start(bf16[128,2048]{1,0:T(8,128)(2,1)S(1)} %fusion.4), channel_id=1, source_target_pairs={{0,1},{1,0},{2,3},{3,2},{4,8},{5,9},{6,10},{7,11},{8,4},{9,5},{10,... | collective-permute-start | bytes 1572872 | tf_op jit(solution)/shard_map/ppermute | solution.py:380
  (30 other events, 464.9 us)

commit v3 on v2

--- a/solution.py
+++ b/solution.py
@@ -18,7 +18,7 @@
 norm_eps = 1e-05
 masked_score = -1e30
 log2_e = 1.4426950408889634
-VMEM_LIMIT = 52 * 1024 * 1024
+VMEM_LIMIT = 42 * 1024 * 1024
 GROUP = 2
 BLOCK = 512
 VMEM = pl.BlockSpec(memory_space=pltpu.VMEM)
@@ -58,7 +58,7 @@
     w_query, w_out, table = refs[:3]
     outs, refs = refs[-12 - streams : -12], refs[3 : -12 - streams] + refs[-12:]
     kv_pieces = refs[:-12]
-    held, query_w, out_w, rows_table, kv, query, top, acc, flat, sems, q_sems, o_sems = refs[-12:]
+    flat, held, query_w, out_w, rows_table, kv, query, top, acc, sems, q_sems, o_sems = refs[-12:]
     rows = held.shape[0]
     each = rows // streams
     width = held.shape[1] // count
@@ -106,13 +106,11 @@
         copy.start()
     out_parts = out_w.shape[0]
     out_columns = out_w.shape[2]
+    far = jnp.where(rank < count // 2, count - 1, 0)
 
     def out_copy(k):
-        return pltpu.make_async_copy(
-            w_out.at[:, pl.ds(pl.multiple_of(k * out_columns, out_columns), out_columns)],
-            out_w.at[k],
-            o_sems.at[k * o_sems.shape[0] // out_parts],
-        )
+        at = pl.multiple_of(far * width + k * out_columns, out_columns)
+        return pltpu.make_async_copy(w_out.at[:, pl.ds(at, out_columns)], out_w.at[k], o_sems.at[k])
 
     wait_for(held, sems.at[0])
     table_copy.wait()
@@ -171,17 +169,59 @@
         span = slice(h * rows, (h + 1) * rows)
         flat[:, h * HD : (h + 1) * HD] = (acc[span, :HD] / acc[span, HD:]).astype(jnp.bfloat16)
 
-    per_block = width // out_columns
+    for k in range(out_parts):
+        out_copy(k).wait()
+        mixed = jnp.dot(flat[...], out_w[k], preferred_element_type=jnp.float32)
+        for j in range(streams):
+            outs[j][:, k * out_columns : (k + 1) * out_columns] = mixed[
+                j * each : (j + 1) * each
+            ].astype(jnp.bfloat16)
+
+
+def output_kernel(flat, w_out, *refs):
+    outs, weight, sems = refs[:-2], refs[-2], refs[-1]
+    count, each, width = outs[0].shape
+    parts, _, columns = weight.shape
+    per_block = parts // count
+
+    def copy(k):
+        at = pl.multiple_of(k * columns, columns)
+        return pltpu.make_async_copy(w_out.at[:, pl.ds(at, columns)], weight.at[k], sems.at[k])
+
+    for k in range(parts):
+        copy(k).start()
 
     @pl.loop(0, count)
     def _(b):
         for k in range(per_block):
-            out_copy(b * per_block + k).wait()
-            mixed = jnp.dot(flat[...], out_w[b * per_block + k], preferred_element_type=jnp.float32)
-            for j in range(streams):
-                outs[j][b, :, k * out_columns : (k + 1) * out_columns] = mixed[
-                    j * each : (j + 1) * each
-                ].astype(jnp.bfloat16)
+            copy(b * per_block + k).wait()
+            mixed = jnp.dot(flat[...], weight[b * per_block + k], preferred_element_type=jnp.float32)
+            for j, out in enumerate(outs):
+                out[b, :, k * columns : (k + 1) * columns] = mixed[j * each : (j + 1) * each].astype(
+                    jnp.bfloat16
+                )
+
+
+def output_terms(count, streams, flat, w_out):
+    rows, inner = flat.shape
+    width = w_out.shape[1] // count
+    columns = min(width, 1024)
+    parts = w_out.shape[1] // columns
+    return pl.pallas_call(
+        output_kernel,
+        out_shape=[jax.ShapeDtypeStruct((count, rows // streams, width), jnp.bfloat16)] * streams,
+        in_specs=[VMEM, ANY],
+        out_specs=[VMEM] * streams,
+        scratch_shapes=[
+            pltpu.VMEM((parts, inner, columns), jnp.bfloat16),
+            pltpu.SemaphoreType.DMA((parts,)),
+        ],
+        compiler_params=pltpu.CompilerParams(vmem_limit_bytes=VMEM_LIMIT),
+        cost_estimate=pl.CostEstimate(
+            flops=rows * inner * width * count, bytes_accessed=0, transcendentals=0
+        ),
+        name="output_terms",
+    )(flat, in_hbm(w_out))
 
 
 def chunk_terms(count, low, each, scaled, arrived, info, w_query, w_out, table, kv_pieces):
@@ -195,12 +235,13 @@
     pieces_of = [[(kind, step) for kind, step, _ in of] for of in arrived]
     q_columns = min(columns, 256)
     o_columns = min(width, 1024)
-    q_parts, o_parts = columns // q_columns, model // o_columns
+    q_parts, o_parts = columns // q_columns, width // o_columns
     return pl.pallas_call(
         functools.partial(chunk_kernel, count, pieces_of, low),
-        out_shape=[jax.ShapeDtypeStruct((count, each, width), jnp.bfloat16)] * len(arrived),
+        out_shape=[jax.ShapeDtypeStruct((each, width), jnp.bfloat16)] * len(arrived)
+        + [jax.ShapeDtypeStruct((rows, inner), jnp.bfloat16)],
         in_specs=[SMEM] + [ANY] * (len(pieces) + 3 + len(kv_pieces)),
-        out_specs=[VMEM] * len(arrived),
+        out_specs=[VMEM] * (len(arrived) + 1),
         scratch_shapes=[
             pltpu.VMEM((rows, model), jnp.bfloat16),
             pltpu.VMEM((q_parts, model, q_columns), jnp.bfloat16),
@@ -210,7 +251,6 @@
             pltpu.VMEM((heads * rows, HD), jnp.bfloat16),
             pltpu.VMEM((heads * rows, HD), jnp.float32),
             pltpu.VMEM((heads * rows, 2 * HD), jnp.float32),
-            pltpu.VMEM((rows, inner), jnp.bfloat16),
             pltpu.SemaphoreType.DMA((3,)),
             pltpu.SemaphoreType.DMA((q_parts,)),
             pltpu.SemaphoreType.DMA((o_parts,)),
@@ -382,15 +422,17 @@
     def term(self, terms, upward, step):
         dest = jnp.where(upward, self.rank + self.count - step, self.rank - self.count + step)
         valid = (dest >= 0) & (dest < self.count)
+        if terms is None:
+            return None, valid
         return lax.dynamic_index_in_dim(terms, jnp.clip(dest, 0, self.count - 1), 0, False), valid
 
-    def round(self, step, own, terms, last, earlier):
+    def round(self, step, own, terms, first, last, earlier):
         count = self.count
         from_outer, from_inner = last
         gather_outer = own is not None and step < count
         gather_inner = own is not None and step < count - 1
-        scatter_outer = terms is not None and step > 1
-        scatter_inner = terms is not None and step > 2
+        scatter_outer = first is not None and step > 1
+        scatter_inner = first is not None and step > 2
         to_outer = to_inner = None
         if gather_outer:
             to_outer = own if step == 1 else from_inner
@@ -398,6 +440,8 @@
             to_inner = own if step == 1 else from_outer
         if scatter_outer:
             mine, valid = self.term(terms, self.even, step - 1)
+            if step == 2:
+                mine = first
             if step > 3:
                 added = (mine.astype(jnp.float32) + from_inner.astype(jnp.float32)).astype(jnp.bfloat16)
                 mine = jnp.where(self.middle, added, mine)
@@ -407,7 +451,7 @@
             mine = (mine.astype(jnp.float32) + from_outer.astype(jnp.float32)).astype(jnp.bfloat16)
             to_inner = mine if to_inner is None else jnp.where(valid, mine, to_inner)
         to_outer, to_inner = after((to_outer, to_inner), earlier)
-        alone = step if terms is None and step > 1 else None
+        alone = step if first is None and step > 1 else None
         got_outer = None if to_outer is None else self.outer(to_outer, alone)
         got_inner = None if to_inner is None else self.inner(to_inner)
         return got_outer, got_inner
@@ -415,7 +459,7 @@
     def scatter(self, terms, earlier):
         last = (None, None)
         for step in range(2, self.count + 1):
-            last = self.round(step, None, terms, last, earlier)
+            last = self.round(step, None, terms, self.term(terms, self.even, 1)[0], last, earlier)
         return self.total(terms, last)
 
     def add(self, a, b):
@@ -493,6 +537,7 @@
         kv_pieces = None
         last = [(None, None)] * STREAMS
         terms = [None] * STREAMS
+        firsts = [None] * STREAMS
         history = []
         for period in range(PERIODS + 1):
             gather = period < PERIODS
@@ -500,15 +545,17 @@
             arrived = [[] for _ in range(STREAMS)]
             for step in range(1, count + 1):
                 for j in range(STREAMS):
-                    if not (gather and step < count) and not (terms[j] is not None and step > 1):
+                    if not (gather and step < count) and not (firsts[j] is not None and step > 1):
                         continue
                     if gather and step == 1:
                         low = (period * STREAMS + j) * chunk
                         owns[j] = scaled[low : low + chunk]
                     earlier = [history[-STREAMS - 1 : -STREAMS], last[j]]
 
-                    last[j] = line.round(step, owns[j], terms[j], last[j], earlier)
+                    last[j] = line.round(step, owns[j], terms[j], firsts[j], last[j], earlier)
                     history.append(last[j])
+                    if firsts[j] is not None and j == 0 and step == 2:
+                        terms = output_terms(count, STREAMS, after(flat, last[j]), w_out)
                     if gather and step < count:
                         arrived[j].append(("outer", step, last[j][0]))
                         if step < count - 1:
@@ -531,14 +578,15 @@
                     for d in range(1, sp_count)
                 ]
             for j in range(STREAMS):
-                if terms[j] is not None:
+                if period > 0:
                     low = ((period - 1) * STREAMS + j) * chunk
                     out = finish(count, low, infos[0], hidden, terms[j], last[j], out)
             if gather:
                 low = period * STREAMS * chunk
-                terms = chunk_terms(
+                *firsts, flat = chunk_terms(
                     count, low, chunk, scaled, arrived, infos[period], w_query, w_out, table, kv_pieces
                 )
+                terms = [None] * STREAMS
         return out
 
     return body

time: 269 us -> 261 us (0.970)
  Pallas kernels: 64.9 us -> 59.2 us
  starting transfers between devices: 55.7 us -> 51.6 us
    ppermute x17, waiting for transfers between devices: 29 us -> 55.1 us  [inner(): return lax.ppermute(value, ('tp', 'sp'), self.inner_pairs)]
    ppermute x22, waiting for transfers between devices: 95.1 us -> 70.6 us  [outer(): return lax.ppermute(value, 'tp', pairs)]
    pallas_call x2, Pallas kernels: 47.7 us -> 31.3 us  [chunk_terms(): pl.pallas_call(functools.partial(chunk_kernel, count, pieces_of, low), ou...]
    pallas_call x0 -> x2, Pallas kernels: none -> 14.9 us  [output_terms(): pl.pallas_call(output_kernel, out_shape=[jax.ShapeDtypeStruct((count, row...]
    ppermute x22, starting transfers between devices: 41 us -> 35.2 us  [outer(): return lax.ppermute(value, 'tp', pairs)]
    pallas_call x4, Pallas kernels: 11.5 us -> 7.27 us  [finish(): pl.pallas_call(functools.partial(finish_kernel, count, low, inner is not...]
  transfers between devices with their start and end apart: 48 -> 48, of which waited for: 27 -> 31; matrix products, arithmetic and copies ran while one was open for 4% -> 3% of each run, Pallas kernels for 23% -> 22%
where the time goes in v3:
time: 261 us; the launch traced here: 258 us
  waiting for transfers between devices  130 us (50%)
  Pallas kernels  59.2 us (23%)
  starting transfers between devices  51.6 us (20%)
  other arithmetic  8.11 us (3%)
  between operations  5.74 us (2%)
  local copies, waits for them, and re-layouts  3.17 us (1%)
    ppermute x22, waiting for transfers between devices, outer(): return lax.ppermute(value, 'tp', pairs)  70.6 us
    ppermute x17, waiting for transfers between devices, inner(): return lax.ppermute(value, ('tp', 'sp'), self.inner_pairs)  55.1 us
    ppermute x22, starting transfers between devices, outer(): return lax.ppermute(value, 'tp', pairs)  35.2 us
    pallas_call x2, Pallas kernels, chunk_terms(): pl.pallas_call(functools.partial(chunk_kernel, count, pieces_of, low), ou...  31.3 us
    pallas_call x2, Pallas kernels, output_terms(): pl.pallas_call(output_kernel, out_shape=[jax.ShapeDtypeStruct((count, row...  14.9 us
    ppermute x17, starting transfers between devices, inner(): return lax.ppermute(value, ('tp', 'sp'), self.inner_pairs)  9.7 us
    pallas_call x4, Pallas kernels, finish(): pl.pallas_call(functools.partial(finish_kernel, count, low, inner is not...  7.27 us
    pallas_call x1, Pallas kernels, kv_terms_of(): pl.pallas_call(functools.partial(kv_kernel, HQ // KV, slots), out_shape=s...  5.55 us
  transfers between devices with their start and end apart: 48, of which 31 were waited for; matrix products, arithmetic and copies ran while one was open for 3% of the time, Pallas kernels for 22%

profile of v3, /device:TPU:10, one launch (start us, length us, event | category | flops | bytes accessed | tf_op | source)
XLA Modules:
  0.0 258.0 jit_solution(8256569078678509262)
XLA Ops:
  0.7 2.3 fusion.1
  3.0 1.6 collective-permute-start.17
  9.2 2.7 %collective-permute-start.6 = (bf16[128,2048]{1,0:T(8,128)(2,1)}, bf16[128,2048]{1,0:T(8,128)(2,1)S(1)}, u32[]{:S(2)}, u32[]{:S(2)}) collective-permute-start(bf16[128,2048]{1,0:T(8,128)(2,1)} %get-tuple-element.63), channel_id=1, source_target_pairs={{0,1},{1,0},{2,3},{3,2},{4,8},{5,9},{6,10},{7,11},{8,4},{9,5},{10,... | collective-permute-start | bytes 1572872 | tf_op jit(solution)/shard_map/ppermute | solution.py:420
  12.1 5.5 %kv_terms.1 = (bf16[128,2048]{1,0:T(8,128)(2,1)S(1)}, bf16[128,2048]{1,0:T(8,128)(2,1)S(1)}, bf16[64,2048]{1,0:T(8,128)(2,1)S(1)}, bf16[64,2048]{1,0:T(8,128)(2,1)S(1)}) custom-call(s32[4]{0:T(128)S(1)} %pad_add_fusion.info_ref, bf16[512,2048]{1,0:T(8,128)(2,1)} %copy-done.3, bf16[2048,512]{1,0:T(8,128)(2,1)} %w_key.1, bf16[2048,512]{1,0:T(8,128)(2,1)} %w_value.1), custom_call_target="tpu_custom_call" | custom-call | bytes 2097152 | tf_op jit(solution)/shard_map/kv_terms/pallas_call | solution.py:297
  19.7 2.3 collective-permute-done.2
  23.2 3.4 %collective-permute-start.4 = (bf16[128,2048]{1,0:T(8,128)(2,1)}, bf16[128,2048]{1,0:T(8,128)(2,1)S(1)}, u32[]{:S(2)}, u32[]{:S(2)}) collective-permute-start(bf16[128,2048]{1,0:T(8,128)(2,1)} %get-tuple-element.61), channel_id=1, source_target_pairs={{0,4},{4,0},{8,12},{12,8},{1,5},{5,1},{9,13},{13,9},{2,6},{6,2},{1... | collective-permute-start | bytes 1572872 | tf_op jit(solution)/shard_map/ppermute | solution.py:417
  26.8 2.0 collective-permute-start.10
  28.9 5.6 %collective-permute-done.18 = bf16[128,2048]{1,0:T(8,128)(2,1)} collective-permute-done((bf16[128,2048]{1,0:T(8,128)(2,1)S(1)}, bf16[128,2048]{1,0:T(8,128)(2,1)}, u32[]{:S(2)}, u32[]{:S(2)}) %collective-permute-start.18) | collective-permute-done | bytes 524320 | tf_op jit(solution)/shard_map/ppermute | solution.py:417
  35.7 2.1 collective-permute-done.3.refs_6_
  37.8 6.5 %collective-permute-done.4.refs_5_ = bf16[128,2048]{1,0:T(8,128)(2,1)S(1)} collective-permute-done((bf16[128,2048]{1,0:T(8,128)(2,1)}, bf16[128,2048]{1,0:T(8,128)(2,1)S(1)}, u32[]{:S(2)}, u32[]{:S(2)}) %collective-permute-start.4) | collective-permute-done | bytes 524320 | tf_op jit(solution)/shard_map/ppermute | solution.py:417
  44.2 1.5 collective-permute-start.19
  50.3 4.4 %collective-permute-start.11 = (bf16[128,2048]{1,0:T(8,128)(2,1)S(1)}, bf16[128,2048]{1,0:T(8,128)(2,1)S(1)}, u32[]{:S(2)}, u32[]{:S(2)}) collective-permute-start(bf16[128,2048]{1,0:T(8,128)(2,1)S(1)} %collective-permute-done.9.refs_3_), channel_id=1, source_target_pairs={{4,0},{8,12},{5,1},{9,13},{6,2},{10,14},{7,3},{11,15},{20,16},{24,... | collective-permute-start | bytes 1572872 | tf_op jit(solution)/shard_map/ppermute | solution.py:417
  54.8 5.5 %collective-permute-done.19 = bf16[128,2048]{1,0:T(8,128)(2,1)S(1)} collective-permute-done((bf16[128,2048]{1,0:T(8,128)(2,1)S(1)}, bf16[128,2048]{1,0:T(8,128)(2,1)S(1)}, u32[]{:S(2)}, u32[]{:S(2)}) %collective-permute-start.19) | collective-permute-done | bytes 524320 | tf_op jit(solution)/shard_map/ppermute | solution.py:420
  61.6 8.9 %collective-permute-done.8.refs_8_ = bf16[128,2048]{1,0:T(8,128)(2,1)} collective-permute-done((bf16[128,2048]{1,0:T(8,128)(2,1)S(1)}, bf16[128,2048]{1,0:T(8,128)(2,1)}, u32[]{:S(2)}, u32[]{:S(2)}) %collective-permute-start.8) | collective-permute-done | bytes 524320 | tf_op jit(solution)/shard_map/ppermute | solution.py:420
  71.1 4.0 %collective-permute-start.14 = (bf16[128,2048]{1,0:T(8,128)(2,1)}, bf16[128,2048]{1,0:T(8,128)(2,1)S(1)}, u32[]{:S(2)}, u32[]{:S(2)}) collective-permute-start(bf16[128,2048]{1,0:T(8,128)(2,1)} %collective-permute-done.8.refs_8_), channel_id=1, source_target_pairs={{4,0},{8,12},{5,1},{9,13},{6,2},{10,14},{7,3},{11,15},{20,16},{24,... | collective-permute-start | bytes 1572872 | tf_op jit(solution)/shard_map/ppermute | solution.py:417
  75.5 3.0 %collective-permute-done.20 = bf16[64,2048]{1,0:T(8,128)(2,1)S(1)} collective-permute-done((bf16[64,2048]{1,0:T(8,128)(2,1)S(1)}, bf16[64,2048]{1,0:T(8,128)(2,1)S(1)}, u32[]{:S(2)}, u32[]{:S(2)}) %collective-permute-start.20) | collective-permute-done | bytes 262176 | tf_op jit(solution)/shard_map/ppermute | solution.py:417
  78.8 1.7 collective-permute-start.22
  86.1 2.9 %collective-permute-done.14.refs_9_ = bf16[128,2048]{1,0:T(8,128)(2,1)S(1)} collective-permute-done((bf16[128,2048]{1,0:T(8,128)(2,1)}, bf16[128,2048]{1,0:T(8,128)(2,1)S(1)}, u32[]{:S(2)}, u32[]{:S(2)}) %collective-permute-start.14) | collective-permute-done | bytes 524320 | tf_op jit(solution)/shard_map/ppermute | solution.py:417
  89.1 2.4 collective-permute-start.12
  93.4 15.6 %chunk_terms.2 = (bf16[128,2048]{1,0:T(8,128)(2,1)S(1)}, bf16[128,2048]{1,0:T(8,128)(2,1)S(1)}, bf16[256,1024]{1,0:T(8,128)(2,1)S(1)}) custom-call(s32[3]{0:T(128)S(1)} %add_add_fusion.1.info_ref, bf16[512,2048]{1,0:T(8,128)(2,1)} %copy-done.3, bf16[128,2048]{1,0:T(8,128)(2,1)} %copy-done.15, bf16[128,2048]{1,0:T(8,128)(2,1)} %copy-done.16, ...), custom_call_target="tpu_custom_call" | custom-call | flops 2147483648 | tf_op jit(solution)/shard_map/chunk_terms/pallas_call | solution.py:239
  109.1 2.6 %collective-permute-start.24 = (bf16[128,2048]{1,0:T(8,128)(2,1)S(1)}, bf16[128,2048]{1,0:T(8,128)(2,1)S(1)}, u32[]{:S(2)}, u32[]{:S(2)}) collective-permute-start(bf16[128,2048]{1,0:T(8,128)(2,1)S(1)} %broadcast_select_fusion.1), channel_id=1, source_target_pairs={{0,4},{4,0},{8,12},{12,8},{1,5},{5,1},{9,13},{13,9},{2,6},{6,2},{1... | collective-permute-start | bytes 1572872 | tf_op jit(solution)/shard_map/ppermute | solution.py:417
  111.9 2.4 collective-permute-done.26.refs_5_
  114.3 1.7 collective-permute-start.29
  116.2 8.5 %collective-permute-done.24.refs_2_ = bf16[128,2048]{1,0:T(8,128)(2,1)S(1)} collective-permute-done((bf16[128,2048]{1,0:T(8,128)(2,1)S(1)}, bf16[128,2048]{1,0:T(8,128)(2,1)S(1)}, u32[]{:S(2)}, u32[]{:S(2)}) %collective-permute-start.24) | collective-permute-done | bytes 524320 | tf_op jit(solution)/shard_map/ppermute | solution.py:417
  125.1 7.6 %output_terms.2 = (bf16[4,128,2048]{2,1,0:T(8,128)(2,1)S(1)}, bf16[4,128,2048]{2,1,0:T(8,128)(2,1)S(1)}) custom-call(bf16[256,1024]{1,0:T(8,128)(2,1)S(1)} %get-tuple-element.83.flat, bf16[1024,8192]{1,0:T(8,128)(2,1)} %w_out.3), custom_call_target="tpu_custom_call" | custom-call | flops 2147483648 | tf_op jit(solution)/shard_map/output_terms/pallas_call | solution.py:210
  133.0 1.6 collective-permute-start.28
  134.7 1.7 collective-permute-done.30.refs_8_
  138.2 10.6 %collective-permute-done.33 = bf16[128,2048]{1,0:T(8,128)(2,1)S(1)} collective-permute-done((bf16[128,2048]{1,0:T(8,128)(2,1)S(1)}, bf16[128,2048]{1,0:T(8,128)(2,1)S(1)}, u32[]{:S(2)}, u32[]{:S(2)}) %collective-permute-start.33) | collective-permute-done | bytes 524320 | tf_op jit(solution)/shard_map/ppermute | solution.py:420
  149.7 10.4 %collective-permute-done.32 = bf16[128,2048]{1,0:T(8,128)(2,1)S(1)} collective-permute-done((bf16[128,2048]{1,0:T(8,128)(2,1)S(1)}, bf16[128,2048]{1,0:T(8,128)(2,1)S(1)}, u32[]{:S(2)}, u32[]{:S(2)}) %collective-permute-start.32) | collective-permute-done | bytes 524320 | tf_op jit(solution)/shard_map/ppermute | solution.py:420
  161.1 15.8 %chunk_terms.3 = (bf16[128,2048]{1,0:T(8,128)(2,1)S(1)}, bf16[128,2048]{1,0:T(8,128)(2,1)S(1)}, bf16[256,1024]{1,0:T(8,128)(2,1)S(1)}) custom-call(s32[3]{0:T(128)S(1)} %add_add_fusion.2.info_ref, bf16[512,2048]{1,0:T(8,128)(2,1)} %copy-done.3, bf16[128,2048]{1,0:T(8,128)(2,1)} %copy-done.24, bf16[128,2048]{1,0:T(8,128)(2,1)} %copy-done.4, ...), custom_call_target="tpu_custom_call" | custom-call | flops 2147483648 | tf_op jit(solution)/shard_map/chunk_terms/pallas_call | solution.py:239
  176.9 2.3 collective-permute-start.36
  179.1 1.5 collective-permute-done.37.outer
  180.6 2.0 collective-permute-done.38.inner
  183.1 8.9 %collective-permute-done.36 = bf16[128,2048]{1,0:T(8,128)(2,1)S(1)} collective-permute-done((bf16[128,2048]{1,0:T(8,128)(2,1)S(1)}, bf16[128,2048]{1,0:T(8,128)(2,1)S(1)}, u32[]{:S(2)}, u32[]{:S(2)}) %collective-permute-start.36) | collective-permute-done | bytes 524320 | tf_op jit(solution)/shard_map/ppermute | solution.py:417
  192.0 7.4 %output_terms.3 = (bf16[4,128,2048]{2,1,0:T(8,128)(2,1)S(1)}, bf16[4,128,2048]{2,1,0:T(8,128)(2,1)S(1)}) custom-call(bf16[256,1024]{1,0:T(8,128)(2,1)S(1)} %get-tuple-element.100.flat, bf16[1024,8192]{1,0:T(8,128)(2,1)} %w_out.3), custom_call_target="tpu_custom_call" | custom-call | flops 2147483648 | tf_op jit(solution)/shard_map/output_terms/pallas_call | solution.py:210
  199.4 3.8 %collective-permute-done.39 = bf16[128,2048]{1,0:T(8,128)(2,1)S(1)} collective-permute-done((bf16[128,2048]{1,0:T(8,128)(2,1)S(1)}, bf16[128,2048]{1,0:T(8,128)(2,1)S(1)}, u32[]{:S(2)}, u32[]{:S(2)}) %collective-permute-start.39) | collective-permute-done | bytes 524320 | tf_op jit(solution)/shard_map/ppermute | solution.py:417
  203.4 2.6 collective-permute-start.41
  207.7 10.5 %collective-permute-done.40 = bf16[128,2048]{1,0:T(8,128)(2,1)S(1)} collective-permute-done((bf16[128,2048]{1,0:T(8,128)(2,1)S(1)}, bf16[128,2048]{1,0:T(8,128)(2,1)S(1)}, u32[]{:S(2)}, u32[]{:S(2)}) %collective-permute-start.40) | collective-permute-done | bytes 524320 | tf_op jit(solution)/shard_map/ppermute | solution.py:420
  218.8 10.8 %collective-permute-done.42 = bf16[128,2048]{1,0:T(8,128)(2,1)S(1)} collective-permute-done((bf16[128,2048]{1,0:T(8,128)(2,1)S(1)}, bf16[128,2048]{1,0:T(8,128)(2,1)S(1)}, u32[]{:S(2)}, u32[]{:S(2)}) %collective-permute-start.42) | collective-permute-done | bytes 524320 | tf_op jit(solution)/shard_map/ppermute | solution.py:417
  229.9 1.8 collective-permute-start.46
  232.0 1.7 collective-permute-start.45
  233.8 1.8 finish.4.refs_0_
  235.6 1.8 finish.5.refs_0_
  237.4 7.4 %collective-permute-done.46.outer = bf16[128,2048]{1,0:T(8,128)(2,1)S(1)} collective-permute-done((bf16[128,2048]{1,0:T(8,128)(2,1)S(1)}, bf16[128,2048]{1,0:T(8,128)(2,1)S(1)}, u32[]{:S(2)}, u32[]{:S(2)}) %collective-permute-start.46) | collective-permute-done | bytes 524320 | tf_op jit(solution)/shard_map/ppermute | solution.py:417
  244.8 1.8 collective-permute-done.47.inner
  246.6 1.8 finish.6.refs_0_
  248.4 6.4 %collective-permute-done.44.outer = bf16[128,2048]{1,0:T(8,128)(2,1)S(1)} collective-permute-done((bf16[128,2048]{1,0:T(8,128)(2,1)S(1)}, bf16[128,2048]{1,0:T(8,128)(2,1)S(1)}, u32[]{:S(2)}, u32[]{:S(2)}) %collective-permute-start.44) | collective-permute-done | bytes 524320 | tf_op jit(solution)/shard_map/ppermute | solution.py:417
  256.0 1.8 finish.7
  (151 shorter events, 29.5 us)
Async XLA Ops:
  3.0 9.0 %collective-permute-start.17 = (f32[512]{0:T(512)S(1)}, f32[512]{0:T(512)S(1)}, u32[]{:S(2)}, u32[]{:S(2)}) collective-permute-start(f32[512]{0:T(512)S(1)} %get-tuple-element.121), channel_id=1, source_target_pairs={{0,12},{4,8},{8,4},{12,0},{1,13},{5,9},{9,5},{13,1},{2,14},{6,10},... | collective-permute-start | bytes 6152 | tf_op jit(solution)/shard_map/ppermute | solution.py:388
  4.6 7.4 %collective-permute-start.16 = (f32[512]{0:T(512)S(1)}, f32[512]{0:T(512)S(1)}, u32[]{:S(2)}, u32[]{:S(2)}) collective-permute-start(f32[512]{0:T(512)S(1)} %get-tuple-element.121), channel_id=1, source_target_pairs={{0,8},{4,12},{8,0},{12,4},{1,9},{5,13},{9,1},{13,5},{2,10},{6,14},... | collective-permute-start | bytes 6152 | tf_op jit(solution)/shard_map/ppermute | solution.py:388
  5.9 6.2 %collective-permute-start.15 = (f32[512]{0:T(512)S(1)}, f32[512]{0:T(512)S(1)}, u32[]{:S(2)}, u32[]{:S(2)}) collective-permute-start(f32[512]{0:T(512)S(1)} %get-tuple-element.121), channel_id=1, source_target_pairs={{0,4},{4,0},{8,12},{12,8},{1,5},{5,1},{9,13},{13,9},{2,6},{6,2},{1... | collective-permute-start | bytes 6152 | tf_op jit(solution)/shard_map/ppermute | solution.py:388
  8.5 18.2 %collective-permute-start.5 = (bf16[128,2048]{1,0:T(8,128)(2,1)}, bf16[128,2048]{1,0:T(8,128)(2,1)S(1)}, u32[]{:S(2)}, u32[]{:S(2)}) collective-permute-start(bf16[128,2048]{1,0:T(8,128)(2,1)} %get-tuple-element.63), channel_id=1, source_target_pairs={{0,4},{4,0},{8,12},{12,8},{1,5},{5,1},{9,13},{13,9},{2,6},{6,2},{1... | collective-permute-start | bytes 1572872 | tf_op jit(solution)/shard_map/ppermute | solution.py:417
  9.2 17.4 %collective-permute-start.6 = (bf16[128,2048]{1,0:T(8,128)(2,1)}, bf16[128,2048]{1,0:T(8,128)(2,1)S(1)}, u32[]{:S(2)}, u32[]{:S(2)}) collective-permute-start(bf16[128,2048]{1,0:T(8,128)(2,1)} %get-tuple-element.63), channel_id=1, source_target_pairs={{0,1},{1,0},{2,3},{3,2},{4,8},{5,9},{6,10},{7,11},{8,4},{9,5},{10,... | collective-permute-start | bytes 1572872 | tf_op jit(solution)/shard_map/ppermute | solution.py:420
  17.6 16.9 %collective-permute-start.18 = (bf16[128,2048]{1,0:T(8,128)(2,1)S(1)}, bf16[128,2048]{1,0:T(8,128)(2,1)}, u32[]{:S(2)}, u32[]{:S(2)}) collective-permute-start(bf16[128,2048]{1,0:T(8,128)(2,1)S(1)} %get-tuple-element.76), channel_id=1, source_target_pairs={{0,4},{12,8},{1,5},{13,9},{2,6},{14,10},{3,7},{15,11},{16,20},{28,... | collective-permute-start | bytes 1572872 | tf_op jit(solution)/shard_map/ppermute | solution.py:417
  19.1 3.0 %collective-permute-start.2 = (s32[4]{0:T(128)S(1)}, s32[4]{0:T(128)S(1)}, u32[]{:S(2)}, u32[]{:S(2)}) collective-permute-start(s32[4]{0:T(128)S(1)} %convert_reduce_fusion), channel_id=1, source_target_pairs={{0,3},{1,2},{2,1},{3,0},{4,7},{5,6},{6,5},{7,4},{8,11},{9,10},{10,... | collective-permute-start | bytes 56 | tf_op jit(solution)/shard_map/ppermute | solution.py:388
  19.1 3.6 %collective-permute-start.1 = (s32[4]{0:T(128)S(1)}, s32[4]{0:T(128)S(1)}, u32[]{:S(2)}, u32[]{:S(2)}) collective-permute-start(s32[4]{0:T(128)S(1)} %convert_reduce_fusion), channel_id=1, source_target_pairs={{0,2},{1,3},{2,0},{3,1},{4,6},{5,7},{6,4},{7,5},{8,10},{9,11},{10,... | collective-permute-start | bytes 56 | tf_op jit(solution)/shard_map/ppermute | solution.py:388
  22.1 1.1 collective-permute-start
  22.7 15.0 %collective-permute-start.3 = (bf16[128,2048]{1,0:T(8,128)(2,1)}, bf16[128,2048]{1,0:T(8,128)(2,1)S(1)}, u32[]{:S(2)}, u32[]{:S(2)}) collective-permute-start(bf16[128,2048]{1,0:T(8,128)(2,1)} %get-tuple-element.61), channel_id=1, source_target_pairs={{0,1},{1,0},{2,3},{3,2},{4,8},{5,9},{6,10},{7,11},{8,4},{9,5},{10,... | collective-permute-start | bytes 1572872 | tf_op jit(solution)/shard_map/ppermute | solution.py:420
  23.2 21.0 %collective-permute-start.4 = (bf16[128,2048]{1,0:T(8,128)(2,1)}, bf16[128,2048]{1,0:T(8,128)(2,1)S(1)}, u32[]{:S(2)}, u32[]{:S(2)}) collective-permute-start(bf16[128,2048]{1,0:T(8,128)(2,1)} %get-tuple-element.61), channel_id=1, source_target_pairs={{0,4},{4,0},{8,12},{12,8},{1,5},{5,1},{9,13},{13,9},{2,6},{6,2},{1... | collective-permute-start | bytes 1572872 | tf_op jit(solution)/shard_map/ppermute | solution.py:417
  26.7 22.3 %collective-permute-start.9 = (bf16[128,2048]{1,0:T(8,128)(2,1)S(1)}, bf16[128,2048]{1,0:T(8,128)(2,1)S(1)}, u32[]{:S(2)}, u32[]{:S(2)}) collective-permute-start(bf16[128,2048]{1,0:T(8,128)(2,1)S(1)} %collective-permute-done.5.refs_0_), channel_id=1, source_target_pairs={{0,1},{1,0},{2,3},{3,2},{4,8},{5,9},{6,10},{7,11},{8,4},{9,5},{10,... | collective-permute-start | bytes 1572872 | tf_op jit(solution)/shard_map/ppermute | solution.py:420
  26.8 23.5 %collective-permute-start.10 = (bf16[128,2048]{1,0:T(8,128)(2,1)S(1)}, bf16[128,2048]{1,0:T(8,128)(2,1)S(1)}, u32[]{:S(2)}, u32[]{:S(2)}) collective-permute-start(bf16[128,2048]{1,0:T(8,128)(2,1)S(1)} %collective-permute-done.6.refs_1_), channel_id=1, source_target_pairs={{4,0},{8,12},{5,1},{9,13},{6,2},{10,14},{7,3},{11,15},{20,16},{24,... | collective-permute-start | bytes 1572872 | tf_op jit(solution)/shard_map/ppermute | solution.py:417
  44.2 16.0 %collective-permute-start.19 = (bf16[128,2048]{1,0:T(8,128)(2,1)S(1)}, bf16[128,2048]{1,0:T(8,128)(2,1)S(1)}, u32[]{:S(2)}, u32[]{:S(2)}) collective-permute-start(bf16[128,2048]{1,0:T(8,128)(2,1)S(1)} %add_convert_fusion.4), channel_id=1, source_target_pairs={{0,1},{1,0},{2,3},{3,2},{4,8},{5,9},{6,10},{7,11},{8,4},{9,5},{10,... | collective-permute-start | bytes 1572872 | tf_op jit(solution)/shard_map/ppermute | solution.py:420
  45.8 15.8 %collective-permute-start.7 = (bf16[128,2048]{1,0:T(8,128)(2,1)S(1)}, bf16[128,2048]{1,0:T(8,128)(2,1)S(1)}, u32[]{:S(2)}, u32[]{:S(2)}) collective-permute-start(bf16[128,2048]{1,0:T(8,128)(2,1)S(1)} %collective-permute-done.3.refs_6_), channel_id=1, source_target_pairs={{4,0},{8,12},{5,1},{9,13},{6,2},{10,14},{7,3},{11,15},{20,16},{24,... | collective-permute-start | bytes 1572872 | tf_op jit(solution)/shard_map/ppermute | solution.py:417
  47.1 23.3 %collective-permute-start.8 = (bf16[128,2048]{1,0:T(8,128)(2,1)S(1)}, bf16[128,2048]{1,0:T(8,128)(2,1)}, u32[]{:S(2)}, u32[]{:S(2)}) collective-permute-start(bf16[128,2048]{1,0:T(8,128)(2,1)S(1)} %collective-permute-done.4.refs_5_), channel_id=1, source_target_pairs={{0,1},{1,0},{2,3},{3,2},{4,8},{5,9},{6,10},{7,11},{8,4},{9,5},{10,... | collective-permute-start | bytes 1572872 | tf_op jit(solution)/shard_map/ppermute | solution.py:420
  50.3 24.7 %collective-permute-start.11 = (bf16[128,2048]{1,0:T(8,128)(2,1)S(1)}, bf16[128,2048]{1,0:T(8,128)(2,1)S(1)}, u32[]{:S(2)}, u32[]{:S(2)}) collective-permute-start(bf16[128,2048]{1,0:T(8,128)(2,1)S(1)} %collective-permute-done.9.refs_3_), channel_id=1, source_target_pairs={{4,0},{8,12},{5,1},{9,13},{6,2},{10,14},{7,3},{11,15},{20,16},{24,... | collective-permute-start | bytes 1572872 | tf_op jit(solution)/shard_map/ppermute | solution.py:417
  70.4 8.0 %collective-permute-start.20 = (bf16[64,2048]{1,0:T(8,128)(2,1)S(1)}, bf16[64,2048]{1,0:T(8,128)(2,1)S(1)}, u32[]{:S(2)}, u32[]{:S(2)}) collective-permute-start(bf16[64,2048]{1,0:T(8,128)(2,1)S(1)} %fusion.14), channel_id=1, source_target_pairs={{0,4},{4,0},{8,12},{12,8},{1,5},{5,1},{9,13},{13,9},{2,6},{6,2},{1... | collective-permute-start | bytes 786440 | tf_op jit(solution)/shard_map/ppermute | solution.py:417
  71.1 17.9 %collective-permute-start.14 = (bf16[128,2048]{1,0:T(8,128)(2,1)}, bf16[128,2048]{1,0:T(8,128)(2,1)S(1)}, u32[]{:S(2)}, u32[]{:S(2)}) collective-permute-start(bf16[128,2048]{1,0:T(8,128)(2,1)} %collective-permute-done.8.refs_8_), channel_id=1, source_target_pairs={{4,0},{8,12},{5,1},{9,13},{6,2},{10,14},{7,3},{11,15},{20,16},{24,... | collective-permute-start | bytes 1572872 | tf_op jit(solution)/shard_map/ppermute | solution.py:417
  75.1 33.9 %collective-permute-start.13 = (bf16[128,2048]{1,0:T(8,128)(2,1)}, bf16[128,2048]{1,0:T(8,128)(2,1)S(1)}, u32[]{:S(2)}, u32[]{:S(2)}) collective-permute-start(bf16[128,2048]{1,0:T(8,128)(2,1)} %get-tuple-element.70), channel_id=1, source_target_pairs={{0,1},{1,0},{2,3},{3,2},{4,8},{5,9},{6,10},{7,11},{8,4},{9,5},{10,... | collective-permute-start | bytes 1572872 | tf_op jit(solution)/shard_map/ppermute | solution.py:420
  78.7 12.7 %collective-permute-start.21 = (bf16[512,256]{1,0:T(8,128)(2,1)S(1)}, bf16[512,256]{1,0:T(8,128)(2,1)S(1)}, u32[]{:S(2)}, u32[]{:S(2)}) collective-permute-start(bf16[512,256]{1,0:T(8,128)(2,1)S(1)} %kv_total.1.refs_13_), channel_id=1, source_target_pairs={{0,1},{1,0},{2,3},{3,2},{4,5},{5,4},{6,7},{7,6},{8,9},{9,8},{10,11... | collective-permute-start | bytes 786440 | tf_op jit(solution)/shard_map/ppermute | solution.py:577
  78.8 12.7 %collective-permute-start.22 = (bf16[512,256]{1,0:T(8,128)(2,1)S(1)}, bf16[512,256]{1,0:T(8,128)(2,1)S(1)}, u32[]{:S(2)}, u32[]{:S(2)}) collective-permute-start(bf16[512,256]{1,0:T(8,128)(2,1)S(1)} %kv_total.1.refs_13_), channel_id=1, source_target_pairs={{0,2},{1,3},{2,0},{3,1},{4,6},{5,7},{6,4},{7,5},{8,10},{9,11},{10,... | collective-permute-start | bytes 786440 | tf_op jit(solution)/shard_map/ppermute | solution.py:577
  80.4 12.2 %collective-permute-start.23 = (bf16[512,256]{1,0:T(8,128)(2,1)S(1)}, bf16[512,256]{1,0:T(8,128)(2,1)S(1)}, u32[]{:S(2)}, u32[]{:S(2)}) collective-permute-start(bf16[512,256]{1,0:T(8,128)(2,1)S(1)} %kv_total.1.refs_13_), channel_id=1, source_target_pairs={{0,3},{1,2},{2,1},{3,0},{4,7},{5,6},{6,5},{7,4},{8,11},{9,10},{10,... | collective-permute-start | bytes 786440 | tf_op jit(solution)/shard_map/ppermute | solution.py:577
  89.1 20.0 %collective-permute-start.12 = (bf16[128,2048]{1,0:T(8,128)(2,1)}, bf16[128,2048]{1,0:T(8,128)(2,1)S(1)}, u32[]{:S(2)}, u32[]{:S(2)}) collective-permute-start(bf16[128,2048]{1,0:T(8,128)(2,1)} %get-tuple-element.70), channel_id=1, source_target_pairs={{0,4},{4,0},{8,12},{12,8},{1,5},{5,1},{9,13},{13,9},{2,6},{6,2},{1... | collective-permute-start | bytes 1572872 | tf_op jit(solution)/shard_map/ppermute | solution.py:417
  91.4 22.9 %collective-permute-start.26 = (bf16[128,2048]{1,0:T(8,128)(2,1)}, bf16[128,2048]{1,0:T(8,128)(2,1)S(1)}, u32[]{:S(2)}, u32[]{:S(2)}) collective-permute-start(bf16[128,2048]{1,0:T(8,128)(2,1)} %get-tuple-element.86), channel_id=1, source_target_pairs={{0,4},{4,0},{8,12},{12,8},{1,5},{5,1},{9,13},{13,9},{2,6},{6,2},{1... | collective-permute-start | bytes 1572872 | tf_op jit(solution)/shard_map/ppermute | solution.py:417
  91.5 20.4 %collective-permute-start.27 = (bf16[128,2048]{1,0:T(8,128)(2,1)}, bf16[128,2048]{1,0:T(8,128)(2,1)S(1)}, u32[]{:S(2)}, u32[]{:S(2)}) collective-permute-start(bf16[128,2048]{1,0:T(8,128)(2,1)} %get-tuple-element.86), channel_id=1, source_target_pairs={{0,1},{1,0},{2,3},{3,2},{4,8},{5,9},{6,10},{7,11},{8,4},{9,5},{10,... | collective-permute-start | bytes 1572872 | tf_op jit(solution)/shard_map/ppermute | solution.py:420
  109.1 15.6 %collective-permute-start.24 = (bf16[128,2048]{1,0:T(8,128)(2,1)S(1)}, bf16[128,2048]{1,0:T(8,128)(2,1)S(1)}, u32[]{:S(2)}, u32[]{:S(2)}) collective-permute-start(bf16[128,2048]{1,0:T(8,128)(2,1)S(1)} %broadcast_select_fusion.1), channel_id=1, source_target_pairs={{0,4},{4,0},{8,12},{12,8},{1,5},{5,1},{9,13},{13,9},{2,6},{6,2},{1... | collective-permute-start | bytes 1572872 | tf_op jit(solution)/shard_map/ppermute | solution.py:417
  111.7 13.4 %collective-permute-start.25 = (bf16[128,2048]{1,0:T(8,128)(2,1)S(1)}, bf16[128,2048]{1,0:T(8,128)(2,1)S(1)}, u32[]{:S(2)}, u32[]{:S(2)}) collective-permute-start(bf16[128,2048]{1,0:T(8,128)(2,1)S(1)} %collective-permute-done.12.refs_0_), channel_id=1, source_target_pairs={{0,1},{1,0},{2,3},{3,2},{4,8},{5,9},{6,10},{7,11},{8,4},{9,5},{10,... | collective-permute-start | bytes 1572872 | tf_op jit(solution)/shard_map/ppermute | solution.py:420
  114.3 22.1 %collective-permute-start.29 = (bf16[128,2048]{1,0:T(8,128)(2,1)S(1)}, bf16[128,2048]{1,0:T(8,128)(2,1)S(1)}, u32[]{:S(2)}, u32[]{:S(2)}) collective-permute-start(bf16[128,2048]{1,0:T(8,128)(2,1)S(1)} %broadcast_select_fusion), channel_id=1, source_target_pairs={{0,4},{4,0},{8,12},{12,8},{1,5},{5,1},{9,13},{13,9},{2,6},{6,2},{1... | collective-permute-start | bytes 1572872 | tf_op jit(solution)/shard_map/ppermute | solution.py:417
  116.1 20.3 %collective-permute-start.30 = (bf16[128,2048]{1,0:T(8,128)(2,1)S(1)}, bf16[128,2048]{1,0:T(8,128)(2,1)S(1)}, u32[]{:S(2)}, u32[]{:S(2)}) collective-permute-start(bf16[128,2048]{1,0:T(8,128)(2,1)S(1)} %collective-permute-done.26.refs_5_), channel_id=1, source_target_pairs={{0,1},{1,0},{2,3},{3,2},{4,8},{5,9},{6,10},{7,11},{8,4},{9,5},{10,... | collective-permute-start | bytes 1572872 | tf_op jit(solution)/shard_map/ppermute | solution.py:420
  133.0 16.1 %collective-permute-start.28 = (bf16[128,2048]{1,0:T(8,128)(2,1)S(1)}, bf16[128,2048]{1,0:T(8,128)(2,1)S(1)}, u32[]{:S(2)}, u32[]{:S(2)}) collective-permute-start(bf16[128,2048]{1,0:T(8,128)(2,1)S(1)} %bitcast_select_fusion.1), channel_id=1, source_target_pairs={{0,4},{4,0},{8,12},{12,8},{1,5},{5,1},{9,13},{13,9},{2,6},{6,2},{1... | collective-permute-start | bytes 1572872 | tf_op jit(solution)/shard_map/ppermute | solution.py:417
  134.6 14.3 %collective-permute-start.33 = (bf16[128,2048]{1,0:T(8,128)(2,1)S(1)}, bf16[128,2048]{1,0:T(8,128)(2,1)S(1)}, u32[]{:S(2)}, u32[]{:S(2)}) collective-permute-start(bf16[128,2048]{1,0:T(8,128)(2,1)S(1)} %fusion.9), channel_id=1, source_target_pairs={{0,1},{1,0},{2,3},{3,2},{4,8},{5,9},{6,10},{7,11},{8,4},{9,5},{10,... | collective-permute-start | bytes 1572872 | tf_op jit(solution)/shard_map/ppermute | solution.py:420
  136.6 23.7 %collective-permute-start.31 = (bf16[128,2048]{1,0:T(8,128)(2,1)S(1)}, bf16[128,2048]{1,0:T(8,128)(2,1)S(1)}, u32[]{:S(2)}, u32[]{:S(2)}) collective-permute-start(bf16[128,2048]{1,0:T(8,128)(2,1)S(1)} %bitcast_select_fusion), channel_id=1, source_target_pairs={{0,4},{4,0},{8,12},{12,8},{1,5},{5,1},{9,13},{13,9},{2,6},{6,2},{1... | collective-permute-start | bytes 1572872 | tf_op jit(solution)/shard_map/ppermute | solution.py:417
  137.9 22.2 %collective-permute-start.32 = (bf16[128,2048]{1,0:T(8,128)(2,1)S(1)}, bf16[128,2048]{1,0:T(8,128)(2,1)S(1)}, u32[]{:S(2)}, u32[]{:S(2)}) collective-permute-start(bf16[128,2048]{1,0:T(8,128)(2,1)S(1)} %fusion.8), channel_id=1, source_target_pairs={{0,1},{1,0},{2,3},{3,2},{4,8},{5,9},{6,10},{7,11},{8,4},{9,5},{10,... | collective-permute-start | bytes 1572872 | tf_op jit(solution)/shard_map/ppermute | solution.py:420
  149.3 27.6 %collective-permute-start.34 = (bf16[128,2048]{1,0:T(8,128)(2,1)S(1)}, bf16[128,2048]{1,0:T(8,128)(2,1)S(1)}, u32[]{:S(2)}, u32[]{:S(2)}) collective-permute-start(bf16[128,2048]{1,0:T(8,128)(2,1)S(1)} %fusion.10), channel_id=1, source_target_pairs={{0,4},{4,0},{8,12},{12,8},{1,5},{5,1},{9,13},{13,9},{2,6},{6,2},{1... | collective-permute-start | bytes 1572872 | tf_op jit(solution)/shard_map/ppermute | solution.py:417
  149.6 27.2 %collective-permute-start.35 = (bf16[128,2048]{1,0:T(8,128)(2,1)S(1)}, bf16[128,2048]{1,0:T(8,128)(2,1)S(1)}, u32[]{:S(2)}, u32[]{:S(2)}) collective-permute-start(bf16[128,2048]{1,0:T(8,128)(2,1)S(1)} %fusion.7), channel_id=1, source_target_pairs={{0,1},{1,0},{2,3},{3,2},{4,8},{5,9},{6,10},{7,11},{8,4},{9,5},{10,... | collective-permute-start | bytes 1572872 | tf_op jit(solution)/shard_map/ppermute | solution.py:420
  160.5 20.1 %collective-permute-start.37 = (bf16[128,2048]{1,0:T(8,128)(2,1)S(1)}, bf16[128,2048]{1,0:T(8,128)(2,1)S(1)}, u32[]{:S(2)}, u32[]{:S(2)}) collective-permute-start(bf16[128,2048]{1,0:T(8,128)(2,1)S(1)} %fusion.11), channel_id=1, source_target_pairs={{0,4},{4,0},{8,12},{12,8},{1,5},{5,1},{9,13},{13,9},{2,6},{6,2},{1... | collective-permute-start | bytes 1572872 | tf_op jit(solution)/shard_map/ppermute | solution.py:417
  160.9 21.7 %collective-permute-start.38 = (bf16[128,2048]{1,0:T(8,128)(2,1)S(1)}, bf16[128,2048]{1,0:T(8,128)(2,1)S(1)}, u32[]{:S(2)}, u32[]{:S(2)}) collective-permute-start(bf16[128,2048]{1,0:T(8,128)(2,1)S(1)} %fusion.5), channel_id=1, source_target_pairs={{0,1},{1,0},{2,3},{3,2},{4,8},{5,9},{6,10},{7,11},{8,4},{9,5},{10,... | collective-permute-start | bytes 1572872 | tf_op jit(solution)/shard_map/ppermute | solution.py:420
  176.9 15.1 %collective-permute-start.36 = (bf16[128,2048]{1,0:T(8,128)(2,1)S(1)}, bf16[128,2048]{1,0:T(8,128)(2,1)S(1)}, u32[]{:S(2)}, u32[]{:S(2)}) collective-permute-start(bf16[128,2048]{1,0:T(8,128)(2,1)S(1)} %get-tuple-element.99), channel_id=1, source_target_pairs={{0,4},{4,0},{8,12},{12,8},{1,5},{5,1},{9,13},{13,9},{2,6},{6,2},{1... | collective-permute-start | bytes 1572872 | tf_op jit(solution)/shard_map/ppermute | solution.py:417
  182.6 20.6 %collective-permute-start.39 = (bf16[128,2048]{1,0:T(8,128)(2,1)S(1)}, bf16[128,2048]{1,0:T(8,128)(2,1)S(1)}, u32[]{:S(2)}, u32[]{:S(2)}) collective-permute-start(bf16[128,2048]{1,0:T(8,128)(2,1)S(1)} %get-tuple-element.105), channel_id=1, source_target_pairs={{0,4},{4,0},{8,12},{12,8},{1,5},{5,1},{9,13},{13,9},{2,6},{6,2},{1... | collective-permute-start | bytes 1572872 | tf_op jit(solution)/shard_map/ppermute | solution.py:417
  203.4 14.9 %collective-permute-start.40 = (bf16[128,2048]{1,0:T(8,128)(2,1)S(1)}, bf16[128,2048]{1,0:T(8,128)(2,1)S(1)}, u32[]{:S(2)}, u32[]{:S(2)}) collective-permute-start(bf16[128,2048]{1,0:T(8,128)(2,1)S(1)} %fusion.6), channel_id=1, source_target_pairs={{0,1},{1,0},{2,3},{3,2},{4,8},{5,9},{6,10},{7,11},{8,4},{9,5},{10,... | collective-permute-start | bytes 1572872 | tf_op jit(solution)/shard_map/ppermute | solution.py:420
  203.4 15.2 %collective-permute-start.41 = (bf16[128,2048]{1,0:T(8,128)(2,1)S(1)}, bf16[128,2048]{1,0:T(8,128)(2,1)S(1)}, u32[]{:S(2)}, u32[]{:S(2)}) collective-permute-start(bf16[128,2048]{1,0:T(8,128)(2,1)S(1)} %dynamic-slice_bitcast_fusion.1), channel_id=1, source_target_pairs={{0,4},{4,0},{8,12},{12,8},{1,5},{5,1},{9,13},{13,9},{2,6},{6,2},{1... | collective-permute-start | bytes 1572872 | tf_op jit(solution)/shard_map/ppermute | solution.py:417
  206.2 23.4 %collective-permute-start.42 = (bf16[128,2048]{1,0:T(8,128)(2,1)S(1)}, bf16[128,2048]{1,0:T(8,128)(2,1)S(1)}, u32[]{:S(2)}, u32[]{:S(2)}) collective-permute-start(bf16[128,2048]{1,0:T(8,128)(2,1)S(1)} %dynamic-slice_bitcast_fusion), channel_id=1, source_target_pairs={{0,4},{4,0},{8,12},{12,8},{1,5},{5,1},{9,13},{13,9},{2,6},{6,2},{1... | collective-permute-start | bytes 1572872 | tf_op jit(solution)/shard_map/ppermute | solution.py:417
  206.3 23.3 %collective-permute-start.43 = (bf16[128,2048]{1,0:T(8,128)(2,1)S(1)}, bf16[128,2048]{1,0:T(8,128)(2,1)S(1)}, u32[]{:S(2)}, u32[]{:S(2)}) collective-permute-start(bf16[128,2048]{1,0:T(8,128)(2,1)S(1)} %fusion.3), channel_id=1, source_target_pairs={{0,1},{1,0},{2,3},{3,2},{4,8},{5,9},{6,10},{7,11},{8,4},{9,5},{10,... | collective-permute-start | bytes 1572872 | tf_op jit(solution)/shard_map/ppermute | solution.py:420
  229.9 14.9 %collective-permute-start.46 = (bf16[128,2048]{1,0:T(8,128)(2,1)S(1)}, bf16[128,2048]{1,0:T(8,128)(2,1)S(1)}, u32[]{:S(2)}, u32[]{:S(2)}) collective-permute-start(bf16[128,2048]{1,0:T(8,128)(2,1)S(1)} %fusion.13), channel_id=1, source_target_pairs={{0,4},{4,0},{8,12},{12,8},{1,5},{5,1},{9,13},{13,9},{2,6},{6,2},{1... | collective-permute-start | bytes 1572872 | tf_op jit(solution)/shard_map/ppermute | solution.py:417
  231.7 14.9 %collective-permute-start.47 = (bf16[128,2048]{1,0:T(8,128)(2,1)S(1)}, bf16[128,2048]{1,0:T(8,128)(2,1)S(1)}, u32[]{:S(2)}, u32[]{:S(2)}) collective-permute-start(bf16[128,2048]{1,0:T(8,128)(2,1)S(1)} %fusion.2), channel_id=1, source_target_pairs={{0,1},{1,0},{2,3},{3,2},{4,8},{5,9},{6,10},{7,11},{8,4},{9,5},{10,... | collective-permute-start | bytes 1572872 | tf_op jit(solution)/shard_map/ppermute | solution.py:420
  231.7 23.1 %collective-permute-start.44 = (bf16[128,2048]{1,0:T(8,128)(2,1)S(1)}, bf16[128,2048]{1,0:T(8,128)(2,1)S(1)}, u32[]{:S(2)}, u32[]{:S(2)}) collective-permute-start(bf16[128,2048]{1,0:T(8,128)(2,1)S(1)} %fusion.12), channel_id=1, source_target_pairs={{0,4},{4,0},{8,12},{12,8},{1,5},{5,1},{9,13},{13,9},{2,6},{6,2},{1... | collective-permute-start | bytes 1572872 | tf_op jit(solution)/shard_map/ppermute | solution.py:417
  232.0 24.0 %collective-permute-start.45 = (bf16[128,2048]{1,0:T(8,128)(2,1)S(1)}, bf16[128,2048]{1,0:T(8,128)(2,1)S(1)}, u32[]{:S(2)}, u32[]{:S(2)}) collective-permute-start(bf16[128,2048]{1,0:T(8,128)(2,1)S(1)} %fusion.4), channel_id=1, source_target_pairs={{0,1},{1,0},{2,3},{3,2},{4,8},{5,9},{6,10},{7,11},{8,4},{9,5},{10,... | collective-permute-start | bytes 1572872 | tf_op jit(solution)/shard_map/ppermute | solution.py:420
  (27 other events, 417.4 us)

commit v4 on v3

--- a/solution.py
+++ b/solution.py
@@ -143,28 +143,34 @@
     ones = jnp.ones((BLOCK, HD), jnp.bfloat16)
     together = min(heads, GROUP)
 
-    def step(j, carry):
+    tail = (low + rows - 1) % BLOCK + 1 if span % BLOCK == 0 else BLOCK
+
+    def step(j, carry, size=BLOCK):
         offset = pl.multiple_of(j * BLOCK, BLOCK)
-        key_index = column + offset
-        bias = jnp.where((key_index <= row_index) & (key_index >= first), 0.0, masked_score)
-        key = kv[pl.ds(offset, BLOCK), :HD]
-        value = jnp.concatenate([kv[pl.ds(offset, BLOCK), HD:], ones], axis=1)
+        key_index = column[:, :size] + offset
+        bias = jnp.where(
+            (key_index <= row_index[:, :size]) & (key_index >= first), 0.0, masked_score
+        )
+        key = kv[pl.ds(offset, size), :HD]
+        value = jnp.concatenate([kv[pl.ds(offset, size), HD:], ones[:size]], axis=1)
         for g in range(heads // together):
-            span = slice(g * together * rows, (g + 1) * together * rows)
+            at = slice(g * together * rows, (g + 1) * together * rows)
             scores = lax.dot_general(
-                query[span], key, (((1,), (1,)), ((), ())), preferred_element_type=jnp.float32
+                query[at], key, (((1,), (1,)), ((), ())), preferred_element_type=jnp.float32
             )
-            scores = (scores.reshape(together, rows, BLOCK) + bias[None]).reshape(-1, BLOCK)
-            old = top[span]
+            scores = (scores.reshape(together, rows, size) + bias[None]).reshape(-1, size)
+            old = top[at]
             new = jnp.maximum(old, jnp.max(scores, axis=1, keepdims=True))
             exps = jnp.exp2(scores - new[:, :1]).astype(jnp.bfloat16)
             mixed = jnp.dot(exps, value, preferred_element_type=jnp.float32)
             keep = jnp.exp2(old - new)
-            acc[span] = acc[span] * jnp.concatenate([keep, keep], axis=1) + mixed
-            top[span] = new
+            acc[at] = acc[at] * jnp.concatenate([keep, keep], axis=1) + mixed
+            top[at] = new
         return carry
 
-    lax.fori_loop(start, (base + low + rows - 1) // BLOCK + 1, step, 0)
+    final = (base + low + rows - 1) // BLOCK
+    lax.fori_loop(start, final, step, 0)
+    step(final, 0, tail)
     for h in range(heads):
         span = slice(h * rows, (h + 1) * rows)
         flat[:, h * HD : (h + 1) * HD] = (acc[span, :HD] / acc[span, HD:]).astype(jnp.bfloat16)

time: 261 us -> 261 us (level); the launches traced: 258 us -> 261 us
  Pallas kernels: 59.2 us -> 63.2 us
    pallas_call x2, Pallas kernels: 31.3 us -> 35.3 us  [chunk_terms(): pl.pallas_call(functools.partial(chunk_kernel, count, pieces_of, low), ou...]
  transfers between devices with their start and end apart: 48 -> 48, of which waited for: 31 -> 30; matrix products, arithmetic and copies ran while one was open for 3% -> 3% of each run, Pallas kernels for 22% -> 24%
where the time goes in v4:
time: 261 us
  waiting for transfers between devices  130 us (50%)
  Pallas kernels  63.2 us (24%)
  starting transfers between devices  50.4 us (19%)
  other arithmetic  8.11 us (3%)
  between operations  5.77 us (2%)
  local copies, waits for them, and re-layouts  3.51 us (1%)
    ppermute x22, waiting for transfers between devices, outer(): return lax.ppermute(value, 'tp', pairs)  68.9 us
    ppermute x17, waiting for transfers between devices, inner(): return lax.ppermute(value, ('tp', 'sp'), self.inner_pairs)  56.5 us
    pallas_call x2, Pallas kernels, chunk_terms(): pl.pallas_call(functools.partial(chunk_kernel, count, pieces_of, low), ou...  35.3 us
    ppermute x22, starting transfers between devices, outer(): return lax.ppermute(value, 'tp', pairs)  34.4 us
    pallas_call x2, Pallas kernels, output_terms(): pl.pallas_call(output_kernel, out_shape=[jax.ShapeDtypeStruct((count, row...  14.9 us
    ppermute x17, starting transfers between devices, inner(): return lax.ppermute(value, ('tp', 'sp'), self.inner_pairs)  9.26 us
    pallas_call x4, Pallas kernels, finish(): pl.pallas_call(functools.partial(finish_kernel, count, low, inner is not...  7.27 us
    pallas_call x1, Pallas kernels, kv_terms_of(): pl.pallas_call(functools.partial(kv_kernel, HQ // KV, slots), out_shape=s...  5.55 us
  transfers between devices with their start and end apart: 48, of which 30 were waited for; matrix products, arithmetic and copies ran while one was open for 3% of the time, Pallas kernels for 24%

profile of v4, /device:TPU:10, one launch (start us, length us, event | category | flops | bytes accessed | tf_op | source)
XLA Modules:
  0.0 260.8 jit_solution(18308576049735017556)
XLA Ops:
  0.7 2.3 fusion.1
  3.0 1.6 collective-permute-start.17
  9.2 2.7 %collective-permute-start.6 = (bf16[128,2048]{1,0:T(8,128)(2,1)}, bf16[128,2048]{1,0:T(8,128)(2,1)S(1)}, u32[]{:S(2)}, u32[]{:S(2)}) collective-permute-start(bf16[128,2048]{1,0:T(8,128)(2,1)} %get-tuple-element.63), channel_id=1, source_target_pairs={{0,1},{1,0},{2,3},{3,2},{4,8},{5,9},{6,10},{7,11},{8,4},{9,5},{10,... | collective-permute-start | bytes 1572872 | tf_op jit(solution)/shard_map/ppermute | solution.py:426
  12.1 5.5 %kv_terms.1 = (bf16[128,2048]{1,0:T(8,128)(2,1)S(1)}, bf16[128,2048]{1,0:T(8,128)(2,1)S(1)}, bf16[64,2048]{1,0:T(8,128)(2,1)S(1)}, bf16[64,2048]{1,0:T(8,128)(2,1)S(1)}) custom-call(s32[4]{0:T(128)S(1)} %pad_add_fusion.info_ref, bf16[512,2048]{1,0:T(8,128)(2,1)} %copy-done.3, bf16[2048,512]{1,0:T(8,128)(2,1)} %w_key.1, bf16[2048,512]{1,0:T(8,128)(2,1)} %w_value.1), custom_call_target="tpu_custom_call" | custom-call | bytes 2097152 | tf_op jit(solution)/shard_map/kv_terms/pallas_call | solution.py:303
  19.7 2.3 collective-permute-done.2
  23.2 3.4 %collective-permute-start.4 = (bf16[128,2048]{1,0:T(8,128)(2,1)}, bf16[128,2048]{1,0:T(8,128)(2,1)S(1)}, u32[]{:S(2)}, u32[]{:S(2)}) collective-permute-start(bf16[128,2048]{1,0:T(8,128)(2,1)} %get-tuple-element.61), channel_id=1, source_target_pairs={{0,4},{4,0},{8,12},{12,8},{1,5},{5,1},{9,13},{13,9},{2,6},{6,2},{1... | collective-permute-start | bytes 1572872 | tf_op jit(solution)/shard_map/ppermute | solution.py:423
  26.8 2.0 collective-permute-start.10
  28.9 5.6 %collective-permute-done.18 = bf16[128,2048]{1,0:T(8,128)(2,1)} collective-permute-done((bf16[128,2048]{1,0:T(8,128)(2,1)S(1)}, bf16[128,2048]{1,0:T(8,128)(2,1)}, u32[]{:S(2)}, u32[]{:S(2)}) %collective-permute-start.18) | collective-permute-done | bytes 524320 | tf_op jit(solution)/shard_map/ppermute | solution.py:423
  35.7 2.1 collective-permute-done.3.refs_6_
  37.8 6.5 %collective-permute-done.4.refs_5_ = bf16[128,2048]{1,0:T(8,128)(2,1)S(1)} collective-permute-done((bf16[128,2048]{1,0:T(8,128)(2,1)}, bf16[128,2048]{1,0:T(8,128)(2,1)S(1)}, u32[]{:S(2)}, u32[]{:S(2)}) %collective-permute-start.4) | collective-permute-done | bytes 524320 | tf_op jit(solution)/shard_map/ppermute | solution.py:423
  44.2 1.5 collective-permute-start.19
  49.0 1.4 collective-permute-done.10.refs_2_
  50.3 4.4 %collective-permute-start.11 = (bf16[128,2048]{1,0:T(8,128)(2,1)S(1)}, bf16[128,2048]{1,0:T(8,128)(2,1)S(1)}, u32[]{:S(2)}, u32[]{:S(2)}) collective-permute-start(bf16[128,2048]{1,0:T(8,128)(2,1)S(1)} %collective-permute-done.9.refs_3_), channel_id=1, source_target_pairs={{4,0},{8,12},{5,1},{9,13},{6,2},{10,14},{7,3},{11,15},{20,16},{24,... | collective-permute-start | bytes 1572872 | tf_op jit(solution)/shard_map/ppermute | solution.py:423
  54.8 5.5 %collective-permute-done.19 = bf16[128,2048]{1,0:T(8,128)(2,1)S(1)} collective-permute-done((bf16[128,2048]{1,0:T(8,128)(2,1)S(1)}, bf16[128,2048]{1,0:T(8,128)(2,1)S(1)}, u32[]{:S(2)}, u32[]{:S(2)}) %collective-permute-start.19) | collective-permute-done | bytes 524320 | tf_op jit(solution)/shard_map/ppermute | solution.py:426
  61.6 8.9 %collective-permute-done.8.refs_8_ = bf16[128,2048]{1,0:T(8,128)(2,1)} collective-permute-done((bf16[128,2048]{1,0:T(8,128)(2,1)S(1)}, bf16[128,2048]{1,0:T(8,128)(2,1)}, u32[]{:S(2)}, u32[]{:S(2)}) %collective-permute-start.8) | collective-permute-done | bytes 524320 | tf_op jit(solution)/shard_map/ppermute | solution.py:426
  71.1 4.0 %collective-permute-start.14 = (bf16[128,2048]{1,0:T(8,128)(2,1)}, bf16[128,2048]{1,0:T(8,128)(2,1)S(1)}, u32[]{:S(2)}, u32[]{:S(2)}) collective-permute-start(bf16[128,2048]{1,0:T(8,128)(2,1)} %collective-permute-done.8.refs_8_), channel_id=1, source_target_pairs={{4,0},{8,12},{5,1},{9,13},{6,2},{10,14},{7,3},{11,15},{20,16},{24,... | collective-permute-start | bytes 1572872 | tf_op jit(solution)/shard_map/ppermute | solution.py:423
  75.5 3.0 %collective-permute-done.20 = bf16[64,2048]{1,0:T(8,128)(2,1)S(1)} collective-permute-done((bf16[64,2048]{1,0:T(8,128)(2,1)S(1)}, bf16[64,2048]{1,0:T(8,128)(2,1)S(1)}, u32[]{:S(2)}, u32[]{:S(2)}) %collective-permute-start.20) | collective-permute-done | bytes 262176 | tf_op jit(solution)/shard_map/ppermute | solution.py:423
  78.8 1.7 collective-permute-start.22
  86.1 2.9 %collective-permute-done.14.refs_9_ = bf16[128,2048]{1,0:T(8,128)(2,1)S(1)} collective-permute-done((bf16[128,2048]{1,0:T(8,128)(2,1)}, bf16[128,2048]{1,0:T(8,128)(2,1)S(1)}, u32[]{:S(2)}, u32[]{:S(2)}) %collective-permute-start.14) | collective-permute-done | bytes 524320 | tf_op jit(solution)/shard_map/ppermute | solution.py:423
  89.1 2.4 collective-permute-start.12
  93.4 17.7 %chunk_terms.2 = (bf16[128,2048]{1,0:T(8,128)(2,1)S(1)}, bf16[128,2048]{1,0:T(8,128)(2,1)S(1)}, bf16[256,1024]{1,0:T(8,128)(2,1)S(1)}) custom-call(s32[3]{0:T(128)S(1)} %add_add_fusion.1.info_ref, bf16[512,2048]{1,0:T(8,128)(2,1)} %copy-done.3, bf16[128,2048]{1,0:T(8,128)(2,1)} %copy-done.15, bf16[128,2048]{1,0:T(8,128)(2,1)} %copy-done.16, ...), custom_call_target="tpu_custom_call" | custom-call | flops 2147483648 | tf_op jit(solution)/shard_map/chunk_terms/pallas_call | solution.py:245
  111.2 2.6 collective-permute-start.24
  114.3 2.3 collective-permute-start.29
  116.8 7.8 %collective-permute-done.24.refs_2_ = bf16[128,2048]{1,0:T(8,128)(2,1)S(1)} collective-permute-done((bf16[128,2048]{1,0:T(8,128)(2,1)S(1)}, bf16[128,2048]{1,0:T(8,128)(2,1)S(1)}, u32[]{:S(2)}, u32[]{:S(2)}) %collective-permute-start.24) | collective-permute-done | bytes 524320 | tf_op jit(solution)/shard_map/ppermute | solution.py:423
  124.6 2.6 collective-permute-done.25.refs_3_
  127.2 7.6 %output_terms.2 = (bf16[4,128,2048]{2,1,0:T(8,128)(2,1)S(1)}, bf16[4,128,2048]{2,1,0:T(8,128)(2,1)S(1)}) custom-call(bf16[256,1024]{1,0:T(8,128)(2,1)S(1)} %get-tuple-element.83.flat, bf16[1024,8192]{1,0:T(8,128)(2,1)} %w_out.3), custom_call_target="tpu_custom_call" | custom-call | flops 2147483648 | tf_op jit(solution)/shard_map/output_terms/pallas_call | solution.py:216
  135.2 3.2 %collective-permute-done.30.refs_8_ = bf16[128,2048]{1,0:T(8,128)(2,1)S(1)} collective-permute-done((bf16[128,2048]{1,0:T(8,128)(2,1)S(1)}, bf16[128,2048]{1,0:T(8,128)(2,1)S(1)}, u32[]{:S(2)}, u32[]{:S(2)}) %collective-permute-start.30) | collective-permute-done | bytes 524320 | tf_op jit(solution)/shard_map/ppermute | solution.py:426
  138.7 1.4 collective-permute-start.31
  140.3 9.7 %collective-permute-done.33 = bf16[128,2048]{1,0:T(8,128)(2,1)S(1)} collective-permute-done((bf16[128,2048]{1,0:T(8,128)(2,1)S(1)}, bf16[128,2048]{1,0:T(8,128)(2,1)S(1)}, u32[]{:S(2)}, u32[]{:S(2)}) %collective-permute-start.33) | collective-permute-done | bytes 524320 | tf_op jit(solution)/shard_map/ppermute | solution.py:426
  150.6 10.7 %collective-permute-done.32 = bf16[128,2048]{1,0:T(8,128)(2,1)S(1)} collective-permute-done((bf16[128,2048]{1,0:T(8,128)(2,1)S(1)}, bf16[128,2048]{1,0:T(8,128)(2,1)S(1)}, u32[]{:S(2)}, u32[]{:S(2)}) %collective-permute-start.32) | collective-permute-done | bytes 524320 | tf_op jit(solution)/shard_map/ppermute | solution.py:426
  162.3 17.7 %chunk_terms.3 = (bf16[128,2048]{1,0:T(8,128)(2,1)S(1)}, bf16[128,2048]{1,0:T(8,128)(2,1)S(1)}, bf16[256,1024]{1,0:T(8,128)(2,1)S(1)}) custom-call(s32[3]{0:T(128)S(1)} %add_add_fusion.2.info_ref, bf16[512,2048]{1,0:T(8,128)(2,1)} %copy-done.3, bf16[128,2048]{1,0:T(8,128)(2,1)} %copy-done.24, bf16[128,2048]{1,0:T(8,128)(2,1)} %copy-done.4, ...), custom_call_target="tpu_custom_call" | custom-call | flops 2147483648 | tf_op jit(solution)/shard_map/chunk_terms/pallas_call | solution.py:245
  180.0 3.3 %collective-permute-start.36 = (bf16[128,2048]{1,0:T(8,128)(2,1)S(1)}, bf16[128,2048]{1,0:T(8,128)(2,1)S(1)}, u32[]{:S(2)}, u32[]{:S(2)}) collective-permute-start(bf16[128,2048]{1,0:T(8,128)(2,1)S(1)} %get-tuple-element.99), channel_id=1, source_target_pairs={{0,4},{4,0},{8,12},{12,8},{1,5},{5,1},{9,13},{13,9},{2,6},{6,2},{1... | collective-permute-start | bytes 1572872 | tf_op jit(solution)/shard_map/ppermute | solution.py:423
  183.8 10.7 %collective-permute-done.36 = bf16[128,2048]{1,0:T(8,128)(2,1)S(1)} collective-permute-done((bf16[128,2048]{1,0:T(8,128)(2,1)S(1)}, bf16[128,2048]{1,0:T(8,128)(2,1)S(1)}, u32[]{:S(2)}, u32[]{:S(2)}) %collective-permute-start.36) | collective-permute-done | bytes 524320 | tf_op jit(solution)/shard_map/ppermute | solution.py:423
  194.5 7.4 %output_terms.3 = (bf16[4,128,2048]{2,1,0:T(8,128)(2,1)S(1)}, bf16[4,128,2048]{2,1,0:T(8,128)(2,1)S(1)}) custom-call(bf16[256,1024]{1,0:T(8,128)(2,1)S(1)} %get-tuple-element.100.flat, bf16[1024,8192]{1,0:T(8,128)(2,1)} %w_out.3), custom_call_target="tpu_custom_call" | custom-call | flops 2147483648 | tf_op jit(solution)/shard_map/output_terms/pallas_call | solution.py:216
  201.9 3.8 %collective-permute-done.39 = bf16[128,2048]{1,0:T(8,128)(2,1)S(1)} collective-permute-done((bf16[128,2048]{1,0:T(8,128)(2,1)S(1)}, bf16[128,2048]{1,0:T(8,128)(2,1)S(1)}, u32[]{:S(2)}, u32[]{:S(2)}) %collective-permute-start.39) | collective-permute-done | bytes 524320 | tf_op jit(solution)/shard_map/ppermute | solution.py:423
  206.1 3.2 %collective-permute-start.41 = (bf16[128,2048]{1,0:T(8,128)(2,1)S(1)}, bf16[128,2048]{1,0:T(8,128)(2,1)S(1)}, u32[]{:S(2)}, u32[]{:S(2)}) collective-permute-start(bf16[128,2048]{1,0:T(8,128)(2,1)S(1)} %dynamic-slice_bitcast_fusion.1), channel_id=1, source_target_pairs={{0,4},{4,0},{8,12},{12,8},{1,5},{5,1},{9,13},{13,9},{2,6},{6,2},{1... | collective-permute-start | bytes 1572872 | tf_op jit(solution)/shard_map/ppermute | solution.py:423
  210.2 10.2 %collective-permute-done.40 = bf16[128,2048]{1,0:T(8,128)(2,1)S(1)} collective-permute-done((bf16[128,2048]{1,0:T(8,128)(2,1)S(1)}, bf16[128,2048]{1,0:T(8,128)(2,1)S(1)}, u32[]{:S(2)}, u32[]{:S(2)}) %collective-permute-start.40) | collective-permute-done | bytes 524320 | tf_op jit(solution)/shard_map/ppermute | solution.py:426
  220.6 1.4 collective-permute-done.41
  222.1 10.5 %collective-permute-done.42 = bf16[128,2048]{1,0:T(8,128)(2,1)S(1)} collective-permute-done((bf16[128,2048]{1,0:T(8,128)(2,1)S(1)}, bf16[128,2048]{1,0:T(8,128)(2,1)S(1)}, u32[]{:S(2)}, u32[]{:S(2)}) %collective-permute-start.42) | collective-permute-done | bytes 524320 | tf_op jit(solution)/shard_map/ppermute | solution.py:423
  233.0 1.8 collective-permute-start.46
  235.1 1.7 collective-permute-start.45
  236.8 1.8 finish.4.refs_0_
  238.7 1.8 finish.5.refs_0_
  240.5 7.4 %collective-permute-done.46.outer = bf16[128,2048]{1,0:T(8,128)(2,1)S(1)} collective-permute-done((bf16[128,2048]{1,0:T(8,128)(2,1)S(1)}, bf16[128,2048]{1,0:T(8,128)(2,1)S(1)}, u32[]{:S(2)}, u32[]{:S(2)}) %collective-permute-start.46) | collective-permute-done | bytes 524320 | tf_op jit(solution)/shard_map/ppermute | solution.py:423
  247.9 1.8 collective-permute-done.47.inner
  249.7 1.8 finish.6.refs_0_
  251.5 6.2 %collective-permute-done.44.outer = bf16[128,2048]{1,0:T(8,128)(2,1)S(1)} collective-permute-done((bf16[128,2048]{1,0:T(8,128)(2,1)S(1)}, bf16[128,2048]{1,0:T(8,128)(2,1)S(1)}, u32[]{:S(2)}, u32[]{:S(2)}) %collective-permute-start.44) | collective-permute-done | bytes 524320 | tf_op jit(solution)/shard_map/ppermute | solution.py:423
  258.8 1.8 finish.7
  (151 shorter events, 25.6 us)
Async XLA Ops:
  3.0 9.0 %collective-permute-start.17 = (f32[512]{0:T(512)S(1)}, f32[512]{0:T(512)S(1)}, u32[]{:S(2)}, u32[]{:S(2)}) collective-permute-start(f32[512]{0:T(512)S(1)} %get-tuple-element.121), channel_id=1, source_target_pairs={{0,12},{4,8},{8,4},{12,0},{1,13},{5,9},{9,5},{13,1},{2,14},{6,10},... | collective-permute-start | bytes 6152 | tf_op jit(solution)/shard_map/ppermute | solution.py:394
  4.6 7.4 %collective-permute-start.16 = (f32[512]{0:T(512)S(1)}, f32[512]{0:T(512)S(1)}, u32[]{:S(2)}, u32[]{:S(2)}) collective-permute-start(f32[512]{0:T(512)S(1)} %get-tuple-element.121), channel_id=1, source_target_pairs={{0,8},{4,12},{8,0},{12,4},{1,9},{5,13},{9,1},{13,5},{2,10},{6,14},... | collective-permute-start | bytes 6152 | tf_op jit(solution)/shard_map/ppermute | solution.py:394
  5.9 6.2 %collective-permute-start.15 = (f32[512]{0:T(512)S(1)}, f32[512]{0:T(512)S(1)}, u32[]{:S(2)}, u32[]{:S(2)}) collective-permute-start(f32[512]{0:T(512)S(1)} %get-tuple-element.121), channel_id=1, source_target_pairs={{0,4},{4,0},{8,12},{12,8},{1,5},{5,1},{9,13},{13,9},{2,6},{6,2},{1... | collective-permute-start | bytes 6152 | tf_op jit(solution)/shard_map/ppermute | solution.py:394
  8.5 18.2 %collective-permute-start.5 = (bf16[128,2048]{1,0:T(8,128)(2,1)}, bf16[128,2048]{1,0:T(8,128)(2,1)S(1)}, u32[]{:S(2)}, u32[]{:S(2)}) collective-permute-start(bf16[128,2048]{1,0:T(8,128)(2,1)} %get-tuple-element.63), channel_id=1, source_target_pairs={{0,4},{4,0},{8,12},{12,8},{1,5},{5,1},{9,13},{13,9},{2,6},{6,2},{1... | collective-permute-start | bytes 1572872 | tf_op jit(solution)/shard_map/ppermute | solution.py:423
  9.2 17.4 %collective-permute-start.6 = (bf16[128,2048]{1,0:T(8,128)(2,1)}, bf16[128,2048]{1,0:T(8,128)(2,1)S(1)}, u32[]{:S(2)}, u32[]{:S(2)}) collective-permute-start(bf16[128,2048]{1,0:T(8,128)(2,1)} %get-tuple-element.63), channel_id=1, source_target_pairs={{0,1},{1,0},{2,3},{3,2},{4,8},{5,9},{6,10},{7,11},{8,4},{9,5},{10,... | collective-permute-start | bytes 1572872 | tf_op jit(solution)/shard_map/ppermute | solution.py:426
  17.6 16.9 %collective-permute-start.18 = (bf16[128,2048]{1,0:T(8,128)(2,1)S(1)}, bf16[128,2048]{1,0:T(8,128)(2,1)}, u32[]{:S(2)}, u32[]{:S(2)}) collective-permute-start(bf16[128,2048]{1,0:T(8,128)(2,1)S(1)} %get-tuple-element.76), channel_id=1, source_target_pairs={{0,4},{12,8},{1,5},{13,9},{2,6},{14,10},{3,7},{15,11},{16,20},{28,... | collective-permute-start | bytes 1572872 | tf_op jit(solution)/shard_map/ppermute | solution.py:423
  19.1 3.0 %collective-permute-start.2 = (s32[4]{0:T(128)S(1)}, s32[4]{0:T(128)S(1)}, u32[]{:S(2)}, u32[]{:S(2)}) collective-permute-start(s32[4]{0:T(128)S(1)} %convert_reduce_fusion), channel_id=1, source_target_pairs={{0,3},{1,2},{2,1},{3,0},{4,7},{5,6},{6,5},{7,4},{8,11},{9,10},{10,... | collective-permute-start | bytes 56 | tf_op jit(solution)/shard_map/ppermute | solution.py:394
  19.1 3.6 %collective-permute-start.1 = (s32[4]{0:T(128)S(1)}, s32[4]{0:T(128)S(1)}, u32[]{:S(2)}, u32[]{:S(2)}) collective-permute-start(s32[4]{0:T(128)S(1)} %convert_reduce_fusion), channel_id=1, source_target_pairs={{0,2},{1,3},{2,0},{3,1},{4,6},{5,7},{6,4},{7,5},{8,10},{9,11},{10,... | collective-permute-start | bytes 56 | tf_op jit(solution)/shard_map/ppermute | solution.py:394
  22.1 1.1 collective-permute-start
  22.7 15.0 %collective-permute-start.3 = (bf16[128,2048]{1,0:T(8,128)(2,1)}, bf16[128,2048]{1,0:T(8,128)(2,1)S(1)}, u32[]{:S(2)}, u32[]{:S(2)}) collective-permute-start(bf16[128,2048]{1,0:T(8,128)(2,1)} %get-tuple-element.61), channel_id=1, source_target_pairs={{0,1},{1,0},{2,3},{3,2},{4,8},{5,9},{6,10},{7,11},{8,4},{9,5},{10,... | collective-permute-start | bytes 1572872 | tf_op jit(solution)/shard_map/ppermute | solution.py:426
  23.2 21.0 %collective-permute-start.4 = (bf16[128,2048]{1,0:T(8,128)(2,1)}, bf16[128,2048]{1,0:T(8,128)(2,1)S(1)}, u32[]{:S(2)}, u32[]{:S(2)}) collective-permute-start(bf16[128,2048]{1,0:T(8,128)(2,1)} %get-tuple-element.61), channel_id=1, source_target_pairs={{0,4},{4,0},{8,12},{12,8},{1,5},{5,1},{9,13},{13,9},{2,6},{6,2},{1... | collective-permute-start | bytes 1572872 | tf_op jit(solution)/shard_map/ppermute | solution.py:423
  26.7 22.3 %collective-permute-start.9 = (bf16[128,2048]{1,0:T(8,128)(2,1)S(1)}, bf16[128,2048]{1,0:T(8,128)(2,1)S(1)}, u32[]{:S(2)}, u32[]{:S(2)}) collective-permute-start(bf16[128,2048]{1,0:T(8,128)(2,1)S(1)} %collective-permute-done.5.refs_0_), channel_id=1, source_target_pairs={{0,1},{1,0},{2,3},{3,2},{4,8},{5,9},{6,10},{7,11},{8,4},{9,5},{10,... | collective-permute-start | bytes 1572872 | tf_op jit(solution)/shard_map/ppermute | solution.py:426
  26.8 23.5 %collective-permute-start.10 = (bf16[128,2048]{1,0:T(8,128)(2,1)S(1)}, bf16[128,2048]{1,0:T(8,128)(2,1)S(1)}, u32[]{:S(2)}, u32[]{:S(2)}) collective-permute-start(bf16[128,2048]{1,0:T(8,128)(2,1)S(1)} %collective-permute-done.6.refs_1_), channel_id=1, source_target_pairs={{4,0},{8,12},{5,1},{9,13},{6,2},{10,14},{7,3},{11,15},{20,16},{24,... | collective-permute-start | bytes 1572872 | tf_op jit(solution)/shard_map/ppermute | solution.py:423
  44.2 16.0 %collective-permute-start.19 = (bf16[128,2048]{1,0:T(8,128)(2,1)S(1)}, bf16[128,2048]{1,0:T(8,128)(2,1)S(1)}, u32[]{:S(2)}, u32[]{:S(2)}) collective-permute-start(bf16[128,2048]{1,0:T(8,128)(2,1)S(1)} %add_convert_fusion.4), channel_id=1, source_target_pairs={{0,1},{1,0},{2,3},{3,2},{4,8},{5,9},{6,10},{7,11},{8,4},{9,5},{10,... | collective-permute-start | bytes 1572872 | tf_op jit(solution)/shard_map/ppermute | solution.py:426
  45.8 15.8 %collective-permute-start.7 = (bf16[128,2048]{1,0:T(8,128)(2,1)S(1)}, bf16[128,2048]{1,0:T(8,128)(2,1)S(1)}, u32[]{:S(2)}, u32[]{:S(2)}) collective-permute-start(bf16[128,2048]{1,0:T(8,128)(2,1)S(1)} %collective-permute-done.3.refs_6_), channel_id=1, source_target_pairs={{4,0},{8,12},{5,1},{9,13},{6,2},{10,14},{7,3},{11,15},{20,16},{24,... | collective-permute-start | bytes 1572872 | tf_op jit(solution)/shard_map/ppermute | solution.py:423
  47.1 23.3 %collective-permute-start.8 = (bf16[128,2048]{1,0:T(8,128)(2,1)S(1)}, bf16[128,2048]{1,0:T(8,128)(2,1)}, u32[]{:S(2)}, u32[]{:S(2)}) collective-permute-start(bf16[128,2048]{1,0:T(8,128)(2,1)S(1)} %collective-permute-done.4.refs_5_), channel_id=1, source_target_pairs={{0,1},{1,0},{2,3},{3,2},{4,8},{5,9},{6,10},{7,11},{8,4},{9,5},{10,... | collective-permute-start | bytes 1572872 | tf_op jit(solution)/shard_map/ppermute | solution.py:426
  50.3 24.7 %collective-permute-start.11 = (bf16[128,2048]{1,0:T(8,128)(2,1)S(1)}, bf16[128,2048]{1,0:T(8,128)(2,1)S(1)}, u32[]{:S(2)}, u32[]{:S(2)}) collective-permute-start(bf16[128,2048]{1,0:T(8,128)(2,1)S(1)} %collective-permute-done.9.refs_3_), channel_id=1, source_target_pairs={{4,0},{8,12},{5,1},{9,13},{6,2},{10,14},{7,3},{11,15},{20,16},{24,... | collective-permute-start | bytes 1572872 | tf_op jit(solution)/shard_map/ppermute | solution.py:423
  70.4 8.0 %collective-permute-start.20 = (bf16[64,2048]{1,0:T(8,128)(2,1)S(1)}, bf16[64,2048]{1,0:T(8,128)(2,1)S(1)}, u32[]{:S(2)}, u32[]{:S(2)}) collective-permute-start(bf16[64,2048]{1,0:T(8,128)(2,1)S(1)} %fusion.14), channel_id=1, source_target_pairs={{0,4},{4,0},{8,12},{12,8},{1,5},{5,1},{9,13},{13,9},{2,6},{6,2},{1... | collective-permute-start | bytes 786440 | tf_op jit(solution)/shard_map/ppermute | solution.py:423
  71.1 17.9 %collective-permute-start.14 = (bf16[128,2048]{1,0:T(8,128)(2,1)}, bf16[128,2048]{1,0:T(8,128)(2,1)S(1)}, u32[]{:S(2)}, u32[]{:S(2)}) collective-permute-start(bf16[128,2048]{1,0:T(8,128)(2,1)} %collective-permute-done.8.refs_8_), channel_id=1, source_target_pairs={{4,0},{8,12},{5,1},{9,13},{6,2},{10,14},{7,3},{11,15},{20,16},{24,... | collective-permute-start | bytes 1572872 | tf_op jit(solution)/shard_map/ppermute | solution.py:423
  75.1 36.0 %collective-permute-start.13 = (bf16[128,2048]{1,0:T(8,128)(2,1)}, bf16[128,2048]{1,0:T(8,128)(2,1)S(1)}, u32[]{:S(2)}, u32[]{:S(2)}) collective-permute-start(bf16[128,2048]{1,0:T(8,128)(2,1)} %get-tuple-element.70), channel_id=1, source_target_pairs={{0,1},{1,0},{2,3},{3,2},{4,8},{5,9},{6,10},{7,11},{8,4},{9,5},{10,... | collective-permute-start | bytes 1572872 | tf_op jit(solution)/shard_map/ppermute | solution.py:426
  78.7 12.7 %collective-permute-start.21 = (bf16[512,256]{1,0:T(8,128)(2,1)S(1)}, bf16[512,256]{1,0:T(8,128)(2,1)S(1)}, u32[]{:S(2)}, u32[]{:S(2)}) collective-permute-start(bf16[512,256]{1,0:T(8,128)(2,1)S(1)} %kv_total.1.refs_13_), channel_id=1, source_target_pairs={{0,1},{1,0},{2,3},{3,2},{4,5},{5,4},{6,7},{7,6},{8,9},{9,8},{10,11... | collective-permute-start | bytes 786440 | tf_op jit(solution)/shard_map/ppermute | solution.py:583
  78.8 12.7 %collective-permute-start.22 = (bf16[512,256]{1,0:T(8,128)(2,1)S(1)}, bf16[512,256]{1,0:T(8,128)(2,1)S(1)}, u32[]{:S(2)}, u32[]{:S(2)}) collective-permute-start(bf16[512,256]{1,0:T(8,128)(2,1)S(1)} %kv_total.1.refs_13_), channel_id=1, source_target_pairs={{0,2},{1,3},{2,0},{3,1},{4,6},{5,7},{6,4},{7,5},{8,10},{9,11},{10,... | collective-permute-start | bytes 786440 | tf_op jit(solution)/shard_map/ppermute | solution.py:583
  80.4 12.2 %collective-permute-start.23 = (bf16[512,256]{1,0:T(8,128)(2,1)S(1)}, bf16[512,256]{1,0:T(8,128)(2,1)S(1)}, u32[]{:S(2)}, u32[]{:S(2)}) collective-permute-start(bf16[512,256]{1,0:T(8,128)(2,1)S(1)} %kv_total.1.refs_13_), channel_id=1, source_target_pairs={{0,3},{1,2},{2,1},{3,0},{4,7},{5,6},{6,5},{7,4},{8,11},{9,10},{10,... | collective-permute-start | bytes 786440 | tf_op jit(solution)/shard_map/ppermute | solution.py:583
  89.1 22.1 %collective-permute-start.12 = (bf16[128,2048]{1,0:T(8,128)(2,1)}, bf16[128,2048]{1,0:T(8,128)(2,1)S(1)}, u32[]{:S(2)}, u32[]{:S(2)}) collective-permute-start(bf16[128,2048]{1,0:T(8,128)(2,1)} %get-tuple-element.70), channel_id=1, source_target_pairs={{0,4},{4,0},{8,12},{12,8},{1,5},{5,1},{9,13},{13,9},{2,6},{6,2},{1... | collective-permute-start | bytes 1572872 | tf_op jit(solution)/shard_map/ppermute | solution.py:423
  91.4 22.9 %collective-permute-start.26 = (bf16[128,2048]{1,0:T(8,128)(2,1)}, bf16[128,2048]{1,0:T(8,128)(2,1)S(1)}, u32[]{:S(2)}, u32[]{:S(2)}) collective-permute-start(bf16[128,2048]{1,0:T(8,128)(2,1)} %get-tuple-element.86), channel_id=1, source_target_pairs={{0,4},{4,0},{8,12},{12,8},{1,5},{5,1},{9,13},{13,9},{2,6},{6,2},{1... | collective-permute-start | bytes 1572872 | tf_op jit(solution)/shard_map/ppermute | solution.py:423
  91.5 22.4 %collective-permute-start.27 = (bf16[128,2048]{1,0:T(8,128)(2,1)}, bf16[128,2048]{1,0:T(8,128)(2,1)S(1)}, u32[]{:S(2)}, u32[]{:S(2)}) collective-permute-start(bf16[128,2048]{1,0:T(8,128)(2,1)} %get-tuple-element.86), channel_id=1, source_target_pairs={{0,1},{1,0},{2,3},{3,2},{4,8},{5,9},{6,10},{7,11},{8,4},{9,5},{10,... | collective-permute-start | bytes 1572872 | tf_op jit(solution)/shard_map/ppermute | solution.py:426
  111.2 13.4 %collective-permute-start.24 = (bf16[128,2048]{1,0:T(8,128)(2,1)S(1)}, bf16[128,2048]{1,0:T(8,128)(2,1)S(1)}, u32[]{:S(2)}, u32[]{:S(2)}) collective-permute-start(bf16[128,2048]{1,0:T(8,128)(2,1)S(1)} %broadcast_select_fusion.1), channel_id=1, source_target_pairs={{0,4},{4,0},{8,12},{12,8},{1,5},{5,1},{9,13},{13,9},{2,6},{6,2},{1... | collective-permute-start | bytes 1572872 | tf_op jit(solution)/shard_map/ppermute | solution.py:423
  113.8 13.4 %collective-permute-start.25 = (bf16[128,2048]{1,0:T(8,128)(2,1)S(1)}, bf16[128,2048]{1,0:T(8,128)(2,1)S(1)}, u32[]{:S(2)}, u32[]{:S(2)}) collective-permute-start(bf16[128,2048]{1,0:T(8,128)(2,1)S(1)} %collective-permute-done.12.refs_0_), channel_id=1, source_target_pairs={{0,1},{1,0},{2,3},{3,2},{4,8},{5,9},{6,10},{7,11},{8,4},{9,5},{10,... | collective-permute-start | bytes 1572872 | tf_op jit(solution)/shard_map/ppermute | solution.py:426
  114.3 24.2 %collective-permute-start.29 = (bf16[128,2048]{1,0:T(8,128)(2,1)S(1)}, bf16[128,2048]{1,0:T(8,128)(2,1)S(1)}, u32[]{:S(2)}, u32[]{:S(2)}) collective-permute-start(bf16[128,2048]{1,0:T(8,128)(2,1)S(1)} %broadcast_select_fusion), channel_id=1, source_target_pairs={{0,4},{4,0},{8,12},{12,8},{1,5},{5,1},{9,13},{13,9},{2,6},{6,2},{1... | collective-permute-start | bytes 1572872 | tf_op jit(solution)/shard_map/ppermute | solution.py:423
  116.7 21.8 %collective-permute-start.30 = (bf16[128,2048]{1,0:T(8,128)(2,1)S(1)}, bf16[128,2048]{1,0:T(8,128)(2,1)S(1)}, u32[]{:S(2)}, u32[]{:S(2)}) collective-permute-start(bf16[128,2048]{1,0:T(8,128)(2,1)S(1)} %collective-permute-done.26.refs_5_), channel_id=1, source_target_pairs={{0,1},{1,0},{2,3},{3,2},{4,8},{5,9},{6,10},{7,11},{8,4},{9,5},{10,... | collective-permute-start | bytes 1572872 | tf_op jit(solution)/shard_map/ppermute | solution.py:426
  135.0 15.2 %collective-permute-start.28 = (bf16[128,2048]{1,0:T(8,128)(2,1)S(1)}, bf16[128,2048]{1,0:T(8,128)(2,1)S(1)}, u32[]{:S(2)}, u32[]{:S(2)}) collective-permute-start(bf16[128,2048]{1,0:T(8,128)(2,1)S(1)} %bitcast_select_fusion.1), channel_id=1, source_target_pairs={{0,4},{4,0},{8,12},{12,8},{1,5},{5,1},{9,13},{13,9},{2,6},{6,2},{1... | collective-permute-start | bytes 1572872 | tf_op jit(solution)/shard_map/ppermute | solution.py:423
  135.1 14.9 %collective-permute-start.33 = (bf16[128,2048]{1,0:T(8,128)(2,1)S(1)}, bf16[128,2048]{1,0:T(8,128)(2,1)S(1)}, u32[]{:S(2)}, u32[]{:S(2)}) collective-permute-start(bf16[128,2048]{1,0:T(8,128)(2,1)S(1)} %fusion.9), channel_id=1, source_target_pairs={{0,1},{1,0},{2,3},{3,2},{4,8},{5,9},{6,10},{7,11},{8,4},{9,5},{10,... | collective-permute-start | bytes 1572872 | tf_op jit(solution)/shard_map/ppermute | solution.py:426
  138.7 22.8 %collective-permute-start.31 = (bf16[128,2048]{1,0:T(8,128)(2,1)S(1)}, bf16[128,2048]{1,0:T(8,128)(2,1)S(1)}, u32[]{:S(2)}, u32[]{:S(2)}) collective-permute-start(bf16[128,2048]{1,0:T(8,128)(2,1)S(1)} %bitcast_select_fusion), channel_id=1, source_target_pairs={{0,4},{4,0},{8,12},{12,8},{1,5},{5,1},{9,13},{13,9},{2,6},{6,2},{1... | collective-permute-start | bytes 1572872 | tf_op jit(solution)/shard_map/ppermute | solution.py:423
  140.0 21.3 %collective-permute-start.32 = (bf16[128,2048]{1,0:T(8,128)(2,1)S(1)}, bf16[128,2048]{1,0:T(8,128)(2,1)S(1)}, u32[]{:S(2)}, u32[]{:S(2)}) collective-permute-start(bf16[128,2048]{1,0:T(8,128)(2,1)S(1)} %fusion.8), channel_id=1, source_target_pairs={{0,1},{1,0},{2,3},{3,2},{4,8},{5,9},{6,10},{7,11},{8,4},{9,5},{10,... | collective-permute-start | bytes 1572872 | tf_op jit(solution)/shard_map/ppermute | solution.py:426
  150.4 29.5 %collective-permute-start.34 = (bf16[128,2048]{1,0:T(8,128)(2,1)S(1)}, bf16[128,2048]{1,0:T(8,128)(2,1)S(1)}, u32[]{:S(2)}, u32[]{:S(2)}) collective-permute-start(bf16[128,2048]{1,0:T(8,128)(2,1)S(1)} %fusion.10), channel_id=1, source_target_pairs={{0,4},{4,0},{8,12},{12,8},{1,5},{5,1},{9,13},{13,9},{2,6},{6,2},{1... | collective-permute-start | bytes 1572872 | tf_op jit(solution)/shard_map/ppermute | solution.py:423
  150.5 29.4 %collective-permute-start.35 = (bf16[128,2048]{1,0:T(8,128)(2,1)S(1)}, bf16[128,2048]{1,0:T(8,128)(2,1)S(1)}, u32[]{:S(2)}, u32[]{:S(2)}) collective-permute-start(bf16[128,2048]{1,0:T(8,128)(2,1)S(1)} %fusion.7), channel_id=1, source_target_pairs={{0,1},{1,0},{2,3},{3,2},{4,8},{5,9},{6,10},{7,11},{8,4},{9,5},{10,... | collective-permute-start | bytes 1572872 | tf_op jit(solution)/shard_map/ppermute | solution.py:426
  161.6 21.6 %collective-permute-start.37 = (bf16[128,2048]{1,0:T(8,128)(2,1)S(1)}, bf16[128,2048]{1,0:T(8,128)(2,1)S(1)}, u32[]{:S(2)}, u32[]{:S(2)}) collective-permute-start(bf16[128,2048]{1,0:T(8,128)(2,1)S(1)} %fusion.11), channel_id=1, source_target_pairs={{0,4},{4,0},{8,12},{12,8},{1,5},{5,1},{9,13},{13,9},{2,6},{6,2},{1... | collective-permute-start | bytes 1572872 | tf_op jit(solution)/shard_map/ppermute | solution.py:423
  161.7 22.0 %collective-permute-start.38 = (bf16[128,2048]{1,0:T(8,128)(2,1)S(1)}, bf16[128,2048]{1,0:T(8,128)(2,1)S(1)}, u32[]{:S(2)}, u32[]{:S(2)}) collective-permute-start(bf16[128,2048]{1,0:T(8,128)(2,1)S(1)} %fusion.5), channel_id=1, source_target_pairs={{0,1},{1,0},{2,3},{3,2},{4,8},{5,9},{6,10},{7,11},{8,4},{9,5},{10,... | collective-permute-start | bytes 1572872 | tf_op jit(solution)/shard_map/ppermute | solution.py:426
  180.0 14.5 %collective-permute-start.36 = (bf16[128,2048]{1,0:T(8,128)(2,1)S(1)}, bf16[128,2048]{1,0:T(8,128)(2,1)S(1)}, u32[]{:S(2)}, u32[]{:S(2)}) collective-permute-start(bf16[128,2048]{1,0:T(8,128)(2,1)S(1)} %get-tuple-element.99), channel_id=1, source_target_pairs={{0,4},{4,0},{8,12},{12,8},{1,5},{5,1},{9,13},{13,9},{2,6},{6,2},{1... | collective-permute-start | bytes 1572872 | tf_op jit(solution)/shard_map/ppermute | solution.py:423
  183.8 22.0 %collective-permute-start.39 = (bf16[128,2048]{1,0:T(8,128)(2,1)S(1)}, bf16[128,2048]{1,0:T(8,128)(2,1)S(1)}, u32[]{:S(2)}, u32[]{:S(2)}) collective-permute-start(bf16[128,2048]{1,0:T(8,128)(2,1)S(1)} %get-tuple-element.105), channel_id=1, source_target_pairs={{0,4},{4,0},{8,12},{12,8},{1,5},{5,1},{9,13},{13,9},{2,6},{6,2},{1... | collective-permute-start | bytes 1572872 | tf_op jit(solution)/shard_map/ppermute | solution.py:423
  205.9 14.6 %collective-permute-start.40 = (bf16[128,2048]{1,0:T(8,128)(2,1)S(1)}, bf16[128,2048]{1,0:T(8,128)(2,1)S(1)}, u32[]{:S(2)}, u32[]{:S(2)}) collective-permute-start(bf16[128,2048]{1,0:T(8,128)(2,1)S(1)} %fusion.6), channel_id=1, source_target_pairs={{0,1},{1,0},{2,3},{3,2},{4,8},{5,9},{6,10},{7,11},{8,4},{9,5},{10,... | collective-permute-start | bytes 1572872 | tf_op jit(solution)/shard_map/ppermute | solution.py:426
  206.1 15.9 %collective-permute-start.41 = (bf16[128,2048]{1,0:T(8,128)(2,1)S(1)}, bf16[128,2048]{1,0:T(8,128)(2,1)S(1)}, u32[]{:S(2)}, u32[]{:S(2)}) collective-permute-start(bf16[128,2048]{1,0:T(8,128)(2,1)S(1)} %dynamic-slice_bitcast_fusion.1), channel_id=1, source_target_pairs={{0,4},{4,0},{8,12},{12,8},{1,5},{5,1},{9,13},{13,9},{2,6},{6,2},{1... | collective-permute-start | bytes 1572872 | tf_op jit(solution)/shard_map/ppermute | solution.py:423
  209.5 23.2 %collective-permute-start.42 = (bf16[128,2048]{1,0:T(8,128)(2,1)S(1)}, bf16[128,2048]{1,0:T(8,128)(2,1)S(1)}, u32[]{:S(2)}, u32[]{:S(2)}) collective-permute-start(bf16[128,2048]{1,0:T(8,128)(2,1)S(1)} %dynamic-slice_bitcast_fusion), channel_id=1, source_target_pairs={{0,4},{4,0},{8,12},{12,8},{1,5},{5,1},{9,13},{13,9},{2,6},{6,2},{1... | collective-permute-start | bytes 1572872 | tf_op jit(solution)/shard_map/ppermute | solution.py:423
  209.6 23.1 %collective-permute-start.43 = (bf16[128,2048]{1,0:T(8,128)(2,1)S(1)}, bf16[128,2048]{1,0:T(8,128)(2,1)S(1)}, u32[]{:S(2)}, u32[]{:S(2)}) collective-permute-start(bf16[128,2048]{1,0:T(8,128)(2,1)S(1)} %fusion.3), channel_id=1, source_target_pairs={{0,1},{1,0},{2,3},{3,2},{4,8},{5,9},{6,10},{7,11},{8,4},{9,5},{10,... | collective-permute-start | bytes 1572872 | tf_op jit(solution)/shard_map/ppermute | solution.py:426
  233.0 14.9 %collective-permute-start.46 = (bf16[128,2048]{1,0:T(8,128)(2,1)S(1)}, bf16[128,2048]{1,0:T(8,128)(2,1)S(1)}, u32[]{:S(2)}, u32[]{:S(2)}) collective-permute-start(bf16[128,2048]{1,0:T(8,128)(2,1)S(1)} %fusion.13), channel_id=1, source_target_pairs={{0,4},{4,0},{8,12},{12,8},{1,5},{5,1},{9,13},{13,9},{2,6},{6,2},{1... | collective-permute-start | bytes 1572872 | tf_op jit(solution)/shard_map/ppermute | solution.py:423
  234.8 14.9 %collective-permute-start.47 = (bf16[128,2048]{1,0:T(8,128)(2,1)S(1)}, bf16[128,2048]{1,0:T(8,128)(2,1)S(1)}, u32[]{:S(2)}, u32[]{:S(2)}) collective-permute-start(bf16[128,2048]{1,0:T(8,128)(2,1)S(1)} %fusion.2), channel_id=1, source_target_pairs={{0,1},{1,0},{2,3},{3,2},{4,8},{5,9},{6,10},{7,11},{8,4},{9,5},{10,... | collective-permute-start | bytes 1572872 | tf_op jit(solution)/shard_map/ppermute | solution.py:426
  235.1 22.5 %collective-permute-start.44 = (bf16[128,2048]{1,0:T(8,128)(2,1)S(1)}, bf16[128,2048]{1,0:T(8,128)(2,1)S(1)}, u32[]{:S(2)}, u32[]{:S(2)}) collective-permute-start(bf16[128,2048]{1,0:T(8,128)(2,1)S(1)} %fusion.12), channel_id=1, source_target_pairs={{0,4},{4,0},{8,12},{12,8},{1,5},{5,1},{9,13},{13,9},{2,6},{6,2},{1... | collective-permute-start | bytes 1572872 | tf_op jit(solution)/shard_map/ppermute | solution.py:423
  235.1 23.7 %collective-permute-start.45 = (bf16[128,2048]{1,0:T(8,128)(2,1)S(1)}, bf16[128,2048]{1,0:T(8,128)(2,1)S(1)}, u32[]{:S(2)}, u32[]{:S(2)}) collective-permute-start(bf16[128,2048]{1,0:T(8,128)(2,1)S(1)} %fusion.4), channel_id=1, source_target_pairs={{0,1},{1,0},{2,3},{3,2},{4,8},{5,9},{6,10},{7,11},{8,4},{9,5},{10,... | collective-permute-start | bytes 1572872 | tf_op jit(solution)/shard_map/ppermute | solution.py:426
  (27 other events, 420.8 us)
